TPU v7x, 256 devices: a whole 4x4x8 slice. The times are simulated.
256 devices in a mesh: expert: 128 (over y, x, z), rep: 2 (over core).
Axes of the slice: x: 4, y: 4, z: 8, core: 2. Of those that a mesh axis runs over, the one named last changes fastest.
Arguments:
- inputs: bfloat16 [32768, 2048], P(('expert', 'rep')), may hold values from -6 to 6
- out_grad: bfloat16 [32768, 2048], P(('expert', 'rep')), may hold values from -3 to 3
- expert_ids: int32 [32768, 2], P(('expert', 'rep')), may hold values from 0 to 127, all different within a row; in each aligned block of 128 rows (0 to 127, 128 to 255, ...) at most 4 rows name the same one
- gates: float32 [32768, 2], P(('expert', 'rep')), may hold values from 0.1 to 1
- gate_w: bfloat16 [128, 2048, 768], P('expert', 'rep'), may hold values from -0.125 to 0.125
- up_w: bfloat16 [128, 2048, 768], P('expert', 'rep'), may hold values from -0.125 to 0.125
- down_w: bfloat16 [128, 768, 2048], P('expert', None, 'rep'), may hold values from -0.21875 to 0.21875
Outputs:
- input_grad: bfloat16 [32768, 2048], P(('expert', 'rep'))
- gate_w_grad: bfloat16 [128, 2048, 768], P('expert', 'rep')
- up_w_grad: bfloat16 [128, 2048, 768], P('expert', 'rep')
- down_w_grad: bfloat16 [128, 768, 2048], P('expert', None, 'rep')
Inputs may be any that keep to these rules, and one draw needn't show every extreme that they name: `expert_ids`: each row names 2 different experts; within the 128 rows of one device no expert is named more than 4 times.
All inputs are finite; a program needn't handle non-finite values.
Results may differ from a plain program's by a relative error of at most 0.0065.
Values may be sent and summed in bfloat16 or wider, within the bound.
No kernel may reach another device: no remote copies, remote signals or barrier semaphores. Data moves between devices by JAX's collectives and lax.ppermute only.
A program may use at most 128 MiB of HBM per device.

v0:
```python
import jax
import jax.numpy as jnp
from jax import lax
from jax.sharding import PartitionSpec as P


def arrange(received, owners, local_exp, capacity):
    feature_n = received.shape[1]
    shaped = received.reshape(owners, local_exp, capacity, feature_n)
    return shaped.transpose(1, 0, 2, 3).reshape(local_exp, owners * capacity, feature_n)


def restore(slot_rows, owners, capacity):
    local_exp = slot_rows.shape[0]
    feature_n = slot_rows.shape[2]
    shaped = slot_rows.reshape(local_exp, owners, capacity, feature_n)
    return shaped.transpose(1, 0, 2, 3).reshape(owners * local_exp * capacity, feature_n)


def local(inputs, out_grad, expert_ids, gates, gate_w, up_w, down_w):
    tok_dev = inputs.shape[0]
    feature_n = inputs.shape[1]
    topk_n = expert_ids.shape[1]
    local_exp = gate_w.shape[0]
    owners = lax.axis_size("expert")
    expert_total = local_exp * owners
    capacity = 2 * tok_dev * topk_n // expert_total
    pair_count = tok_dev * topk_n
    slot_total = expert_total * capacity
    flat_ids = expert_ids.reshape(pair_count)
    one_hot = (flat_ids[:, None] == jnp.arange(expert_total, dtype=jnp.int32)[None, :]).astype(
        jnp.int32
    )
    rank_index = (
        jnp.sum(jnp.cumsum(one_hot, axis=0, dtype=jnp.int32) * one_hot, axis=1, dtype=jnp.int32) - 1
    )
    slot_index = flat_ids * capacity + rank_index
    input_pairs = jnp.repeat(inputs, topk_n, axis=0)
    scaled_pairs = (
        gates.reshape(pair_count, 1) * jnp.repeat(out_grad, topk_n, axis=0).astype(jnp.float32)
    ).astype(jnp.bfloat16)
    send_inputs = jnp.zeros((slot_total, feature_n), jnp.bfloat16).at[slot_index].set(input_pairs)
    send_grads = jnp.zeros((slot_total, feature_n), jnp.bfloat16).at[slot_index].set(scaled_pairs)
    full_gate, full_up, full_down = (
        lax.all_gather(gate_w, "rep", axis=1, tiled=True),
        lax.all_gather(up_w, "rep", axis=1, tiled=True),
        lax.all_gather(down_w, "rep", axis=2, tiled=True),
    )
    recv_inputs, recv_grads = (
        lax.all_to_all(send_inputs, "expert", split_axis=0, concat_axis=0, tiled=True),
        lax.all_to_all(send_grads, "expert", split_axis=0, concat_axis=0, tiled=True),
    )
    rows_in = arrange(recv_inputs, owners, local_exp, capacity)
    scaled_rows = arrange(recv_grads, owners, local_exp, capacity)
    gate_act = jnp.einsum("erd,edh->erh", rows_in, full_gate, preferred_element_type=jnp.float32)
    up_act = jnp.einsum("erd,edh->erh", rows_in, full_up, preferred_element_type=jnp.float32)
    gate_act, up_act = (gate_act, up_act)
    sigma = jax.nn.sigmoid(gate_act)
    silu_val = gate_act * sigma
    hidden = (silu_val * up_act).astype(jnp.bfloat16)
    hidden_grad = jnp.einsum(
        "erd,ehd->erh", scaled_rows, full_down, preferred_element_type=jnp.float32
    )
    gate_grad = (hidden_grad * up_act * sigma * (1.0 + gate_act * (1.0 - sigma))).astype(
        jnp.bfloat16
    )
    up_grad = (hidden_grad * silu_val).astype(jnp.bfloat16)
    first = jnp.einsum("erh,edh->erd", gate_grad, full_gate, preferred_element_type=jnp.float32)
    slot_grad = (
        first + jnp.einsum("erh,edh->erd", up_grad, full_up, preferred_element_type=jnp.float32)
    ).astype(jnp.bfloat16)
    returned = lax.all_to_all(
        restore(slot_grad, owners, capacity), "expert", split_axis=0, concat_axis=0, tiled=True
    )
    gate_part = jnp.einsum("erd,erh->edh", rows_in, gate_grad, preferred_element_type=jnp.float32)
    up_part = jnp.einsum("erd,erh->edh", rows_in, up_grad, preferred_element_type=jnp.float32)
    down_part = jnp.einsum("erh,erd->ehd", hidden, scaled_rows, preferred_element_type=jnp.float32)
    gate_sum, up_sum, down_sum = (
        lax.psum_scatter(
            gate_part.astype(jnp.bfloat16), "rep", scatter_dimension=1, tiled=True
        ).astype(jnp.float32),
        lax.psum_scatter(
            up_part.astype(jnp.bfloat16), "rep", scatter_dimension=1, tiled=True
        ).astype(jnp.float32),
        lax.psum_scatter(
            down_part.astype(jnp.bfloat16), "rep", scatter_dimension=2, tiled=True
        ).astype(jnp.float32),
    )
    picked = returned[slot_index]
    input_grad = jnp.sum(
        picked.reshape(tok_dev, topk_n, feature_n).astype(jnp.float32), axis=1
    ).astype(jnp.bfloat16)
    return (
        input_grad,
        gate_sum.astype(jnp.bfloat16),
        up_sum.astype(jnp.bfloat16),
        down_sum.astype(jnp.bfloat16),
    )


def solution(mesh):
    return jax.shard_map(
        local,
        mesh=mesh,
        in_specs=(
            P(("expert", "rep"), None),
            P(("expert", "rep"), None),
            P(("expert", "rep"), None),
            P(("expert", "rep"), None),
            P("expert", "rep", None),
            P("expert", "rep", None),
            P("expert", None, "rep"),
        ),
        out_specs=(
            P(("expert", "rep"), None),
            P("expert", "rep", None),
            P("expert", "rep", None),
            P("expert", None, "rep"),
        ),
        check_vma=False,
    )
```

profile of v0, /device:TPU:32, one launch (start us, length us, event | category | flops | bytes accessed | tf_op | source)
XLA Modules:
  0.0 258.0 jit_solution(5080837638696863641)
XLA Ops:
  11.9 2.8 %scatter_custom_fusion.1 = bf16[512,2048]{1,0:T(8,128)(2,1)S(1)} fusion(s32[256]{0:T(256)S(1)} %bitcast.51, bf16[256,2048]{1,0:T(8,128)(2,1)S(1)} %reshape.167, bf16[]{:T(256)} %constant.6.clone.1), kind=kCustom, calls=%fused_computation.28 | custom fusion | bytes 2097154 | tf_op jit(solution)/shard_map/scatter | solution.py:42
  14.7 2.3 all_to_all.27
  17.0 15.5 %all-to-all-start.1 = ((bf16[128,4,2048]{2,1,0:T(4,128)(2,1)}), bf16[128,4,2048]{2,1,0:T(4,128)(2,1)}, u32[]{:S(2)}, u32[]{:S(2)}) async-start(bf16[128,4,2048]{2,1,0:T(4,128)(2,1)} %all_to_all.27), calls=%async_computation.1 | async-start | bytes 4194304 | tf_op jit(solution)/shard_map/all_to_all | solution.py:50
  34.3 2.4 broadcast_in_dim.4
  36.6 2.7 %convert_element_type.59 = f32[256,2048]{1,0:T(8,128)S(1)} reshape(f32[128,2,2048]{2,1,0:T(2,128)} %broadcast_in_dim.4) | data formatting | bytes 4194304 | tf_op jit(solution)/shard_map/convert_element_type | solution.py:40
  39.3 3.8 %scatter_custom_fusion = bf16[512,2048]{1,0:T(8,128)(2,1)} fusion(s32[256]{0:T(256)S(1)} %bitcast.52, f32[256,2048]{1,0:T(8,128)S(1)} %convert_element_type.59, f32[256]{0:T(256)S(1)} %mul.61, bf16[]{:T(256)} %constant.6.clone.1), kind=kCustom, calls=%fused_computation.26 | custom fusion | flops 1048576 | bytes 4195330 | tf_op jit(solution)/shard_map/scatter | solution.py:43
  43.1 4.1 %all_to_all.24 = bf16[128,4,2048]{2,1,0:T(4,128)(2,1)} reshape(bf16[512,2048]{1,0:T(8,128)(2,1)} %scatter_custom_fusion) | data formatting | bytes 4194304 | tf_op jit(solution)/shard_map/all_to_all | solution.py:51
  47.2 38.7 %all-to-all-done.1 = bf16[128,4,2048]{2,1,0:T(4,128)(2,1)} async-done(((bf16[128,4,2048]{2,1,0:T(4,128)(2,1)}), bf16[128,4,2048]{2,1,0:T(4,128)(2,1)}, u32[]{:S(2)}, u32[]{:S(2)}) %all-to-all-start.1) | async-done | bytes 2097184 | tf_op jit(solution)/shard_map/all_to_all | solution.py:50
  86.0 6.8 %all-to-all-start = ((bf16[128,4,2048]{2,1,0:T(4,128)(2,1)}), bf16[128,4,2048]{2,1,0:T(4,128)(2,1)S(1)}, u32[]{:S(2)}, u32[]{:S(2)}) async-start(bf16[128,4,2048]{2,1,0:T(4,128)(2,1)} %all_to_all.24), calls=%async_computation | async-start | bytes 4194304 | tf_op jit(solution)/shard_map/all_to_all | solution.py:51
  93.6 4.0 %all_to_all.29 = bf16[512,2048]{1,0:T(8,128)(2,1)} reshape(bf16[128,4,2048]{2,1,0:T(4,128)(2,1)} %all-to-all-done.1) | data formatting | bytes 4194304 | tf_op jit(solution)/shard_map/all_to_all | solution.py:50
  97.5 47.5 %all-to-all-done = bf16[128,4,2048]{2,1,0:T(4,128)(2,1)S(1)} async-done(((bf16[128,4,2048]{2,1,0:T(4,128)(2,1)}), bf16[128,4,2048]{2,1,0:T(4,128)(2,1)S(1)}, u32[]{:S(2)}, u32[]{:S(2)}) %all-to-all-start) | async-done | bytes 2097184 | tf_op jit(solution)/shard_map/all_to_all | solution.py:51
  145.1 2.1 all_to_all.26
  147.1 5.6 %fusion.2 = f32[512,768]{1,0:T(8,128)} fusion(bf16[512,2048]{1,0:T(8,128)(2,1)} %all_to_all.29, bf16[1,2048,768]{2,1,0:T(8,128)(2,1)} %all-gather.8.cloned.1.call-done), kind=kOutput, calls=%fused_computation.9 | convolution fusion | flops 1610612736 | bytes 6815744 | tf_op jit(solution)/shard_map/erd,edh->erh/dot_general | solution.py:55
  152.8 3.8 %fusion.6 = f32[512,768]{1,0:T(8,128)S(1)} fusion(bf16[512,2048]{1,0:T(8,128)(2,1)S(1)} %copy-done, bf16[1,2048,768]{2,1,0:T(8,128)(2,1)} %all-gather.6.cloned.1.call-done), kind=kOutput, calls=%fused_computation.13 | convolution fusion | flops 1610612736 | bytes 6815744 | tf_op jit(solution)/shard_map/erd,edh->erh/dot_general | solution.py:56
  157.7 3.6 %fusion.12 = bf16[1,768,2048]{2,1,0:T(8,128)(2,1)} fusion(bf16[512,2048]{1,0:T(8,128)(2,1)S(1)} %copy-done.1, f32[512,768]{1,0:T(8,128)S(1)} %fusion.6, f32[512,768]{1,0:T(8,128)S(1)} %copy-done.9), kind=kOutput, calls=%fused_computation.19 | convolution fusion | flops 1614544896 | bytes 8388608 | tf_op jit(solution)/shard_map/erh,erd->ehd/dot_general | solution.py:77
  161.4 6.6 %multiply_convert_fusion.2 = (bf16[512,768]{1,0:T(8,128)(2,1)S(1)}, bf16[512,768]{1,0:T(8,128)(2,1)}) fusion(f32[512,768]{1,0:T(8,128)} %fusion.2, f32[512,768]{1,0:T(8,128)} %copy-done.10, bf16[512,2048]{1,0:T(8,128)(2,1)} %all_to_all.26, bf16[1,768,2048]{2,1,0:T(8,128)(2,1)} %all-gather.4.cloned.1.call-done), kind=kOutput, calls=%fused_computation.22 | convolution fusion | flops 1615724544 | bytes 9961472 | tf_op jit(solution)/shard_map/erd,ehd->erh/dot_general | solution.py:61
  168.0 3.5 %fusion.11 = bf16[1,2048,768]{2,1,0:T(8,128)(2,1)} fusion(bf16[512,2048]{1,0:T(8,128)(2,1)S(1)} %copy-done, bf16[512,768]{1,0:T(8,128)(2,1)S(1)} %get-tuple-element.4), kind=kOutput, calls=%fused_computation.18 | convolution fusion | flops 1612185600 | bytes 6029312 | tf_op jit(solution)/shard_map/erd,erh->edh/dot_general | solution.py:76
  172.6 3.5 %fusion.10 = bf16[1,2048,768]{2,1,0:T(8,128)(2,1)} fusion(bf16[512,2048]{1,0:T(8,128)(2,1)S(1)} %copy-done, bf16[512,768]{1,0:T(8,128)(2,1)S(1)} %copy-done.8), kind=kOutput, calls=%fused_computation.17 | convolution fusion | flops 1612185600 | bytes 6029312 | tf_op jit(solution)/shard_map/erd,erh->edh/dot_general | solution.py:75
  178.0 3.1 %fusion = f32[512,2048]{1,0:T(8,128)S(1)} fusion(bf16[512,768]{1,0:T(8,128)(2,1)} %get-tuple-element.5, bf16[1,2048,768]{2,1,0:T(8,128)(2,1)S(1)} %copy-done.4), kind=kOutput, calls=%fused_computation.7 | convolution fusion | flops 1610612736 | bytes 8126464 | tf_op jit(solution)/shard_map/erh,edh->erd/dot_general | solution.py:68
  183.0 2.2 all_to_all.30
  185.2 7.7 %all-to-all-start.2 = ((bf16[128,4,2048]{2,1,0:T(4,128)(2,1)}), bf16[128,4,2048]{2,1,0:T(4,128)(2,1)}, u32[]{:S(2)}, u32[]{:S(2)}) async-start(bf16[128,4,2048]{2,1,0:T(4,128)(2,1)} %all_to_all.30), calls=%async_computation.2 | async-start | bytes 4194304 | tf_op jit(solution)/shard_map/all_to_all | solution.py:72
  192.9 49.9 %all-to-all-done.2 = bf16[128,4,2048]{2,1,0:T(4,128)(2,1)} async-done(((bf16[128,4,2048]{2,1,0:T(4,128)(2,1)}), bf16[128,4,2048]{2,1,0:T(4,128)(2,1)}, u32[]{:S(2)}, u32[]{:S(2)}) %all-to-all-start.2) | async-done | bytes 2097184 | tf_op jit(solution)/shard_map/all_to_all | solution.py:72
  242.8 2.5 all_to_all.32
  247.5 3.6 %reduce_sum.22 = bf16[128,2048]{1,0:T(8,128)(2,1)} reduce(bf16[128,2,2048]{2,1,0:T(2,128)(2,1)S(1)} %reshape.146, bf16[]{:T(256)} %constant.6.clone.1), dimensions={1}, to_apply=%region_5.6 | reduce | flops 262144 | bytes 1572866 | tf_op jit(solution)/shard_map/reduce_sum | solution.py:90
  (65 shorter events, 15.3 us)
Async XLA Ops:
  17.0 68.9 %all-to-all-start.1 = ((bf16[128,4,2048]{2,1,0:T(4,128)(2,1)}), bf16[128,4,2048]{2,1,0:T(4,128)(2,1)}, u32[]{:S(2)}, u32[]{:S(2)}) async-start(bf16[128,4,2048]{2,1,0:T(4,128)(2,1)} %all_to_all.27), calls=%async_computation.1 | async-start | bytes 4194304 | tf_op jit(solution)/shard_map/all_to_all | solution.py:50
  32.5 1.5 copy-start.3
  32.5 1.8 copy-start.2
  32.5 114.6 %all-gather.8.cloned.1.call-start = ((), (), s32[]{:S(2)}) async-start(), calls=%async_computation.8 | async-start | bytes 4718592 | tf_op jit(solution)/shard_map/all_gather | solution.py:45
  33.2 119.5 %all-gather.6.cloned.1.call-start = ((), (), s32[]{:S(2)}) async-start(), calls=%async_computation.7 | async-start | bytes 4718592 | tf_op jit(solution)/shard_map/all_gather | solution.py:46
  86.0 59.1 %all-to-all-start = ((bf16[128,4,2048]{2,1,0:T(4,128)(2,1)}), bf16[128,4,2048]{2,1,0:T(4,128)(2,1)S(1)}, u32[]{:S(2)}, u32[]{:S(2)}) async-start(bf16[128,4,2048]{2,1,0:T(4,128)(2,1)} %all_to_all.24), calls=%async_computation | async-start | bytes 4194304 | tf_op jit(solution)/shard_map/all_to_all | solution.py:51
  92.8 68.6 %all-gather.4.cloned.1.call-start = ((), (), s32[]{:S(2)}) async-start(), calls=%async_computation.6 | async-start | bytes 4718592 | tf_op jit(solution)/shard_map/all_gather | solution.py:47
  93.5 157.6 %reduce-scatter.8.cloned.1.call-start = ((), (), s32[]{:S(2)}) async-start(), calls=%async_computation.11 | async-start | bytes 4718592 | tf_op jit(solution)/shard_map/reduce_scatter | solution.py:85
  147.1 5.6 %copy-start = (bf16[512,2048]{1,0:T(8,128)(2,1)S(1)}, bf16[512,2048]{1,0:T(8,128)(2,1)}, u32[]{:S(2)}) copy-start(bf16[512,2048]{1,0:T(8,128)(2,1)} %all_to_all.29) | copy-start | bytes 6291460
  152.7 5.0 %copy-start.1 = (bf16[512,2048]{1,0:T(8,128)(2,1)S(1)}, bf16[512,2048]{1,0:T(8,128)(2,1)}, u32[]{:S(2)}) copy-start(bf16[512,2048]{1,0:T(8,128)(2,1)} %all_to_all.26) | copy-start | bytes 6291460
  152.7 5.0 %copy-start.9 = (f32[512,768]{1,0:T(8,128)S(1)}, f32[512,768]{1,0:T(8,128)}, u32[]{:S(2)}) copy-start(f32[512,768]{1,0:T(8,128)} %fusion.2) | copy-start | bytes 4718596
  156.6 1.1 copy-start.10
  161.4 89.8 %reduce-scatter.6.cloned.1.call-start = ((), (), s32[]{:S(2)}) async-start(), calls=%async_computation.10 | async-start | bytes 4718592 | tf_op jit(solution)/shard_map/reduce_scatter | solution.py:82
  168.0 3.5 %copy-start.6 = (bf16[512,768]{1,0:T(8,128)(2,1)}, bf16[512,768]{1,0:T(8,128)(2,1)S(1)}, u32[]{:S(2)}) copy-start(bf16[512,768]{1,0:T(8,128)(2,1)S(1)} %get-tuple-element.4) | copy-start | bytes 2359300
  171.5 1.1 copy-start.8
  171.5 79.6 %reduce-scatter.4.cloned.1.call-start = ((), (), s32[]{:S(2)}) async-start(), calls=%async_computation.9 | async-start | bytes 4718592 | tf_op jit(solution)/shard_map/reduce_scatter | solution.py:79
  176.1 1.9 copy-start.4
  178.0 3.1 %copy-start.5 = (bf16[1,2048,768]{2,1,0:T(8,128)(2,1)S(1)}, bf16[1,2048,768]{2,1,0:T(8,128)(2,1)}, u32[]{:S(2)}) copy-start(bf16[1,2048,768]{2,1,0:T(8,128)(2,1)} %all-gather.6.cloned.1.call-done) | copy-start | bytes 9437188
  178.0 3.1 %copy-start.7 = (bf16[512,768]{1,0:T(8,128)(2,1)S(1)}, bf16[512,768]{1,0:T(8,128)(2,1)}, u32[]{:S(2)}) copy-start(bf16[512,768]{1,0:T(8,128)(2,1)} %copy-done.6) | copy-start | bytes 2359300
  185.2 57.7 %all-to-all-start.2 = ((bf16[128,4,2048]{2,1,0:T(4,128)(2,1)}), bf16[128,4,2048]{2,1,0:T(4,128)(2,1)}, u32[]{:S(2)}, u32[]{:S(2)}) async-start(bf16[128,4,2048]{2,1,0:T(4,128)(2,1)} %all_to_all.30), calls=%async_computation.2 | async-start | bytes 4194304 | tf_op jit(solution)/shard_map/all_to_all | solution.py:72
Sparse Core Ops, SparseCore 0:
  35.1 18.8 all-gather.7
  55.9 18.7 all-gather.5
  95.4 18.9 all-gather.3
  161.5 9.2 reduce-scatter.7
  173.8 17.5 reduce-scatter.5
  194.3 17.4 reduce-scatter.3
where the time goes:
time: 259 us; the launch traced here: 258 us
  waiting for transfers between devices  138 us (53%)
  local copies, waits for them, and re-layouts  34.8 us (13%)
  matrix products  31.5 us (12%)
  starting transfers between devices  30.5 us (12%)
  between operations  14.4 us (6%)
  other arithmetic  8.56 us (3%)
    all_to_all x1, waiting for transfers between devices, local(): lax.all_to_all(restore(slot_grad, owners, capacity), 'expert', split_axis...  49.9 us
    all_to_all x1, waiting for transfers between devices, local(): lax.all_to_all(send_grads, 'expert', split_axis=0, concat_axis=0, tiled=T...  47.5 us
    all_to_all x1, waiting for transfers between devices, local(): lax.all_to_all(send_inputs, 'expert', split_axis=0, concat_axis=0, tiled=...  38.7 us
    all_to_all x1, starting transfers between devices, local(): lax.all_to_all(send_inputs, 'expert', split_axis=0, concat_axis=0, tiled=...  15.5 us
    all_to_all x1, starting transfers between devices, local(): lax.all_to_all(restore(slot_grad, owners, capacity), 'expert', split_axis...  7.72 us
    all_to_all x1, starting transfers between devices, local(): lax.all_to_all(send_grads, 'expert', split_axis=0, concat_axis=0, tiled=T...  6.84 us
    dot_general x1, matrix products, local(): jnp.einsum('erd,ehd->erh', scaled_rows, full_down, preferred_element_type...  6.56 us
    all_to_all x2, local copies, waits for them, and re-layouts, local(): lax.all_to_all(send_inputs, 'expert', split_axis=0, concat_axis=0, tiled=...  6.22 us
  transfers between devices with their start and end apart: 9, of which 3 were waited for; matrix products, arithmetic and copies ran while one was open for 18% of the time, Pallas kernels for 0%

commit v1 on v0

v1 whole, which is shorter than its diff:
```python
import functools

import jax
import jax.numpy as jnp
from jax import lax
from jax.experimental import pallas as pl
from jax.experimental.pallas import tpu as pltpu
from jax.sharding import PartitionSpec as P

RING = 8
CAP = 4
META = 128
HALF = 1024
COLS = 1024
HTILE = 256
WTILE = 256
CHUNKS = ((0,), (1, -1), (2, -2), (3, -3, 4))
BF = jnp.bfloat16
F32 = jnp.float32
VMEM_LIMIT = 32 * 1024 * 1024
TOKEN_COST = pl.CostEstimate(flops=1, bytes_accessed=1, transcendentals=0)


def far_memory(values):
    return [pltpu.with_memory_space_constraint(value, pltpu.HBM) for value in values]


def dot(a, b, ca, cb):
    return lax.dot_general(a, b, (((ca,), (cb,)), ((), ())), preferred_element_type=F32)


def by_token(columns):
    tokens = columns.shape[0]
    same = lax.broadcasted_iota(jnp.int32, (tokens, tokens), 0) == lax.broadcasted_iota(
        jnp.int32, (tokens, tokens), 1
    )
    return dot(columns, same.astype(F32).astype(BF), 0, 0)


def hits(meta, owner, slot):
    tokens = meta.shape[1]
    first = owner == meta[0:1, :].astype(jnp.int32)
    second = owner == meta[1:2, :].astype(jnp.int32)
    named = (first | second).astype(F32).astype(BF)
    before = (
        lax.broadcasted_iota(jnp.int32, (tokens, tokens), 0)
        < lax.broadcasted_iota(jnp.int32, (tokens, tokens), 1)
    )
    rank = dot(named, before.astype(F32).astype(BF), 1, 0)
    hit = (first | second) & (rank.astype(jnp.int32) == slot)
    gate_first = meta[2:3, :] + meta[3:4, :] + meta[4:5, :]
    gate_second = meta[5:6, :] + meta[6:7, :] + meta[7:8, :]
    gate = jnp.where(first, gate_first, 0.0) + jnp.where(second, gate_second, 0.0)
    return hit, jnp.sum(jnp.where(hit, gate, 0.0), axis=1, keepdims=True)


def pack_kernel(x_ref, grad_ref, ids_ref, gates_ref, out_ref):
    width = x_ref.shape[1]
    tokens = x_ref.shape[0]
    out_ref[:, 0:width] = x_ref[...]
    out_ref[:, width : 2 * width] = grad_ref[...]
    lane = lax.broadcasted_iota(jnp.int32, (tokens, META), 1)
    packed = jnp.zeros((tokens, META), F32)
    for k in range(2):
        packed = jnp.where(lane == k, ids_ref[:, k : k + 1].astype(F32), packed)
        rest = gates_ref[:, k : k + 1]
        for part in range(3):
            piece = rest.astype(BF).astype(F32)
            packed = jnp.where(lane == 2 + 3 * k + part, piece, packed)
            rest = rest - piece
    out_ref[:, 2 * width :] = packed.astype(BF)


def pack(x, grad, ids, gates):
    return pl.pallas_call(
        pack_kernel,
        out_shape=jax.ShapeDtypeStruct((x.shape[0], 2 * x.shape[1] + META), BF),
        compiler_params=pltpu.CompilerParams(vmem_limit_bytes=VMEM_LIMIT),
        cost_estimate=TOKEN_COST,
    )(*far_memory([x, grad]), ids, gates)


def build_kernel(jobs, sources, outs, waits, place_ref, *refs):
    refs = refs[waits:]
    metas, data = refs[:sources], refs[sources : 3 * sources]
    out_refs, picks = refs[3 * sources : 3 * sources + outs], refs[3 * sources + outs :]
    place = place_ref[0]

    @pl.when(pl.program_id(0) == 0)
    def _():
        by = [by_token(meta[...]) for meta in metas]
        for number, (source, offset, start, groups, _, _, _) in enumerate(jobs):
            pick, scale = picks[2 * number], picks[2 * number + 1]
            row = lax.broadcasted_iota(jnp.int32, (groups * 2 * CAP, 128), 0)
            owner = ((row >> 3) + start) * RING + lax.rem(place + offset + RING, RING)
            is_grad = ((row >> 2) & 1) == 1
            hit, gate = hits(by[source], owner, row & 3)
            pick[:, 0:128] = (hit & ~is_grad).astype(F32).astype(BF)
            pick[:, 128:256] = (hit & is_grad).astype(F32).astype(BF)
            scale[...] = jnp.where(is_grad, gate, 1.0)

    for number, (source, _, _, groups, out, to, at) in enumerate(jobs):
        stacked = jnp.concatenate([data[2 * source][...], data[2 * source + 1][...]], axis=0)
        value = dot(picks[2 * number][...], stacked, 1, 0) * picks[2 * number + 1][:, 0:1]
        out_refs[out][to : to + groups, at] = value.astype(BF).reshape(
            groups, 2 * CAP, value.shape[1]
        )


def build(jobs, place, planes, shapes, after=()):
    features = (planes[0].shape[1] - META) // 2
    sources = len(planes)
    tokens = planes[0].shape[0]
    steps = features // COLS
    scratch = []
    for job in jobs:
        rows = job[3] * 2 * CAP
        scratch += [pltpu.VMEM((rows, 256), BF), pltpu.VMEM((rows, 128), F32)]
    shapes = [shape + (2 * CAP,) for shape in shapes]
    return pl.pallas_call(
        functools.partial(build_kernel, jobs, sources, len(shapes), len(after)),
        grid=(steps,),
        out_shape=[pltpu.HBM(shape + (features,), BF) for shape in shapes],
        in_specs=[pl.BlockSpec(memory_space=pltpu.SMEM)]
        + [pl.BlockSpec(memory_space=pl.ANY) for _ in after]
        + [pl.BlockSpec((tokens, META), lambda c: (0, 2 * features // META))] * sources
        + [
            pl.BlockSpec((tokens, COLS), lambda c: (0, c)),
            pl.BlockSpec((tokens, COLS), lambda c: (0, c + steps)),
        ]
        * sources,
        out_specs=[pl.BlockSpec(shape + (COLS,), lambda c: (0, 0, 0, c)) for shape in shapes],
        scratch_shapes=scratch,
        compiler_params=pltpu.CompilerParams(vmem_limit_bytes=VMEM_LIMIT),
        cost_estimate=TOKEN_COST,
    )(place, *after, *planes, *[p for p in planes for _ in range(2)])


def join_kernel(left_ref, right_ref, far_left_ref, far_right_ref, after_ref, out_ref):
    del after_ref
    half = far_left_ref.shape[0]
    out_ref[:, 0:1] = left_ref[...]
    out_ref[:, 1:2] = right_ref[...]
    out_ref[0:half, 2:3] = far_left_ref[...]
    out_ref[half:, 2:3] = far_right_ref[...]


def join(third, fourth, groups, after):
    features = third[0].shape[3]
    shape = (groups, 1, 2 * CAP)
    specs = [pl.BlockSpec(shape + (COLS,), lambda c: (0, 0, 0, c))] * 2
    specs += [pl.BlockSpec(v.shape[:3] + (COLS,), lambda c: (0, 0, 0, c)) for v in fourth]
    return pl.pallas_call(
        join_kernel,
        grid=(features // COLS,),
        out_shape=pltpu.HBM((groups, 3, 2 * CAP, features), BF),
        in_specs=specs + [pl.BlockSpec(memory_space=pl.ANY)],
        out_specs=pl.BlockSpec((groups, 3, 2 * CAP, COLS), lambda c: (0, 0, 0, c)),
        compiler_params=pltpu.CompilerParams(vmem_limit_bytes=VMEM_LIMIT),
        cost_estimate=TOKEN_COST,
    )(*third, *fourth, after)


def expert_kernel(chunks, groups, place_ref, *refs):
    recvs, refs = refs[: len(chunks)], refs[len(chunks) :]
    wg_own, wg_oth, wu_own, wu_oth, wd_own, wd_oth = refs[:6]
    x_own, x_oth, s_own, s_oth, hid_ref, gg_ref, ug_ref, back = refs[6:14]
    acc_own, acc_oth, stage, sems = refs[14:]
    step = pl.program_id(0)
    place = place_ref[0]
    rep = place_ref[1]

    @pl.when(step == 0)
    def _():
        start = 0
        for recv, planes in zip(recvs, chunks):
            slots = groups * len(planes) * CAP
            row = lax.broadcasted_iota(jnp.int32, (slots, 2 * slots), 0)
            col = lax.broadcasted_iota(jnp.int32, (slots, 2 * slots), 1)
            source = (row >> 2) * 8 + (row & 3)
            take_x = (col == source).astype(F32).astype(BF)
            take_s = (col == source + 4).astype(F32).astype(BF)
            for half, x_ref, s_ref in ((rep, x_own, s_own), (1 - rep, x_oth, s_oth)):
                at = pl.ds(pl.multiple_of(half * HALF, HALF), HALF)
                rows = recv[:, :, :, at].reshape(2 * slots, HALF)
                x_ref[start : start + slots] = dot(take_x, rows, 1, 0).astype(BF)
                s_ref[start : start + slots] = dot(take_s, rows, 1, 0).astype(BF)
            start += slots

    gate = dot(x_own[...], wg_own[...], 1, 0) + dot(x_oth[...], wg_oth[...], 1, 0)
    up = dot(x_own[...], wu_own[...], 1, 0) + dot(x_oth[...], wu_oth[...], 1, 0)
    hidden_grad = dot(s_own[...], wd_own[...], 1, 1) + dot(s_oth[...], wd_oth[...], 1, 1)
    sigma = jax.nn.sigmoid(gate)
    silu = gate * sigma
    hid_ref[...] = (silu * up).astype(BF)
    gate_grad = (hidden_grad * up * sigma * (1.0 + gate * (1.0 - sigma))).astype(BF)
    up_grad = (hidden_grad * silu).astype(BF)
    gg_ref[...] = gate_grad
    ug_ref[...] = up_grad
    new_own = dot(gate_grad, wg_own[...], 1, 1) + dot(up_grad, wu_own[...], 1, 1)
    new_oth = dot(gate_grad, wg_oth[...], 1, 1) + dot(up_grad, wu_oth[...], 1, 1)

    @pl.when(step == 0)
    def _():
        acc_own[...] = new_own
        acc_oth[...] = new_oth

    @pl.when(step > 0)
    def _():
        acc_own[...] += new_own
        acc_oth[...] += new_oth

    @pl.when(step == pl.num_programs(0) - 1)
    def _():
        start = 0
        first = 0
        copies = []
        for planes in chunks:
            count = len(planes)
            slots = groups * count * CAP
            row = lax.broadcasted_iota(jnp.int32, (2 * slots, slots), 0)
            col = lax.broadcasted_iota(jnp.int32, (2 * slots, slots), 1)
            same = ((row >> 3) == (col >> 2)) & ((row & 3) == (col & 3))
            upper = (row >> 2) & 1
            put_own = (same & (upper == rep)).astype(F32).astype(BF)
            put_oth = (same & (upper != rep)).astype(F32).astype(BF)
            mixed = dot(put_own, acc_own[start : start + slots].astype(BF), 1, 0) + dot(
                put_oth, acc_oth[start : start + slots].astype(BF), 1, 0
            )
            stage[:, first : first + count] = mixed.astype(BF).reshape(
                groups, count, 2 * CAP, HALF
            )
            for index, plane in enumerate(planes):
                copy = pltpu.make_async_copy(
                    stage.at[:, first + index],
                    back.at[:, lax.rem(place - plane + RING, RING)],
                    sems.at[first + index],
                )
                copy.start()
                copies.append(copy)
            start += slots
            first += count
        for copy in copies:
            copy.wait()


def experts(chunks, groups, place, recvs, weights):
    slots = groups * RING * CAP
    hidden = weights[0].shape[1]
    wide = pl.BlockSpec((HALF, HTILE), lambda h: (0, h))
    tall = pl.BlockSpec((HTILE, HALF), lambda h: (h, 0))
    rows = pl.BlockSpec((slots, HALF), lambda h: (0, 0))
    tile = pl.BlockSpec((slots, HTILE), lambda h: (0, h))
    return pl.pallas_call(
        functools.partial(expert_kernel, chunks, groups),
        grid=(hidden // HTILE,),
        out_shape=(
            [pltpu.HBM((slots, HALF), BF)] * 4
            + [pltpu.HBM((slots, hidden), BF)] * 3
            + [pltpu.HBM((groups, RING, 2 * CAP, HALF), BF)]
        ),
        in_specs=[pl.BlockSpec(memory_space=pltpu.SMEM)]
        + [
            pl.BlockSpec(r.shape, lambda h: (0, 0, 0, 0), pipeline_mode=pl.Buffered(1))
            for r in recvs
        ]
        + [wide] * 4
        + [tall] * 2,
        out_specs=[rows] * 4 + [tile] * 3 + [pl.BlockSpec(memory_space=pl.ANY)],
        scratch_shapes=[
            pltpu.VMEM((slots, HALF), F32),
            pltpu.VMEM((slots, HALF), F32),
            pltpu.VMEM((groups, RING, 2 * CAP, HALF), BF),
            pltpu.SemaphoreType.DMA((RING,)),
        ],
        compiler_params=pltpu.CompilerParams(vmem_limit_bytes=48 * 1024 * 1024),
        cost_estimate=TOKEN_COST,
    )(place, *far_memory(recvs[:3]), recvs[3], *far_memory(weights))


def weight_kernel(has_sum, x_ref, s_ref, gate_ref, up_ref, hid_ref, *refs):
    outs = refs[-3:]
    parts = (
        dot(x_ref[...], gate_ref[...], 0, 0),
        dot(x_ref[...], up_ref[...], 0, 0),
        dot(hid_ref[...], s_ref[...], 0, 0),
    )
    for index, part in enumerate(parts):
        part = part.astype(BF)
        if has_sum:
            part = (part.astype(F32) + refs[index][...].astype(F32)).astype(BF)
        outs[index][...] = part


def weight_grads(x, s, gate, up, hid, received):
    slots, hidden = gate.shape
    wide = pl.BlockSpec((WTILE, hidden), lambda c: (c, 0))
    tall = pl.BlockSpec((hidden, WTILE), lambda c: (0, c))
    part_specs = [wide, wide, tall]
    return pl.pallas_call(
        functools.partial(weight_kernel, bool(received)),
        grid=(HALF // WTILE,),
        out_shape=[
            pltpu.HBM((HALF, hidden), BF),
            pltpu.HBM((HALF, hidden), BF),
            pltpu.HBM((hidden, HALF), BF),
        ],
        in_specs=[pl.BlockSpec((slots, WTILE), lambda c: (0, c))] * 2
        + [pl.BlockSpec((slots, hidden), lambda c: (0, 0))] * 3
        + (part_specs if received else []),
        out_specs=part_specs,
        compiler_params=pltpu.CompilerParams(vmem_limit_bytes=VMEM_LIMIT),
        cost_estimate=TOKEN_COST,
    )(*far_memory([x, s, gate, up, hid]), *received)


def combine_kernel(meta_ref, back_ref, out_ref):
    rows = back_ref.shape[0]
    row = lax.broadcasted_iota(jnp.int32, (rows, 128), 0)
    hit, _ = hits(by_token(meta_ref[...]), row >> 3, row & 3)
    upper = ((row >> 2) & 1) == 1
    low = (hit & ~upper).astype(F32).astype(BF)
    high = (hit & upper).astype(F32).astype(BF)
    out_ref[:, 0:HALF] = dot(low, back_ref[...], 0, 0).astype(BF)
    out_ref[:, HALF : 2 * HALF] = dot(high, back_ref[...], 0, 0).astype(BF)


def combine(packed, back):
    rows = back.shape[0]
    return pl.pallas_call(
        combine_kernel,
        grid=(1,),
        out_shape=jax.ShapeDtypeStruct((128, 2 * HALF), BF),
        in_specs=[
            pl.BlockSpec((128, META), lambda c: (0, 4 * HALF // META)),
            pl.BlockSpec((rows, HALF), lambda c: (0, 0)),
        ],
        out_specs=pl.BlockSpec((128, 2 * HALF), lambda c: (0, 0)),
        compiler_params=pltpu.CompilerParams(vmem_limit_bytes=VMEM_LIMIT),
        cost_estimate=TOKEN_COST,
    )(packed, back)


def local(inputs, out_grad, expert_ids, gates, gate_w, up_w, down_w):
    owners = lax.axis_size("expert")
    groups = owners // RING
    across = [[g * RING + z for g in range(groups)] for z in range(RING)]
    place = jnp.stack(
        [lax.rem(lax.axis_index("expert"), RING), lax.axis_index("rep")]
    ).astype(jnp.int32)

    def hop(value, by):
        pairs = [(g * RING + z, g * RING + (z + by) % RING) for g in range(groups) for z in range(RING)]
        return lax.ppermute(value, "expert", pairs)

    def swap(value):
        return lax.ppermute(value, "rep", [(0, 1), (1, 0)])

    packed = pack(inputs, out_grad, expert_ids, gates)
    data = {0: packed, 1: hop(packed, 1), -1: hop(packed, -1)}
    own = (gate_w[0], up_w[0], down_w[0])
    oth = tuple(swap(w) for w in own)
    weights = (own[0], oth[0], own[1], oth[1], own[2], oth[2])

    def near(planes, after):
        jobs = tuple((i, 0, 0, groups, 0, 0, i) for i in range(len(planes)))
        (sent,) = build(
            jobs,
            place,
            [data[p] for p in planes],
            [(groups, len(planes))],
            after,
        )
        return sent

    def exchange(sent):
        return lax.all_to_all(
            sent, "expert", split_axis=0, concat_axis=0, tiled=True, axis_index_groups=across
        )

    recv_own = exchange(near(CHUNKS[0], ()))
    recv_own, data[1], data[-1] = lax.optimization_barrier((recv_own, data[1], data[-1]))
    for by in (1, -1):
        data[2 * by] = hop(data[by], by)
    recv_next = exchange(near(CHUNKS[1], ()))
    half = groups // 2
    far = build(
        (
            (0, 1, 0, groups, 0, 0, 0),
            (0, 2, 0, half, 0, groups, 0),
            (1, -1, 0, groups, 1, 0, 0),
            (1, -2, half, groups - half, 1, groups, 0),
        ),
        place,
        [data[2], data[-2]],
        [(groups + half, 1), (2 * groups - half, 1)],
        (),
    )
    third = (hop(far[0], 1), hop(far[1], -1))
    recv_second = exchange(near(CHUNKS[2], far_memory([far[0], recv_next])))
    fourth = (hop(third[0][groups:], 1), hop(third[1][groups:], -1))
    recv_far = exchange(join(third, fourth, groups, recv_second))
    x_own, x_oth, s_own, s_oth, hid, gate_grad, up_grad, back = experts(
        CHUNKS, groups, place, (recv_own, recv_next, recv_second, recv_far), weights
    )
    returned = lax.all_to_all(
        back.reshape(owners, 2 * CAP, HALF), "expert", split_axis=0, concat_axis=0, tiled=True
    )
    theirs = weight_grads(x_oth, s_oth, gate_grad, up_grad, hid, ())
    received = tuple(swap(part) for part in theirs)
    grads = weight_grads(x_own, s_own, gate_grad, up_grad, hid, received)
    input_grad = combine(packed, returned.reshape(owners * 2 * CAP, HALF))
    return (input_grad, grads[0][None], grads[1][None], grads[2][None])


def solution(mesh):
    return jax.shard_map(
        local,
        mesh=mesh,
        in_specs=(
            P(("expert", "rep"), None),
            P(("expert", "rep"), None),
            P(("expert", "rep"), None),
            P(("expert", "rep"), None),
            P("expert", "rep", None),
            P("expert", "rep", None),
            P("expert", None, "rep"),
        ),
        out_specs=(
            P(("expert", "rep"), None),
            P("expert", "rep", None),
            P("expert", "rep", None),
            P("expert", None, "rep"),
        ),
        check_vma=False,
    )
```

time: 259 us -> 208 us (0.80)
  Pallas kernels: 0 us -> 51.6 us
  waiting for transfers between devices: 138 us -> 88.6 us
  matrix products: 31.5 us -> 0 us
  local copies, waits for them, and re-layouts: 34.8 us -> 5.76 us
  blocking collectives: 0 us -> 18.4 us
  between operations: 14.4 us -> 0.75 us
  starting transfers between devices: 30.5 us -> 42.2 us
  other arithmetic: 8.56 us -> 0.07 us
    all_to_all x3 -> x4, waiting for transfers between devices: 136 us -> 55.2 us  [the longest x1 30.8 us: local(): lax.all_to_all(back.reshape(owners, 2 * CAP, HALF), 'expert', split_axis=...]
    pallas_call x0 -> x10, Pallas kernels: none -> 51.6 us  [the longest x1 22.6 us: experts(): pl.pallas_call(functools.partial(expert_kernel, chunks, groups), grid=(hi...]
    ppermute x0 -> x14, waiting for transfers between devices: none -> 33.4 us  [the longest x8 25.8 us: hop(): return lax.ppermute(value, 'expert', pairs)]
    dot_general x8 -> x0, matrix products: 31.5 us -> none  [the longest x1 6.56 us: local(): jnp.einsum('erd,ehd->erh', scaled_rows, full_down, preferred_element_type...]
    all_to_all x0 -> x1, blocking collectives: none -> 18.4 us  [exchange(): lax.all_to_all(sent, 'expert', split_axis=0, concat_axis=0, tiled=True, a...]
    all_to_all x6 -> x0, local copies, waits for them, and re-layouts: 17.2 us -> none  [the longest x2 6.22 us: local(): lax.all_to_all(send_inputs, 'expert', split_axis=0, concat_axis=0, tiled=...]
    ppermute x0 -> x14, starting transfers between devices: none -> 12.1 us  [the longest x8 10.9 us: hop(): return lax.ppermute(value, 'expert', pairs)]
    broadcast_in_dim x2 -> x0, local copies, waits for them, and re-layouts: 4.05 us -> none  [the longest x1 2.38 us: local(): jnp.repeat(out_grad, topk_n, axis=0).astype(jnp.float32)]
  transfers between devices with their start and end apart: 9 -> 18, of which waited for: 3 -> 11; matrix products, arithmetic and copies ran while one was open for 18% -> 1% of each run, Pallas kernels for 0% -> 12%
where the time goes in v1:
time: 208 us; the launch traced here: 207 us
  waiting for transfers between devices  88.6 us (43%)
  Pallas kernels  51.6 us (25%)
  starting transfers between devices  42.2 us (20%)
  blocking collectives  18.4 us (9%)
  local copies, waits for them, and re-layouts  5.76 us (3%)
    all_to_all x1, waiting for transfers between devices, local(): lax.all_to_all(back.reshape(owners, 2 * CAP, HALF), 'expert', split_axis=...  30.8 us
    ppermute x8, waiting for transfers between devices, hop(): return lax.ppermute(value, 'expert', pairs)  25.8 us
    all_to_all x3, waiting for transfers between devices, exchange(): lax.all_to_all(sent, 'expert', split_axis=0, concat_axis=0, tiled=True, a...  24.4 us
    pallas_call x1, Pallas kernels, experts(): pl.pallas_call(functools.partial(expert_kernel, chunks, groups), grid=(hi...  22.6 us
    all_to_all x3, starting transfers between devices, exchange(): lax.all_to_all(sent, 'expert', split_axis=0, concat_axis=0, tiled=True, a...  21 us
    all_to_all x1, blocking collectives, exchange(): lax.all_to_all(sent, 'expert', split_axis=0, concat_axis=0, tiled=True, a...  18.4 us
    pallas_call x2, Pallas kernels, weight_grads(): pl.pallas_call(functools.partial(weight_kernel, bool(received)), grid=(HA...  12.5 us
    ppermute x8, starting transfers between devices, hop(): return lax.ppermute(value, 'expert', pairs)  10.9 us
  transfers between devices with their start and end apart: 18, of which 11 were waited for; matrix products, arithmetic and copies ran while one was open for 1% of the time, Pallas kernels for 12%

profile of v1, /device:TPU:32, one launch (start us, length us, event | category | flops | bytes accessed | tf_op | source)
XLA Modules:
  0.0 207.3 jit_solution(2141255269836555639)
XLA Ops:
  5.8 2.3 %shard_map.103 = bf16[16,1,8,2048]{3,2,1,0:T(8,128)(2,1)} custom-call(s32[2]{0:T(128)S(1)} %pad_add_fusion.place_ref, bf16[128,4224]{1,0:T(8,128)(2,1)S(1)} %shard_map.102.refs_0_.refs_1_.refs_2_.meta_ref, bf16[128,4224]{1,0:T(8,128)(2,1)S(1)} %shard_map.102.refs_0_.refs_1_.refs_2_.meta_ref, bf16[128,4224]{1,0:T(8,128)(2,1)S(1)} %shard_map.102.refs_0_.refs_1_.refs_2_.meta_ref), custom_call_target="tpu_custom_call" | custom-call | flops 1 | bytes 1 | tf_op jit(solution)/shard_map/pallas_call | solution.py:120
  8.0 18.4 %all_to_all.25.refs_0_ = bf16[16,1,8,2048]{3,2,1,0:T(8,128)(2,1)} all-to-all(bf16[16,1,8,2048]{3,2,1,0:T(8,128)(2,1)} %shard_map.103), channel_id=1, replica_groups={{0,16,32,48,64,80,96,112,128,144,160,176,192,208,224,240},{2,18,34,50,6..., dimensions={0} | all-to-all | bytes 1048576 | tf_op jit(solution)/shard_map/all_to_all | solution.py:377
  26.4 3.0 %collective-permute-done.1.refs_1_.refs_4_.refs_5_ = bf16[128,4224]{1,0:T(8,128)(2,1)S(1)} collective-permute-done((bf16[128,4224]{1,0:T(8,128)(2,1)S(1)}, bf16[128,4224]{1,0:T(8,128)(2,1)S(1)}, u32[]{:S(2)}, u32[]{:S(2)}) %collective-permute-start.1) | collective-permute-done | bytes 1081376 | tf_op jit(solution)/shard_map/ppermute | solution.py:354
  30.4 2.9 %collective-permute-done.refs_0_.refs_2_.refs_3_ = bf16[128,4224]{1,0:T(8,128)(2,1)} collective-permute-done((bf16[128,4224]{1,0:T(8,128)(2,1)S(1)}, bf16[128,4224]{1,0:T(8,128)(2,1)}, u32[]{:S(2)}, u32[]{:S(2)}) %collective-permute-start) | collective-permute-done | bytes 1081376 | tf_op jit(solution)/shard_map/ppermute | solution.py:354
  33.3 3.0 %collective-permute-start.3 = (bf16[128,4224]{1,0:T(8,128)(2,1)}, bf16[128,4224]{1,0:T(8,128)(2,1)S(1)}, u32[]{:S(2)}, u32[]{:S(2)}) collective-permute-start(bf16[128,4224]{1,0:T(8,128)(2,1)} %copy-done), channel_id=1, source_target_pairs={{0,14},{2,0},{4,2},{6,4},{8,6},{10,8},{12,10},{14,12},{16,30},{18,... | collective-permute-start | bytes 3244040 | tf_op jit(solution)/shard_map/ppermute | solution.py:354
  37.6 2.9 %shard_map.104 = bf16[16,2,8,2048]{3,2,1,0:T(8,128)(2,1)} custom-call(s32[2]{0:T(128)S(1)} %pad_add_fusion.place_ref, bf16[128,4224]{1,0:T(8,128)(2,1)} %collective-permute-done.refs_0_.refs_2_.refs_3_, bf16[128,4224]{1,0:T(8,128)(2,1)S(1)} %copy-done.1, bf16[128,4224]{1,0:T(8,128)(2,1)} %collective-permute-done.refs_0_.refs_2_.refs_3_, ...), custom_call_target="tpu_custom_call" | custom-call | flops 1 | bytes 1 | tf_op jit(solution)/shard_map/pallas_call | solution.py:120
  40.5 7.1 %all-to-all-start.1 = ((bf16[16,2,8,2048]{3,2,1,0:T(8,128)(2,1)}), bf16[16,2,8,2048]{3,2,1,0:T(8,128)(2,1)}, u32[]{:S(2)}, u32[]{:S(2)}) async-start(bf16[16,2,8,2048]{3,2,1,0:T(8,128)(2,1)} %shard_map.104), calls=%async_computation.1 | async-start | bytes 2097152 | tf_op jit(solution)/shard_map/all_to_all | solution.py:377
  47.6 11.6 %collective-permute-done.2.refs_0_.refs_2_.refs_3_.refs_4_.refs_5_ = bf16[128,4224]{1,0:T(8,128)(2,1)S(1)} collective-permute-done((bf16[128,4224]{1,0:T(8,128)(2,1)}, bf16[128,4224]{1,0:T(8,128)(2,1)S(1)}, u32[]{:S(2)}, u32[]{:S(2)}) %collective-permute-start.2) | collective-permute-done | bytes 1081376 | tf_op jit(solution)/shard_map/ppermute | solution.py:354
  59.2 3.0 %shard_map.105 = (bf16[24,1,8,2048]{3,2,1,0:T(8,128)(2,1)}, bf16[24,1,8,2048]{3,2,1,0:T(8,128)(2,1)}) custom-call(s32[2]{0:T(128)S(1)} %pad_add_fusion.place_ref, bf16[128,4224]{1,0:T(8,128)(2,1)S(1)} %collective-permute-done.2.refs_0_.refs_2_.refs_3_.refs_4_.refs_5_, ...), custom_call_target="tpu_custom_call" | custom-call | flops 1 | bytes 1 | tf_op jit(solution)/shard_map/pallas_call | solution.py:120
  62.2 2.9 %collective-permute-start.5 = (bf16[24,1,8,2048]{3,2,1,0:T(8,128)(2,1)}, bf16[24,1,8,2048]{3,2,1,0:T(8,128)(2,1)}, u32[]{:S(2)}, u32[]{:S(2)}) collective-permute-start(bf16[24,1,8,2048]{3,2,1,0:T(8,128)(2,1)} %get-tuple-element.27), channel_id=1, source_target_pairs={{0,14},{2,0},{4,2},{6,4},{8,6},{10,8},{12,10},{14,12},{16,30},{18,... | collective-permute-start | bytes 2359304 | tf_op jit(solution)/shard_map/ppermute | solution.py:354
  65.1 2.7 %shard_map.106 = bf16[16,2,8,2048]{3,2,1,0:T(8,128)(2,1)} custom-call(s32[2]{0:T(128)S(1)} %pad_add_fusion.place_ref, bf16[24,1,8,2048]{3,2,1,0:T(8,128)(2,1)} %get-tuple-element.26.refs_0_, bf16[16,2,8,2048]{3,2,1,0:T(8,128)(2,1)} %all-to-all-done.1.refs_1_, bf16[128,4224]{1,0:T(8,128)(2,1)S(1)} %collective-permute-done.2.refs_0_.refs_2_.refs_3_.refs_4_.refs_5_, ...), custom_call_target="tpu_custom_call" | custom-call | flops 1 | bytes 1 | tf_op jit(solution)/shard_map/pallas_call | solution.py:120
  67.8 7.0 %all-to-all-start.2 = ((bf16[16,2,8,2048]{3,2,1,0:T(8,128)(2,1)}), bf16[16,2,8,2048]{3,2,1,0:T(8,128)(2,1)S(1)}, u32[]{:S(2)}, u32[]{:S(2)}) async-start(bf16[16,2,8,2048]{3,2,1,0:T(8,128)(2,1)} %shard_map.106), calls=%async_computation.2 | async-start | bytes 2097152 | tf_op jit(solution)/shard_map/all_to_all | solution.py:377
  74.8 5.4 %collective-permute-done.5.right_ref = bf16[24,1,8,2048]{3,2,1,0:T(8,128)(2,1)} collective-permute-done((bf16[24,1,8,2048]{3,2,1,0:T(8,128)(2,1)}, bf16[24,1,8,2048]{3,2,1,0:T(8,128)(2,1)}, u32[]{:S(2)}, u32[]{:S(2)}) %collective-permute-start.5) | collective-permute-done | bytes 786464 | tf_op jit(solution)/shard_map/ppermute | solution.py:354
  81.2 2.8 %collective-permute-start.7 = (bf16[8,1,8,2048]{3,2,1,0:T(8,128)(2,1)S(1)}, bf16[8,1,8,2048]{3,2,1,0:T(8,128)(2,1)S(1)}, u32[]{:S(2)}, u32[]{:S(2)}) collective-permute-start(bf16[8,1,8,2048]{3,2,1,0:T(8,128)(2,1)S(1)} %slice.9), channel_id=1, source_target_pairs={{0,14},{2,0},{4,2},{6,4},{8,6},{10,8},{12,10},{14,12},{16,30},{18,... | collective-permute-start | bytes 786440 | tf_op jit(solution)/shard_map/ppermute | solution.py:354
  85.7 4.4 %all-to-all-done.2.after_ref.refs_2_ = bf16[16,2,8,2048]{3,2,1,0:T(8,128)(2,1)S(1)} async-done(((bf16[16,2,8,2048]{3,2,1,0:T(8,128)(2,1)}), bf16[16,2,8,2048]{3,2,1,0:T(8,128)(2,1)S(1)}, u32[]{:S(2)}, u32[]{:S(2)}) %all-to-all-start.2) | async-done | bytes 1048608 | tf_op jit(solution)/shard_map/all_to_all | solution.py:377
  90.1 2.9 %collective-permute-done.6.far_left_ref = bf16[8,1,8,2048]{3,2,1,0:T(8,128)(2,1)S(1)} collective-permute-done((bf16[8,1,8,2048]{3,2,1,0:T(8,128)(2,1)S(1)}, bf16[8,1,8,2048]{3,2,1,0:T(8,128)(2,1)S(1)}, u32[]{:S(2)}, u32[]{:S(2)}) %collective-permute-start.6) | collective-permute-done | bytes 262176 | tf_op jit(solution)/shard_map/ppermute | solution.py:354
  95.3 6.9 %all-to-all-start.3 = ((bf16[16,3,8,2048]{3,2,1,0:T(8,128)(2,1)}), bf16[16,3,8,2048]{3,2,1,0:T(8,128)(2,1)S(1)}, u32[]{:S(2)}, u32[]{:S(2)}) async-start(bf16[16,3,8,2048]{3,2,1,0:T(8,128)(2,1)} %shard_map.107), calls=%async_computation.3 | async-start | bytes 3145728 | tf_op jit(solution)/shard_map/all_to_all | solution.py:377
  102.2 20.0 %all-to-all-done.3.refs_3_ = bf16[16,3,8,2048]{3,2,1,0:T(8,128)(2,1)S(1)} async-done(((bf16[16,3,8,2048]{3,2,1,0:T(8,128)(2,1)}), bf16[16,3,8,2048]{3,2,1,0:T(8,128)(2,1)S(1)}, u32[]{:S(2)}, u32[]{:S(2)}) %all-to-all-start.3) | async-done | bytes 1572896 | tf_op jit(solution)/shard_map/all_to_all | solution.py:377
  122.3 22.6 %shard_map.108 = (bf16[512,1024]{1,0:T(8,128)(2,1)}, bf16[512,1024]{1,0:T(8,128)(2,1)}, bf16[512,1024]{1,0:T(8,128)(2,1)}, bf16[512,1024]{1,0:T(8,128)(2,1)}, bf...) custom-call(s32[2]{0:T(128)S(1)} %pad_add_fusion.place_ref, ...), custom_call_target="tpu_custom_call" | custom-call | flops 1 | bytes 1 | tf_op jit(solution)/shard_map/pallas_call | solution.py:254
  144.8 9.0 %all-to-all-start.4 = ((bf16[128,8,1024]{2,1,0:T(8,128)(2,1)}), bf16[128,8,1024]{2,1,0:T(8,128)(2,1)S(1)}, u32[]{:S(2)}, u32[]{:S(2)}) async-start(bf16[128,8,1024]{2,1,0:T(8,128)(2,1)} %bitcast.11), calls=%async_computation.4 | async-start | bytes 4194304 | tf_op jit(solution)/shard_map/all_to_all | solution.py:406
  153.9 6.2 %shard_map.110 = (bf16[1024,768]{1,0:T(8,128)(2,1)}, bf16[1024,768]{1,0:T(8,128)(2,1)}, bf16[768,1024]{1,0:T(8,128)(2,1)}) custom-call(bf16[512,1024]{1,0:T(8,128)(2,1)} %get-tuple-element.34.x_ref, bf16[512,1024]{1,0:T(8,128)(2,1)} %get-tuple-element.35.s_ref, bf16[512,768]{1,0:T(8,128)(2,1)} %get-tuple-element.31.gate_ref, ...), custom_call_target="tpu_custom_call" | custom-call | flops 1 | bytes 1 | tf_op jit(solution)/shard_map/pallas_call | solution.py:300
  160.7 3.0 %collective-permute-done.11.refs_0_ = bf16[1024,768]{1,0:T(8,128)(2,1)S(1)} collective-permute-done((bf16[1024,768]{1,0:T(8,128)(2,1)}, bf16[1024,768]{1,0:T(8,128)(2,1)S(1)}, u32[]{:S(2)}, u32[]{:S(2)}) %collective-permute-start.11) | collective-permute-done | bytes 1572896 | tf_op jit(solution)/shard_map/ppermute | solution.py:357
  168.2 6.3 %shard_map.111 = (bf16[1024,768]{1,0:T(8,128)(2,1)}, bf16[1024,768]{1,0:T(8,128)(2,1)}, bf16[768,1024]{1,0:T(8,128)(2,1)}) custom-call(bf16[512,1024]{1,0:T(8,128)(2,1)} %get-tuple-element.29.x_ref, bf16[512,1024]{1,0:T(8,128)(2,1)} %get-tuple-element.30.s_ref, bf16[512,768]{1,0:T(8,128)(2,1)} %get-tuple-element.31.gate_ref, ...), custom_call_target="tpu_custom_call" | custom-call | flops 1 | bytes 1 | tf_op jit(solution)/shard_map/pallas_call | solution.py:300
  174.5 30.8 %all-to-all-done.4 = bf16[128,8,1024]{2,1,0:T(8,128)(2,1)S(1)} async-done(((bf16[128,8,1024]{2,1,0:T(8,128)(2,1)}), bf16[128,8,1024]{2,1,0:T(8,128)(2,1)S(1)}, u32[]{:S(2)}, u32[]{:S(2)}) %all-to-all-start.4) | async-done | bytes 2097184 | tf_op jit(solution)/shard_map/all_to_all | solution.py:406
  (34 shorter events, 19.5 us)
Async XLA Ops:
  3.6 25.9 %collective-permute-start.1 = (bf16[128,4224]{1,0:T(8,128)(2,1)S(1)}, bf16[128,4224]{1,0:T(8,128)(2,1)S(1)}, u32[]{:S(2)}, u32[]{:S(2)}) collective-permute-start(bf16[128,4224]{1,0:T(8,128)(2,1)S(1)} %shard_map.102.refs_0_.refs_1_.refs_2_.meta_ref), channel_id=1, source_target_pairs={{0,14},{2,0},{4,2},{6,4},{8,6},{10,8},{12,10},{14,12},{16,30},{18,... | collective-permute-start | bytes 3244040 | tf_op jit(solution)/shard_map/ppermute | solution.py:354
  5.5 27.8 %collective-permute-start = (bf16[128,4224]{1,0:T(8,128)(2,1)S(1)}, bf16[128,4224]{1,0:T(8,128)(2,1)}, u32[]{:S(2)}, u32[]{:S(2)}) collective-permute-start(bf16[128,4224]{1,0:T(8,128)(2,1)S(1)} %shard_map.102.refs_0_.refs_1_.refs_2_.meta_ref), channel_id=1, source_target_pairs={{0,2},{2,4},{4,6},{6,8},{8,10},{10,12},{12,14},{14,0},{16,18},{18,... | collective-permute-start | bytes 3244040 | tf_op jit(solution)/shard_map/ppermute | solution.py:354
  29.5 1.0 copy-start
  33.3 25.8 %collective-permute-start.2 = (bf16[128,4224]{1,0:T(8,128)(2,1)}, bf16[128,4224]{1,0:T(8,128)(2,1)S(1)}, u32[]{:S(2)}, u32[]{:S(2)}) collective-permute-start(bf16[128,4224]{1,0:T(8,128)(2,1)} %collective-permute-done.refs_0_.refs_2_.refs_3_), channel_id=1, source_target_pairs={{0,2},{2,4},{4,6},{6,8},{8,10},{10,12},{12,14},{14,0},{16,18},{18,... | collective-permute-start | bytes 3244040 | tf_op jit(solution)/shard_map/ppermute | solution.py:354
  33.3 25.8 %collective-permute-start.3 = (bf16[128,4224]{1,0:T(8,128)(2,1)}, bf16[128,4224]{1,0:T(8,128)(2,1)S(1)}, u32[]{:S(2)}, u32[]{:S(2)}) collective-permute-start(bf16[128,4224]{1,0:T(8,128)(2,1)} %copy-done), channel_id=1, source_target_pairs={{0,14},{2,0},{4,2},{6,4},{8,6},{10,8},{12,10},{14,12},{16,30},{18,... | collective-permute-start | bytes 3244040 | tf_op jit(solution)/shard_map/ppermute | solution.py:354
  36.3 1.3 copy-start.1
  40.5 24.6 %all-to-all-start.1 = ((bf16[16,2,8,2048]{3,2,1,0:T(8,128)(2,1)}), bf16[16,2,8,2048]{3,2,1,0:T(8,128)(2,1)}, u32[]{:S(2)}, u32[]{:S(2)}) async-start(bf16[16,2,8,2048]{3,2,1,0:T(8,128)(2,1)} %shard_map.104), calls=%async_computation.1 | async-start | bytes 2097152 | tf_op jit(solution)/shard_map/all_to_all | solution.py:377
  62.2 18.1 %collective-permute-start.5 = (bf16[24,1,8,2048]{3,2,1,0:T(8,128)(2,1)}, bf16[24,1,8,2048]{3,2,1,0:T(8,128)(2,1)}, u32[]{:S(2)}, u32[]{:S(2)}) collective-permute-start(bf16[24,1,8,2048]{3,2,1,0:T(8,128)(2,1)} %get-tuple-element.27), channel_id=1, source_target_pairs={{0,14},{2,0},{4,2},{6,4},{8,6},{10,8},{12,10},{14,12},{16,30},{18,... | collective-permute-start | bytes 2359304 | tf_op jit(solution)/shard_map/ppermute | solution.py:354
  65.1 18.8 %collective-permute-start.4 = (bf16[24,1,8,2048]{3,2,1,0:T(8,128)(2,1)}, bf16[24,1,8,2048]{3,2,1,0:T(8,128)(2,1)}, u32[]{:S(2)}, u32[]{:S(2)}) collective-permute-start(bf16[24,1,8,2048]{3,2,1,0:T(8,128)(2,1)} %get-tuple-element.26.refs_0_), channel_id=1, source_target_pairs={{0,2},{2,4},{4,6},{6,8},{8,10},{10,12},{12,14},{14,0},{16,18},{18,... | collective-permute-start | bytes 2359304 | tf_op jit(solution)/shard_map/ppermute | solution.py:354
  67.8 22.3 %all-to-all-start.2 = ((bf16[16,2,8,2048]{3,2,1,0:T(8,128)(2,1)}), bf16[16,2,8,2048]{3,2,1,0:T(8,128)(2,1)S(1)}, u32[]{:S(2)}, u32[]{:S(2)}) async-start(bf16[16,2,8,2048]{3,2,1,0:T(8,128)(2,1)} %shard_map.106), calls=%async_computation.2 | async-start | bytes 2097152 | tf_op jit(solution)/shard_map/all_to_all | solution.py:377
  81.2 8.9 %collective-permute-start.7 = (bf16[8,1,8,2048]{3,2,1,0:T(8,128)(2,1)S(1)}, bf16[8,1,8,2048]{3,2,1,0:T(8,128)(2,1)S(1)}, u32[]{:S(2)}, u32[]{:S(2)}) collective-permute-start(bf16[8,1,8,2048]{3,2,1,0:T(8,128)(2,1)S(1)} %slice.9), channel_id=1, source_target_pairs={{0,14},{2,0},{4,2},{6,4},{8,6},{10,8},{12,10},{14,12},{16,30},{18,... | collective-permute-start | bytes 786440 | tf_op jit(solution)/shard_map/ppermute | solution.py:354
  84.9 8.1 %collective-permute-start.6 = (bf16[8,1,8,2048]{3,2,1,0:T(8,128)(2,1)S(1)}, bf16[8,1,8,2048]{3,2,1,0:T(8,128)(2,1)S(1)}, u32[]{:S(2)}, u32[]{:S(2)}) collective-permute-start(bf16[8,1,8,2048]{3,2,1,0:T(8,128)(2,1)S(1)} %slice.8), channel_id=1, source_target_pairs={{0,2},{2,4},{4,6},{6,8},{8,10},{10,12},{12,14},{14,0},{16,18},{18,... | collective-permute-start | bytes 786440 | tf_op jit(solution)/shard_map/ppermute | solution.py:354
  85.0 17.2 %collective-permute-start.8 = (bf16[1024,768]{1,0:T(8,128)(2,1)}, bf16[1024,768]{1,0:T(8,128)(2,1)}, u32[]{:S(2)}, u32[]{:S(2)}) collective-permute-start(bf16[1024,768]{1,0:T(8,128)(2,1)} %bitcast.12), channel_id=1, source_target_pairs={{0,1},{1,0},{2,3},{3,2},{4,5},{5,4},{6,7},{7,6},{8,9},{9,8},{10,11... | collective-permute-start | bytes 4718600 | tf_op jit(solution)/shard_map/ppermute | solution.py:357
  85.1 17.1 %collective-permute-start.9 = (bf16[1024,768]{1,0:T(8,128)(2,1)}, bf16[1024,768]{1,0:T(8,128)(2,1)}, u32[]{:S(2)}, u32[]{:S(2)}) collective-permute-start(bf16[1024,768]{1,0:T(8,128)(2,1)} %bitcast.14), channel_id=1, source_target_pairs={{0,1},{1,0},{2,3},{3,2},{4,5},{5,4},{6,7},{7,6},{8,9},{9,8},{10,11... | collective-permute-start | bytes 4718600 | tf_op jit(solution)/shard_map/ppermute | solution.py:357
  85.6 16.6 %collective-permute-start.10 = (bf16[768,1024]{1,0:T(8,128)(2,1)}, bf16[768,1024]{1,0:T(8,128)(2,1)}, u32[]{:S(2)}, u32[]{:S(2)}) collective-permute-start(bf16[768,1024]{1,0:T(8,128)(2,1)} %bitcast.16), channel_id=1, source_target_pairs={{0,1},{1,0},{2,3},{3,2},{4,5},{5,4},{6,7},{7,6},{8,9},{9,8},{10,11... | collective-permute-start | bytes 4718600 | tf_op jit(solution)/shard_map/ppermute | solution.py:357
  90.1 5.1 %copy-start.2 = (bf16[16,2,8,2048]{3,2,1,0:T(8,128)(2,1)}, bf16[16,2,8,2048]{3,2,1,0:T(8,128)(2,1)S(1)}, u32[]{:S(2)}) copy-start(bf16[16,2,8,2048]{3,2,1,0:T(8,128)(2,1)S(1)} %all-to-all-done.2.after_ref.refs_2_) | copy-start | bytes 3145732
  95.3 27.0 %all-to-all-start.3 = ((bf16[16,3,8,2048]{3,2,1,0:T(8,128)(2,1)}), bf16[16,3,8,2048]{3,2,1,0:T(8,128)(2,1)S(1)}, u32[]{:S(2)}, u32[]{:S(2)}) async-start(bf16[16,3,8,2048]{3,2,1,0:T(8,128)(2,1)} %shard_map.107), calls=%async_computation.3 | async-start | bytes 3145728 | tf_op jit(solution)/shard_map/all_to_all | solution.py:377
  144.8 60.5 %all-to-all-start.4 = ((bf16[128,8,1024]{2,1,0:T(8,128)(2,1)}), bf16[128,8,1024]{2,1,0:T(8,128)(2,1)S(1)}, u32[]{:S(2)}, u32[]{:S(2)}) async-start(bf16[128,8,1024]{2,1,0:T(8,128)(2,1)} %bitcast.11), calls=%async_computation.4 | async-start | bytes 4194304 | tf_op jit(solution)/shard_map/all_to_all | solution.py:406
  160.1 3.6 %collective-permute-start.11 = (bf16[1024,768]{1,0:T(8,128)(2,1)}, bf16[1024,768]{1,0:T(8,128)(2,1)S(1)}, u32[]{:S(2)}, u32[]{:S(2)}) collective-permute-start(bf16[1024,768]{1,0:T(8,128)(2,1)} %get-tuple-element.36), channel_id=1, source_target_pairs={{0,1},{1,0},{2,3},{3,2},{4,5},{5,4},{6,7},{7,6},{8,9},{9,8},{10,11... | collective-permute-start | bytes 4718600 | tf_op jit(solution)/shard_map/ppermute | solution.py:357
  160.1 5.9 %collective-permute-start.12 = (bf16[1024,768]{1,0:T(8,128)(2,1)}, bf16[1024,768]{1,0:T(8,128)(2,1)S(1)}, u32[]{:S(2)}, u32[]{:S(2)}) collective-permute-start(bf16[1024,768]{1,0:T(8,128)(2,1)} %get-tuple-element.37), channel_id=1, source_target_pairs={{0,1},{1,0},{2,3},{3,2},{4,5},{5,4},{6,7},{7,6},{8,9},{9,8},{10,11... | collective-permute-start | bytes 4718600 | tf_op jit(solution)/shard_map/ppermute | solution.py:357
  160.6 7.6 %collective-permute-start.13 = (bf16[768,1024]{1,0:T(8,128)(2,1)}, bf16[768,1024]{1,0:T(8,128)(2,1)S(1)}, u32[]{:S(2)}, u32[]{:S(2)}) collective-permute-start(bf16[768,1024]{1,0:T(8,128)(2,1)} %get-tuple-element.38), channel_id=1, source_target_pairs={{0,1},{1,0},{2,3},{3,2},{4,5},{5,4},{6,7},{7,6},{8,9},{9,8},{10,11... | collective-permute-start | bytes 4718600 | tf_op jit(solution)/shard_map/ppermute | solution.py:357

commit v2 on v1

--- a/solution.py
+++ b/solution.py
@@ -10,6 +10,7 @@
 RING = 8
 CAP = 4
 META = 128
+EXPERT_LIMIT = 40 * 1024 * 1024
 HALF = 1024
 COLS = 1024
 HTILE = 256
@@ -161,7 +162,8 @@
     )(*third, *fourth, after)
 
 
-def expert_kernel(chunks, groups, place_ref, *refs):
+def expert_kernel(chunks, groups, has_base, place_ref, *refs):
+    refs = refs[1:] if has_base else refs
     recvs, refs = refs[: len(chunks)], refs[len(chunks) :]
     wg_own, wg_oth, wu_own, wu_oth, wd_own, wd_oth = refs[:6]
     x_own, x_oth, s_own, s_oth, hid_ref, gg_ref, ug_ref, back = refs[6:14]
@@ -244,15 +246,18 @@
             copy.wait()
 
 
-def experts(chunks, groups, place, recvs, weights):
-    slots = groups * RING * CAP
+def experts(chunks, groups, place, base, recvs, weights):
+    planes = sum(len(chunk) for chunk in chunks)
+    slots = groups * planes * CAP
     hidden = weights[0].shape[1]
     wide = pl.BlockSpec((HALF, HTILE), lambda h: (0, h))
     tall = pl.BlockSpec((HTILE, HALF), lambda h: (h, 0))
     rows = pl.BlockSpec((slots, HALF), lambda h: (0, 0))
     tile = pl.BlockSpec((slots, HTILE), lambda h: (0, h))
-    return pl.pallas_call(
-        functools.partial(expert_kernel, chunks, groups),
+    has_base = base is not None
+    bases = far_memory([base]) if has_base else []
+    return pl.pallas_call(
+        functools.partial(expert_kernel, chunks, groups, has_base),
         grid=(hidden // HTILE,),
         out_shape=(
             [pltpu.HBM((slots, HALF), BF)] * 4
@@ -260,6 +265,7 @@
             + [pltpu.HBM((groups, RING, 2 * CAP, HALF), BF)]
         ),
         in_specs=[pl.BlockSpec(memory_space=pltpu.SMEM)]
+        + [pl.BlockSpec(memory_space=pl.ANY) for _ in bases]
         + [
             pl.BlockSpec(r.shape, lambda h: (0, 0, 0, 0), pipeline_mode=pl.Buffered(1))
             for r in recvs
@@ -270,48 +276,55 @@
         scratch_shapes=[
             pltpu.VMEM((slots, HALF), F32),
             pltpu.VMEM((slots, HALF), F32),
-            pltpu.VMEM((groups, RING, 2 * CAP, HALF), BF),
-            pltpu.SemaphoreType.DMA((RING,)),
+            pltpu.VMEM((groups, planes, 2 * CAP, HALF), BF),
+            pltpu.SemaphoreType.DMA((planes,)),
         ],
-        compiler_params=pltpu.CompilerParams(vmem_limit_bytes=48 * 1024 * 1024),
-        cost_estimate=TOKEN_COST,
-    )(place, *far_memory(recvs[:3]), recvs[3], *far_memory(weights))
-
-
-def weight_kernel(has_sum, x_ref, s_ref, gate_ref, up_ref, hid_ref, *refs):
-    outs = refs[-3:]
-    parts = (
-        dot(x_ref[...], gate_ref[...], 0, 0),
-        dot(x_ref[...], up_ref[...], 0, 0),
-        dot(hid_ref[...], s_ref[...], 0, 0),
-    )
-    for index, part in enumerate(parts):
-        part = part.astype(BF)
+        input_output_aliases={1: 7} if has_base else {},
+        compiler_params=pltpu.CompilerParams(vmem_limit_bytes=EXPERT_LIMIT),
+        cost_estimate=TOKEN_COST,
+    )(place, *bases, *(recvs if has_base else far_memory(recvs)), *far_memory(weights))
+
+
+def weight_kernel(parts, has_sum, *refs):
+    xs, ss, gates, ups, hids = (refs[i * parts : (i + 1) * parts] for i in range(5))
+    rest = refs[5 * parts :]
+    outs = rest[-3:]
+
+    def total(left, right):
+        value = dot(left[0][...], right[0][...], 0, 0)
+        for i in range(1, parts):
+            value += dot(left[i][...], right[i][...], 0, 0)
+        return value.astype(BF)
+
+    for index, (left, right) in enumerate(((xs, gates), (xs, ups), (hids, ss))):
+        part = total(left, right)
         if has_sum:
-            part = (part.astype(F32) + refs[index][...].astype(F32)).astype(BF)
+            part = (part.astype(F32) + rest[index][...].astype(F32)).astype(BF)
         outs[index][...] = part
 
 
-def weight_grads(x, s, gate, up, hid, received):
-    slots, hidden = gate.shape
+def weight_grads(xs, ss, gates, ups, hids, received):
+    hidden = gates[0].shape[1]
     wide = pl.BlockSpec((WTILE, hidden), lambda c: (c, 0))
     tall = pl.BlockSpec((hidden, WTILE), lambda c: (0, c))
     part_specs = [wide, wide, tall]
-    return pl.pallas_call(
-        functools.partial(weight_kernel, bool(received)),
+    narrow = [*xs, *ss]
+    whole = [*gates, *ups, *hids]
+    return pl.pallas_call(
+        functools.partial(weight_kernel, len(xs), bool(received)),
         grid=(HALF // WTILE,),
         out_shape=[
             pltpu.HBM((HALF, hidden), BF),
             pltpu.HBM((HALF, hidden), BF),
             pltpu.HBM((hidden, HALF), BF),
         ],
-        in_specs=[pl.BlockSpec((slots, WTILE), lambda c: (0, c))] * 2
-        + [pl.BlockSpec((slots, hidden), lambda c: (0, 0))] * 3
+        in_specs=[pl.BlockSpec((v.shape[0], WTILE), lambda c: (0, c)) for v in narrow]
+        + [pl.BlockSpec(v.shape, lambda c: (0, 0)) for v in whole]
         + (part_specs if received else []),
         out_specs=part_specs,
         compiler_params=pltpu.CompilerParams(vmem_limit_bytes=VMEM_LIMIT),
         cost_estimate=TOKEN_COST,
-    )(*far_memory([x, s, gate, up, hid]), *received)
+    )(*far_memory([*narrow, *whole]), *received)
 
 
 def combine_kernel(meta_ref, back_ref, out_ref):
@@ -400,9 +413,11 @@
     recv_second = exchange(near(CHUNKS[2], far_memory([far[0], recv_next])))
     fourth = (hop(third[0][groups:], 1), hop(third[1][groups:], -1))
     recv_far = exchange(join(third, fourth, groups, recv_second))
-    x_own, x_oth, s_own, s_oth, hid, gate_grad, up_grad, back = experts(
-        CHUNKS, groups, place, (recv_own, recv_next, recv_second, recv_far), weights
-    )
+    *early, back = experts(
+        CHUNKS[:3], groups, place, None, (recv_own, recv_next, recv_second), weights
+    )
+    *late, back = experts(CHUNKS[3:], groups, place, back, (recv_far,), weights)
+    x_own, x_oth, s_own, s_oth, hid, gate_grad, up_grad = zip(early, late)
     returned = lax.all_to_all(
         back.reshape(owners, 2 * CAP, HALF), "expert", split_axis=0, concat_axis=0, tiled=True
     )

time: 208 us -> 198 us (0.952)
  waiting for transfers between devices: 88.6 us -> 69.7 us
  Pallas kernels: 51.6 us -> 60 us
    all_to_all x3, waiting for transfers between devices: 24.4 us -> 8.35 us  [exchange(): lax.all_to_all(sent, 'expert', split_axis=0, concat_axis=0, tiled=True, a...]
    pallas_call x3 -> x4, Pallas kernels: 35.1 us -> 43.5 us  [the longest x2 28.6 us: experts(): pl.pallas_call(functools.partial(expert_kernel, chunks, groups, has_base)...]
    all_to_all x1, waiting for transfers between devices: 30.8 us -> 28 us  [local(): lax.all_to_all(back.reshape(owners, 2 * CAP, HALF), 'expert', split_axis=...]
  transfers between devices with their start and end apart: 18 -> 18, of which waited for: 11 -> 11; matrix products, arithmetic and copies ran while one was open for 1% -> 1% of each run, Pallas kernels for 12% -> 22%
where the time goes in v2:
time: 198 us; the launch traced here: 197 us
  waiting for transfers between devices  69.7 us (35%)
  Pallas kernels  60 us (30%)
  starting transfers between devices  42.7 us (22%)
  blocking collectives  18.4 us (9%)
  local copies, waits for them, and re-layouts  5.76 us (3%)
    pallas_call x2, Pallas kernels, experts(): pl.pallas_call(functools.partial(expert_kernel, chunks, groups, has_base)...  28.6 us
    all_to_all x1, waiting for transfers between devices, local(): lax.all_to_all(back.reshape(owners, 2 * CAP, HALF), 'expert', split_axis=...  28 us
    ppermute x8, waiting for transfers between devices, hop(): return lax.ppermute(value, 'expert', pairs)  25.8 us
    all_to_all x3, starting transfers between devices, exchange(): lax.all_to_all(sent, 'expert', split_axis=0, concat_axis=0, tiled=True, a...  21 us
    all_to_all x1, blocking collectives, exchange(): lax.all_to_all(sent, 'expert', split_axis=0, concat_axis=0, tiled=True, a...  18.4 us
    pallas_call x2, Pallas kernels, weight_grads(): pl.pallas_call(functools.partial(weight_kernel, len(xs), bool(received)),...  14.8 us
    ppermute x8, starting transfers between devices, hop(): return lax.ppermute(value, 'expert', pairs)  10.9 us
    pallas_call x4, Pallas kernels, build(): pl.pallas_call(functools.partial(build_kernel, jobs, sources, len(shapes)...  10.8 us
  transfers between devices with their start and end apart: 18, of which 11 were waited for; matrix products, arithmetic and copies ran while one was open for 1% of the time, Pallas kernels for 22%

profile of v2, /device:TPU:32, one launch (start us, length us, event | category | flops | bytes accessed | tf_op | source)
XLA Modules:
  0.0 197.3 jit_solution(5522355972513334395)
XLA Ops:
  8.0 18.4 %all_to_all.25.refs_0_ = bf16[16,1,8,2048]{3,2,1,0:T(8,128)(2,1)} all-to-all(bf16[16,1,8,2048]{3,2,1,0:T(8,128)(2,1)} %shard_map.103), channel_id=1, replica_groups={{0,16,32,48,64,80,96,112,128,144,160,176,192,208,224,240},{2,18,34,50,6..., dimensions={0} | all-to-all | bytes 1048576 | tf_op jit(solution)/shard_map/all_to_all | solution.py:390
  26.4 3.0 %collective-permute-done.1.refs_1_.refs_4_.refs_5_ = bf16[128,4224]{1,0:T(8,128)(2,1)S(1)} collective-permute-done((bf16[128,4224]{1,0:T(8,128)(2,1)S(1)}, bf16[128,4224]{1,0:T(8,128)(2,1)S(1)}, u32[]{:S(2)}, u32[]{:S(2)}) %collective-permute-start.1) | collective-permute-done | bytes 1081376 | tf_op jit(solution)/shard_map/ppermute | solution.py:367
  30.4 2.9 %collective-permute-done.refs_0_.refs_2_.refs_3_ = bf16[128,4224]{1,0:T(8,128)(2,1)} collective-permute-done((bf16[128,4224]{1,0:T(8,128)(2,1)S(1)}, bf16[128,4224]{1,0:T(8,128)(2,1)}, u32[]{:S(2)}, u32[]{:S(2)}) %collective-permute-start) | collective-permute-done | bytes 1081376 | tf_op jit(solution)/shard_map/ppermute | solution.py:367
  33.3 3.0 %collective-permute-start.3 = (bf16[128,4224]{1,0:T(8,128)(2,1)}, bf16[128,4224]{1,0:T(8,128)(2,1)S(1)}, u32[]{:S(2)}, u32[]{:S(2)}) collective-permute-start(bf16[128,4224]{1,0:T(8,128)(2,1)} %copy-done), channel_id=1, source_target_pairs={{0,14},{2,0},{4,2},{6,4},{8,6},{10,8},{12,10},{14,12},{16,30},{18,... | collective-permute-start | bytes 3244040 | tf_op jit(solution)/shard_map/ppermute | solution.py:367
  37.6 2.9 %shard_map.104 = bf16[16,2,8,2048]{3,2,1,0:T(8,128)(2,1)} custom-call(s32[2]{0:T(128)S(1)} %pad_add_fusion.place_ref, bf16[128,4224]{1,0:T(8,128)(2,1)} %collective-permute-done.refs_0_.refs_2_.refs_3_, bf16[128,4224]{1,0:T(8,128)(2,1)S(1)} %copy-done.1, bf16[128,4224]{1,0:T(8,128)(2,1)} %collective-permute-done.refs_0_.refs_2_.refs_3_, ...), custom_call_target="tpu_custom_call" | custom-call | flops 1 | bytes 1 | tf_op jit(solution)/shard_map/pallas_call | solution.py:121
  40.5 7.1 %all-to-all-start.1 = ((bf16[16,2,8,2048]{3,2,1,0:T(8,128)(2,1)}), bf16[16,2,8,2048]{3,2,1,0:T(8,128)(2,1)}, u32[]{:S(2)}, u32[]{:S(2)}) async-start(bf16[16,2,8,2048]{3,2,1,0:T(8,128)(2,1)} %shard_map.104), calls=%async_computation.1 | async-start | bytes 2097152 | tf_op jit(solution)/shard_map/all_to_all | solution.py:390
  47.6 11.6 %collective-permute-done.2.refs_0_.refs_2_.refs_3_.refs_4_.refs_5_ = bf16[128,4224]{1,0:T(8,128)(2,1)S(1)} collective-permute-done((bf16[128,4224]{1,0:T(8,128)(2,1)}, bf16[128,4224]{1,0:T(8,128)(2,1)S(1)}, u32[]{:S(2)}, u32[]{:S(2)}) %collective-permute-start.2) | collective-permute-done | bytes 1081376 | tf_op jit(solution)/shard_map/ppermute | solution.py:367
  59.2 3.0 %shard_map.105 = (bf16[24,1,8,2048]{3,2,1,0:T(8,128)(2,1)}, bf16[24,1,8,2048]{3,2,1,0:T(8,128)(2,1)}) custom-call(s32[2]{0:T(128)S(1)} %pad_add_fusion.place_ref, bf16[128,4224]{1,0:T(8,128)(2,1)S(1)} %collective-permute-done.2.refs_0_.refs_2_.refs_3_.refs_4_.refs_5_, ...), custom_call_target="tpu_custom_call" | custom-call | flops 1 | bytes 1 | tf_op jit(solution)/shard_map/pallas_call | solution.py:121
  62.1 2.9 %collective-permute-start.8 = (bf16[24,1,8,2048]{3,2,1,0:T(8,128)(2,1)}, bf16[24,1,8,2048]{3,2,1,0:T(8,128)(2,1)}, u32[]{:S(2)}, u32[]{:S(2)}) collective-permute-start(bf16[24,1,8,2048]{3,2,1,0:T(8,128)(2,1)} %get-tuple-element.36), channel_id=1, source_target_pairs={{0,14},{2,0},{4,2},{6,4},{8,6},{10,8},{12,10},{14,12},{16,30},{18,... | collective-permute-start | bytes 2359304 | tf_op jit(solution)/shard_map/ppermute | solution.py:367
  65.1 2.7 %shard_map.106 = bf16[16,2,8,2048]{3,2,1,0:T(8,128)(2,1)} custom-call(s32[2]{0:T(128)S(1)} %pad_add_fusion.place_ref, bf16[24,1,8,2048]{3,2,1,0:T(8,128)(2,1)} %get-tuple-element.34.refs_0_, bf16[16,2,8,2048]{3,2,1,0:T(8,128)(2,1)} %all-to-all-done.1.refs_1_, bf16[128,4224]{1,0:T(8,128)(2,1)S(1)} %collective-permute-done.2.refs_0_.refs_2_.refs_3_.refs_4_.refs_5_, ...), custom_call_target="tpu_custom_call" | custom-call | flops 1 | bytes 1 | tf_op jit(solution)/shard_map/pallas_call | solution.py:121
  67.7 7.0 %all-to-all-start.2 = ((bf16[16,2,8,2048]{3,2,1,0:T(8,128)(2,1)}), bf16[16,2,8,2048]{3,2,1,0:T(8,128)(2,1)S(1)}, u32[]{:S(2)}, u32[]{:S(2)}) async-start(bf16[16,2,8,2048]{3,2,1,0:T(8,128)(2,1)} %shard_map.106), calls=%async_computation.2 | async-start | bytes 2097152 | tf_op jit(solution)/shard_map/all_to_all | solution.py:390
  74.8 5.4 %collective-permute-done.8.right_ref = bf16[24,1,8,2048]{3,2,1,0:T(8,128)(2,1)} collective-permute-done((bf16[24,1,8,2048]{3,2,1,0:T(8,128)(2,1)}, bf16[24,1,8,2048]{3,2,1,0:T(8,128)(2,1)}, u32[]{:S(2)}, u32[]{:S(2)}) %collective-permute-start.8) | collective-permute-done | bytes 786464 | tf_op jit(solution)/shard_map/ppermute | solution.py:367
  81.2 2.8 %collective-permute-start.10 = (bf16[8,1,8,2048]{3,2,1,0:T(8,128)(2,1)S(1)}, bf16[8,1,8,2048]{3,2,1,0:T(8,128)(2,1)S(1)}, u32[]{:S(2)}, u32[]{:S(2)}) collective-permute-start(bf16[8,1,8,2048]{3,2,1,0:T(8,128)(2,1)S(1)} %slice.9), channel_id=1, source_target_pairs={{0,14},{2,0},{4,2},{6,4},{8,6},{10,8},{12,10},{14,12},{16,30},{18,... | collective-permute-start | bytes 786440 | tf_op jit(solution)/shard_map/ppermute | solution.py:367
  85.7 4.4 %all-to-all-done.2.refs_2_.after_ref = bf16[16,2,8,2048]{3,2,1,0:T(8,128)(2,1)S(1)} async-done(((bf16[16,2,8,2048]{3,2,1,0:T(8,128)(2,1)}), bf16[16,2,8,2048]{3,2,1,0:T(8,128)(2,1)S(1)}, u32[]{:S(2)}, u32[]{:S(2)}) %all-to-all-start.2) | async-done | bytes 1048608 | tf_op jit(solution)/shard_map/all_to_all | solution.py:390
  90.1 2.9 %collective-permute-done.9.far_left_ref = bf16[8,1,8,2048]{3,2,1,0:T(8,128)(2,1)S(1)} collective-permute-done((bf16[8,1,8,2048]{3,2,1,0:T(8,128)(2,1)S(1)}, bf16[8,1,8,2048]{3,2,1,0:T(8,128)(2,1)S(1)}, u32[]{:S(2)}, u32[]{:S(2)}) %collective-permute-start.9) | collective-permute-done | bytes 262176 | tf_op jit(solution)/shard_map/ppermute | solution.py:367
  95.2 6.9 %all-to-all-start.3 = ((bf16[16,3,8,2048]{3,2,1,0:T(8,128)(2,1)}), bf16[16,3,8,2048]{3,2,1,0:T(8,128)(2,1)S(1)}, u32[]{:S(2)}, u32[]{:S(2)}) async-start(bf16[16,3,8,2048]{3,2,1,0:T(8,128)(2,1)} %shard_map.108), calls=%async_computation.3 | async-start | bytes 3145728 | tf_op jit(solution)/shard_map/all_to_all | solution.py:390
  102.2 16.1 %shard_map.107 = (bf16[320,1024]{1,0:T(8,128)(2,1)}, bf16[320,1024]{1,0:T(8,128)(2,1)}, bf16[320,1024]{1,0:T(8,128)(2,1)}, bf16[320,1024]{1,0:T(8,128)(2,1)}, bf...) custom-call(s32[2]{0:T(128)S(1)} %pad_add_fusion.place_ref, ...), custom_call_target="tpu_custom_call" | custom-call | flops 1 | bytes 1 | tf_op jit(solution)/shard_map/pallas_call | solution.py:259
  118.3 3.9 %all-to-all-done.3.refs_1_ = bf16[16,3,8,2048]{3,2,1,0:T(8,128)(2,1)S(1)} async-done(((bf16[16,3,8,2048]{3,2,1,0:T(8,128)(2,1)}), bf16[16,3,8,2048]{3,2,1,0:T(8,128)(2,1)S(1)}, u32[]{:S(2)}, u32[]{:S(2)}) %all-to-all-start.3) | async-done | bytes 1572896 | tf_op jit(solution)/shard_map/all_to_all | solution.py:390
  122.2 12.5 %shard_map.109 = (bf16[192,1024]{1,0:T(8,128)(2,1)}, bf16[192,1024]{1,0:T(8,128)(2,1)}, bf16[192,1024]{1,0:T(8,128)(2,1)}, bf16[192,1024]{1,0:T(8,128)(2,1)}, bf...) custom-call(s32[2]{0:T(128)S(1)} %pad_add_fusion.place_ref, ...), custom_call_target="tpu_custom_call", output_to_operand_aliasing={{7}: (1, {})} | custom-call | flops 1 | bytes 1 | tf_op jit(solution)/shard_map/pallas_call | solution.py:259
  134.8 9.5 %all-to-all-start.4 = ((bf16[128,8,1024]{2,1,0:T(8,128)(2,1)}), bf16[128,8,1024]{2,1,0:T(8,128)(2,1)S(1)}, u32[]{:S(2)}, u32[]{:S(2)}) async-start(bf16[128,8,1024]{2,1,0:T(8,128)(2,1)} %bitcast.11), calls=%async_computation.4 | async-start | bytes 4194304 | tf_op jit(solution)/shard_map/all_to_all | solution.py:421
  144.3 7.4 %shard_map.111 = (bf16[1024,768]{1,0:T(8,128)(2,1)}, bf16[1024,768]{1,0:T(8,128)(2,1)}, bf16[768,1024]{1,0:T(8,128)(2,1)}) custom-call(bf16[320,1024]{1,0:T(8,128)(2,1)} %get-tuple-element.48.refs_0_, bf16[192,1024]{1,0:T(8,128)(2,1)} %get-tuple-element.49.refs_1_, bf16[320,1024]{1,0:T(8,128)(2,1)} %get-tuple-element.50.refs_2_, ...), custom_call_target="tpu_custom_call" | custom-call | flops 1 | bytes 1 | tf_op jit(solution)/shard_map/pallas_call | solution.py:313
  152.3 3.0 %collective-permute-done.11.refs_10_ = bf16[1024,768]{1,0:T(8,128)(2,1)S(1)} collective-permute-done((bf16[1024,768]{1,0:T(8,128)(2,1)}, bf16[1024,768]{1,0:T(8,128)(2,1)S(1)}, u32[]{:S(2)}, u32[]{:S(2)}) %collective-permute-start.11) | collective-permute-done | bytes 1572896 | tf_op jit(solution)/shard_map/ppermute | solution.py:370
  159.8 7.4 %shard_map.112 = (bf16[1024,768]{1,0:T(8,128)(2,1)}, bf16[1024,768]{1,0:T(8,128)(2,1)}, bf16[768,1024]{1,0:T(8,128)(2,1)}) custom-call(bf16[320,1024]{1,0:T(8,128)(2,1)} %get-tuple-element.38.refs_0_, bf16[192,1024]{1,0:T(8,128)(2,1)} %get-tuple-element.39.refs_1_, bf16[320,1024]{1,0:T(8,128)(2,1)} %get-tuple-element.40.refs_2_, ...), custom_call_target="tpu_custom_call" | custom-call | flops 1 | bytes 1 | tf_op jit(solution)/shard_map/pallas_call | solution.py:313
  167.2 28.0 %all-to-all-done.4 = bf16[128,8,1024]{2,1,0:T(8,128)(2,1)S(1)} async-done(((bf16[128,8,1024]{2,1,0:T(8,128)(2,1)}), bf16[128,8,1024]{2,1,0:T(8,128)(2,1)S(1)}, u32[]{:S(2)}, u32[]{:S(2)}) %all-to-all-start.4) | async-done | bytes 2097184 | tf_op jit(solution)/shard_map/all_to_all | solution.py:421
  (35 shorter events, 21.8 us)
Async XLA Ops:
  3.6 25.9 %collective-permute-start.1 = (bf16[128,4224]{1,0:T(8,128)(2,1)S(1)}, bf16[128,4224]{1,0:T(8,128)(2,1)S(1)}, u32[]{:S(2)}, u32[]{:S(2)}) collective-permute-start(bf16[128,4224]{1,0:T(8,128)(2,1)S(1)} %shard_map.102.refs_0_.refs_1_.refs_2_.meta_ref), channel_id=1, source_target_pairs={{0,14},{2,0},{4,2},{6,4},{8,6},{10,8},{12,10},{14,12},{16,30},{18,... | collective-permute-start | bytes 3244040 | tf_op jit(solution)/shard_map/ppermute | solution.py:367
  5.5 27.8 %collective-permute-start = (bf16[128,4224]{1,0:T(8,128)(2,1)S(1)}, bf16[128,4224]{1,0:T(8,128)(2,1)}, u32[]{:S(2)}, u32[]{:S(2)}) collective-permute-start(bf16[128,4224]{1,0:T(8,128)(2,1)S(1)} %shard_map.102.refs_0_.refs_1_.refs_2_.meta_ref), channel_id=1, source_target_pairs={{0,2},{2,4},{4,6},{6,8},{8,10},{10,12},{12,14},{14,0},{16,18},{18,... | collective-permute-start | bytes 3244040 | tf_op jit(solution)/shard_map/ppermute | solution.py:367
  29.5 1.0 copy-start
  33.3 25.8 %collective-permute-start.2 = (bf16[128,4224]{1,0:T(8,128)(2,1)}, bf16[128,4224]{1,0:T(8,128)(2,1)S(1)}, u32[]{:S(2)}, u32[]{:S(2)}) collective-permute-start(bf16[128,4224]{1,0:T(8,128)(2,1)} %collective-permute-done.refs_0_.refs_2_.refs_3_), channel_id=1, source_target_pairs={{0,2},{2,4},{4,6},{6,8},{8,10},{10,12},{12,14},{14,0},{16,18},{18,... | collective-permute-start | bytes 3244040 | tf_op jit(solution)/shard_map/ppermute | solution.py:367
  33.3 25.8 %collective-permute-start.3 = (bf16[128,4224]{1,0:T(8,128)(2,1)}, bf16[128,4224]{1,0:T(8,128)(2,1)S(1)}, u32[]{:S(2)}, u32[]{:S(2)}) collective-permute-start(bf16[128,4224]{1,0:T(8,128)(2,1)} %copy-done), channel_id=1, source_target_pairs={{0,14},{2,0},{4,2},{6,4},{8,6},{10,8},{12,10},{14,12},{16,30},{18,... | collective-permute-start | bytes 3244040 | tf_op jit(solution)/shard_map/ppermute | solution.py:367
  36.3 1.3 copy-start.1
  40.5 24.6 %all-to-all-start.1 = ((bf16[16,2,8,2048]{3,2,1,0:T(8,128)(2,1)}), bf16[16,2,8,2048]{3,2,1,0:T(8,128)(2,1)}, u32[]{:S(2)}, u32[]{:S(2)}) async-start(bf16[16,2,8,2048]{3,2,1,0:T(8,128)(2,1)} %shard_map.104), calls=%async_computation.1 | async-start | bytes 2097152 | tf_op jit(solution)/shard_map/all_to_all | solution.py:390
  62.1 18.1 %collective-permute-start.8 = (bf16[24,1,8,2048]{3,2,1,0:T(8,128)(2,1)}, bf16[24,1,8,2048]{3,2,1,0:T(8,128)(2,1)}, u32[]{:S(2)}, u32[]{:S(2)}) collective-permute-start(bf16[24,1,8,2048]{3,2,1,0:T(8,128)(2,1)} %get-tuple-element.36), channel_id=1, source_target_pairs={{0,14},{2,0},{4,2},{6,4},{8,6},{10,8},{12,10},{14,12},{16,30},{18,... | collective-permute-start | bytes 2359304 | tf_op jit(solution)/shard_map/ppermute | solution.py:367
  65.1 18.8 %collective-permute-start.7 = (bf16[24,1,8,2048]{3,2,1,0:T(8,128)(2,1)}, bf16[24,1,8,2048]{3,2,1,0:T(8,128)(2,1)}, u32[]{:S(2)}, u32[]{:S(2)}) collective-permute-start(bf16[24,1,8,2048]{3,2,1,0:T(8,128)(2,1)} %get-tuple-element.34.refs_0_), channel_id=1, source_target_pairs={{0,2},{2,4},{4,6},{6,8},{8,10},{10,12},{12,14},{14,0},{16,18},{18,... | collective-permute-start | bytes 2359304 | tf_op jit(solution)/shard_map/ppermute | solution.py:367
  67.7 22.3 %all-to-all-start.2 = ((bf16[16,2,8,2048]{3,2,1,0:T(8,128)(2,1)}), bf16[16,2,8,2048]{3,2,1,0:T(8,128)(2,1)S(1)}, u32[]{:S(2)}, u32[]{:S(2)}) async-start(bf16[16,2,8,2048]{3,2,1,0:T(8,128)(2,1)} %shard_map.106), calls=%async_computation.2 | async-start | bytes 2097152 | tf_op jit(solution)/shard_map/all_to_all | solution.py:390
  81.2 8.9 %collective-permute-start.10 = (bf16[8,1,8,2048]{3,2,1,0:T(8,128)(2,1)S(1)}, bf16[8,1,8,2048]{3,2,1,0:T(8,128)(2,1)S(1)}, u32[]{:S(2)}, u32[]{:S(2)}) collective-permute-start(bf16[8,1,8,2048]{3,2,1,0:T(8,128)(2,1)S(1)} %slice.9), channel_id=1, source_target_pairs={{0,14},{2,0},{4,2},{6,4},{8,6},{10,8},{12,10},{14,12},{16,30},{18,... | collective-permute-start | bytes 786440 | tf_op jit(solution)/shard_map/ppermute | solution.py:367
  84.9 8.1 %collective-permute-start.9 = (bf16[8,1,8,2048]{3,2,1,0:T(8,128)(2,1)S(1)}, bf16[8,1,8,2048]{3,2,1,0:T(8,128)(2,1)S(1)}, u32[]{:S(2)}, u32[]{:S(2)}) collective-permute-start(bf16[8,1,8,2048]{3,2,1,0:T(8,128)(2,1)S(1)} %slice.8), channel_id=1, source_target_pairs={{0,2},{2,4},{4,6},{6,8},{8,10},{10,12},{12,14},{14,0},{16,18},{18,... | collective-permute-start | bytes 786440 | tf_op jit(solution)/shard_map/ppermute | solution.py:367
  85.0 17.2 %collective-permute-start.4 = (bf16[1024,768]{1,0:T(8,128)(2,1)}, bf16[1024,768]{1,0:T(8,128)(2,1)}, u32[]{:S(2)}, u32[]{:S(2)}) collective-permute-start(bf16[1024,768]{1,0:T(8,128)(2,1)} %bitcast.12), channel_id=1, source_target_pairs={{0,1},{1,0},{2,3},{3,2},{4,5},{5,4},{6,7},{7,6},{8,9},{9,8},{10,11... | collective-permute-start | bytes 4718600 | tf_op jit(solution)/shard_map/ppermute | solution.py:370
  85.1 17.1 %collective-permute-start.5 = (bf16[1024,768]{1,0:T(8,128)(2,1)}, bf16[1024,768]{1,0:T(8,128)(2,1)}, u32[]{:S(2)}, u32[]{:S(2)}) collective-permute-start(bf16[1024,768]{1,0:T(8,128)(2,1)} %bitcast.15), channel_id=1, source_target_pairs={{0,1},{1,0},{2,3},{3,2},{4,5},{5,4},{6,7},{7,6},{8,9},{9,8},{10,11... | collective-permute-start | bytes 4718600 | tf_op jit(solution)/shard_map/ppermute | solution.py:370
  85.6 16.6 %collective-permute-start.6 = (bf16[768,1024]{1,0:T(8,128)(2,1)}, bf16[768,1024]{1,0:T(8,128)(2,1)}, u32[]{:S(2)}, u32[]{:S(2)}) collective-permute-start(bf16[768,1024]{1,0:T(8,128)(2,1)} %bitcast.18), channel_id=1, source_target_pairs={{0,1},{1,0},{2,3},{3,2},{4,5},{5,4},{6,7},{7,6},{8,9},{9,8},{10,11... | collective-permute-start | bytes 4718600 | tf_op jit(solution)/shard_map/ppermute | solution.py:370
  90.1 5.1 %copy-start.2 = (bf16[16,2,8,2048]{3,2,1,0:T(8,128)(2,1)}, bf16[16,2,8,2048]{3,2,1,0:T(8,128)(2,1)S(1)}, u32[]{:S(2)}) copy-start(bf16[16,2,8,2048]{3,2,1,0:T(8,128)(2,1)S(1)} %all-to-all-done.2.refs_2_.after_ref) | copy-start | bytes 3145732
  95.2 27.0 %all-to-all-start.3 = ((bf16[16,3,8,2048]{3,2,1,0:T(8,128)(2,1)}), bf16[16,3,8,2048]{3,2,1,0:T(8,128)(2,1)S(1)}, u32[]{:S(2)}, u32[]{:S(2)}) async-start(bf16[16,3,8,2048]{3,2,1,0:T(8,128)(2,1)} %shard_map.108), calls=%async_computation.3 | async-start | bytes 3145728 | tf_op jit(solution)/shard_map/all_to_all | solution.py:390
  134.8 60.4 %all-to-all-start.4 = ((bf16[128,8,1024]{2,1,0:T(8,128)(2,1)}), bf16[128,8,1024]{2,1,0:T(8,128)(2,1)S(1)}, u32[]{:S(2)}, u32[]{:S(2)}) async-start(bf16[128,8,1024]{2,1,0:T(8,128)(2,1)} %bitcast.11), calls=%async_computation.4 | async-start | bytes 4194304 | tf_op jit(solution)/shard_map/all_to_all | solution.py:421
  151.7 3.6 %collective-permute-start.11 = (bf16[1024,768]{1,0:T(8,128)(2,1)}, bf16[1024,768]{1,0:T(8,128)(2,1)S(1)}, u32[]{:S(2)}, u32[]{:S(2)}) collective-permute-start(bf16[1024,768]{1,0:T(8,128)(2,1)} %get-tuple-element.52), channel_id=1, source_target_pairs={{0,1},{1,0},{2,3},{3,2},{4,5},{5,4},{6,7},{7,6},{8,9},{9,8},{10,11... | collective-permute-start | bytes 4718600 | tf_op jit(solution)/shard_map/ppermute | solution.py:370
  151.7 5.9 %collective-permute-start.12 = (bf16[1024,768]{1,0:T(8,128)(2,1)}, bf16[1024,768]{1,0:T(8,128)(2,1)S(1)}, u32[]{:S(2)}, u32[]{:S(2)}) collective-permute-start(bf16[1024,768]{1,0:T(8,128)(2,1)} %get-tuple-element.53), channel_id=1, source_target_pairs={{0,1},{1,0},{2,3},{3,2},{4,5},{5,4},{6,7},{7,6},{8,9},{9,8},{10,11... | collective-permute-start | bytes 4718600 | tf_op jit(solution)/shard_map/ppermute | solution.py:370
  152.2 7.6 %collective-permute-start.13 = (bf16[768,1024]{1,0:T(8,128)(2,1)}, bf16[768,1024]{1,0:T(8,128)(2,1)S(1)}, u32[]{:S(2)}, u32[]{:S(2)}) collective-permute-start(bf16[768,1024]{1,0:T(8,128)(2,1)} %get-tuple-element.54), channel_id=1, source_target_pairs={{0,1},{1,0},{2,3},{3,2},{4,5},{5,4},{6,7},{7,6},{8,9},{9,8},{10,11... | collective-permute-start | bytes 4718600 | tf_op jit(solution)/shard_map/ppermute | solution.py:370

commit v3 on v2

--- a/solution.py
+++ b/solution.py
@@ -13,7 +13,6 @@
 EXPERT_LIMIT = 40 * 1024 * 1024
 HALF = 1024
 COLS = 1024
-HTILE = 256
 WTILE = 256
 CHUNKS = ((0,), (1, -1), (2, -2), (3, -3, 4))
 BF = jnp.bfloat16
@@ -165,124 +164,119 @@
 def expert_kernel(chunks, groups, has_base, place_ref, *refs):
     refs = refs[1:] if has_base else refs
     recvs, refs = refs[: len(chunks)], refs[len(chunks) :]
-    wg_own, wg_oth, wu_own, wu_oth, wd_own, wd_oth = refs[:6]
-    x_own, x_oth, s_own, s_oth, hid_ref, gg_ref, ug_ref, back = refs[6:14]
-    acc_own, acc_oth, stage, sems = refs[14:]
-    step = pl.program_id(0)
+    sources, results, back = refs[:6], refs[6:13], refs[13]
+    held, refs = refs[14:20], refs[20:]
+    x_own, x_oth, s_own, s_oth, hid_ref, gg_ref, ug_ref = refs[:7]
+    stage, load_sems, store_sems, back_sems = refs[7:]
+    wg_own, wg_oth, wu_own, wu_oth, wd_own, wd_oth = held
     place = place_ref[0]
     rep = place_ref[1]
-
-    @pl.when(step == 0)
-    def _():
-        start = 0
-        for recv, planes in zip(recvs, chunks):
-            slots = groups * len(planes) * CAP
-            row = lax.broadcasted_iota(jnp.int32, (slots, 2 * slots), 0)
-            col = lax.broadcasted_iota(jnp.int32, (slots, 2 * slots), 1)
-            source = (row >> 2) * 8 + (row & 3)
-            take_x = (col == source).astype(F32).astype(BF)
-            take_s = (col == source + 4).astype(F32).astype(BF)
-            for half, x_ref, s_ref in ((rep, x_own, s_own), (1 - rep, x_oth, s_oth)):
-                at = pl.ds(pl.multiple_of(half * HALF, HALF), HALF)
-                rows = recv[:, :, :, at].reshape(2 * slots, HALF)
-                x_ref[start : start + slots] = dot(take_x, rows, 1, 0).astype(BF)
-                s_ref[start : start + slots] = dot(take_s, rows, 1, 0).astype(BF)
-            start += slots
-
+    loads = [
+        pltpu.make_async_copy(sources[i], held[i], load_sems.at[i]) for i in range(len(held))
+    ]
+    stores = [
+        pltpu.make_async_copy(refs[i], results[i], store_sems.at[i]) for i in range(len(results))
+    ]
+    for load in loads:
+        load.start()
+    start = 0
+    for recv, planes in zip(recvs, chunks):
+        slots = groups * len(planes) * CAP
+        row = lax.broadcasted_iota(jnp.int32, (2 * slots, 2 * slots), 0)
+        col = lax.broadcasted_iota(jnp.int32, (2 * slots, 2 * slots), 1)
+        grad = (row >= slots).astype(jnp.int32)
+        inner = row - slots * grad
+        take = (col == (inner >> 2) * 8 + (inner & 3) + 4 * grad).astype(F32).astype(BF)
+        for half, x_ref, s_ref in ((rep, x_own, s_own), (1 - rep, x_oth, s_oth)):
+            at = pl.ds(pl.multiple_of(half * HALF, HALF), HALF)
+            both = dot(take, recv[:, :, :, at].reshape(2 * slots, HALF), 1, 0).astype(BF)
+            x_ref[start : start + slots] = both[:slots]
+            s_ref[start : start + slots] = both[slots:]
+        start += slots
+    for store in stores[:4]:
+        store.start()
+    for load in loads[:2]:
+        load.wait()
     gate = dot(x_own[...], wg_own[...], 1, 0) + dot(x_oth[...], wg_oth[...], 1, 0)
+    for load in loads[2:4]:
+        load.wait()
     up = dot(x_own[...], wu_own[...], 1, 0) + dot(x_oth[...], wu_oth[...], 1, 0)
-    hidden_grad = dot(s_own[...], wd_own[...], 1, 1) + dot(s_oth[...], wd_oth[...], 1, 1)
     sigma = jax.nn.sigmoid(gate)
     silu = gate * sigma
     hid_ref[...] = (silu * up).astype(BF)
-    gate_grad = (hidden_grad * up * sigma * (1.0 + gate * (1.0 - sigma))).astype(BF)
-    up_grad = (hidden_grad * silu).astype(BF)
-    gg_ref[...] = gate_grad
-    ug_ref[...] = up_grad
-    new_own = dot(gate_grad, wg_own[...], 1, 1) + dot(up_grad, wu_own[...], 1, 1)
-    new_oth = dot(gate_grad, wg_oth[...], 1, 1) + dot(up_grad, wu_oth[...], 1, 1)
-
-    @pl.when(step == 0)
-    def _():
-        acc_own[...] = new_own
-        acc_oth[...] = new_oth
-
-    @pl.when(step > 0)
-    def _():
-        acc_own[...] += new_own
-        acc_oth[...] += new_oth
-
-    @pl.when(step == pl.num_programs(0) - 1)
-    def _():
-        start = 0
-        first = 0
-        copies = []
-        for planes in chunks:
-            count = len(planes)
-            slots = groups * count * CAP
-            row = lax.broadcasted_iota(jnp.int32, (2 * slots, slots), 0)
-            col = lax.broadcasted_iota(jnp.int32, (2 * slots, slots), 1)
-            same = ((row >> 3) == (col >> 2)) & ((row & 3) == (col & 3))
-            upper = (row >> 2) & 1
-            put_own = (same & (upper == rep)).astype(F32).astype(BF)
-            put_oth = (same & (upper != rep)).astype(F32).astype(BF)
-            mixed = dot(put_own, acc_own[start : start + slots].astype(BF), 1, 0) + dot(
-                put_oth, acc_oth[start : start + slots].astype(BF), 1, 0
+    for load in loads[4:]:
+        load.wait()
+    hidden_grad = dot(s_own[...], wd_own[...], 1, 1) + dot(s_oth[...], wd_oth[...], 1, 1)
+    gg_ref[...] = (hidden_grad * up * sigma * (1.0 + gate * (1.0 - sigma))).astype(BF)
+    ug_ref[...] = (hidden_grad * silu).astype(BF)
+    for store in stores[4:]:
+        store.start()
+    slot_own = dot(gg_ref[...], wg_own[...], 1, 1) + dot(ug_ref[...], wu_own[...], 1, 1)
+    slot_own = slot_own.astype(BF)
+    slot_oth = dot(gg_ref[...], wg_oth[...], 1, 1) + dot(ug_ref[...], wu_oth[...], 1, 1)
+    slot_oth = slot_oth.astype(BF)
+    start = 0
+    first = 0
+    copies = []
+    for planes in chunks:
+        count = len(planes)
+        slots = groups * count * CAP
+        row = lax.broadcasted_iota(jnp.int32, (2 * slots, slots), 0)
+        col = lax.broadcasted_iota(jnp.int32, (2 * slots, slots), 1)
+        same = ((row >> 3) == (col >> 2)) & ((row & 3) == (col & 3))
+        upper = (row >> 2) & 1
+        put_own = (same & (upper == rep)).astype(F32).astype(BF)
+        put_oth = (same & (upper != rep)).astype(F32).astype(BF)
+        mixed = dot(put_own, slot_own[start : start + slots], 1, 0) + dot(
+            put_oth, slot_oth[start : start + slots], 1, 0
+        )
+        stage[:, first : first + count] = mixed.astype(BF).reshape(groups, count, 2 * CAP, HALF)
+        for index, plane in enumerate(planes):
+            copy = pltpu.make_async_copy(
+                stage.at[:, first + index],
+                back.at[:, lax.rem(place - plane + RING, RING)],
+                back_sems.at[first + index],
             )
-            stage[:, first : first + count] = mixed.astype(BF).reshape(
-                groups, count, 2 * CAP, HALF
-            )
-            for index, plane in enumerate(planes):
-                copy = pltpu.make_async_copy(
-                    stage.at[:, first + index],
-                    back.at[:, lax.rem(place - plane + RING, RING)],
-                    sems.at[first + index],
-                )
-                copy.start()
-                copies.append(copy)
-            start += slots
-            first += count
-        for copy in copies:
-            copy.wait()
+            copy.start()
+            copies.append(copy)
+        start += slots
+        first += count
+    for copy in copies + stores:
+        copy.wait()
 
 
 def experts(chunks, groups, place, base, recvs, weights):
     planes = sum(len(chunk) for chunk in chunks)
     slots = groups * planes * CAP
     hidden = weights[0].shape[1]
-    wide = pl.BlockSpec((HALF, HTILE), lambda h: (0, h))
-    tall = pl.BlockSpec((HTILE, HALF), lambda h: (h, 0))
-    rows = pl.BlockSpec((slots, HALF), lambda h: (0, 0))
-    tile = pl.BlockSpec((slots, HTILE), lambda h: (0, h))
     has_base = base is not None
     bases = far_memory([base]) if has_base else []
+    anywhere = pl.BlockSpec(memory_space=pl.ANY)
     return pl.pallas_call(
         functools.partial(expert_kernel, chunks, groups, has_base),
-        grid=(hidden // HTILE,),
         out_shape=(
             [pltpu.HBM((slots, HALF), BF)] * 4
             + [pltpu.HBM((slots, hidden), BF)] * 3
             + [pltpu.HBM((groups, RING, 2 * CAP, HALF), BF)]
         ),
         in_specs=[pl.BlockSpec(memory_space=pltpu.SMEM)]
-        + [pl.BlockSpec(memory_space=pl.ANY) for _ in bases]
+        + [anywhere for _ in bases]
+        + [pl.BlockSpec(memory_space=pltpu.VMEM) for _ in recvs]
+        + [anywhere] * 6,
+        out_specs=[anywhere] * 8,
+        scratch_shapes=[pltpu.VMEM(w.shape, BF) for w in weights]
+        + [pltpu.VMEM((slots, HALF), BF)] * 4
+        + [pltpu.VMEM((slots, hidden), BF)] * 3
         + [
-            pl.BlockSpec(r.shape, lambda h: (0, 0, 0, 0), pipeline_mode=pl.Buffered(1))
-            for r in recvs
-        ]
-        + [wide] * 4
-        + [tall] * 2,
-        out_specs=[rows] * 4 + [tile] * 3 + [pl.BlockSpec(memory_space=pl.ANY)],
-        scratch_shapes=[
-            pltpu.VMEM((slots, HALF), F32),
-            pltpu.VMEM((slots, HALF), F32),
             pltpu.VMEM((groups, planes, 2 * CAP, HALF), BF),
+            pltpu.SemaphoreType.DMA((6,)),
+            pltpu.SemaphoreType.DMA((7,)),
             pltpu.SemaphoreType.DMA((planes,)),
         ],
         input_output_aliases={1: 7} if has_base else {},
         compiler_params=pltpu.CompilerParams(vmem_limit_bytes=EXPERT_LIMIT),
         cost_estimate=TOKEN_COST,
-    )(place, *bases, *(recvs if has_base else far_memory(recvs)), *far_memory(weights))
+    )(place, *bases, *recvs, *far_memory(weights))
 
 
 def weight_kernel(parts, has_sum, *refs):
@@ -380,7 +374,7 @@
         (sent,) = build(
             jobs,
             place,
-            [data[p] for p in planes],
+            far_memory([data[p] for p in planes]) if planes == CHUNKS[1] else [data[p] for p in planes],
             [(groups, len(planes))],
             after,
         )

time: 198 us -> 196 us (0.990)
  Pallas kernels: 60 us -> 55.1 us
  waiting for transfers between devices: 69.7 us -> 73.8 us
    pallas_call x2, Pallas kernels: 28.6 us -> 23.5 us  [experts(): pl.pallas_call(functools.partial(expert_kernel, chunks, groups, has_base)...]
    all_to_all x3, waiting for transfers between devices: 8.35 us -> 11.7 us  [exchange(): lax.all_to_all(sent, 'expert', split_axis=0, concat_axis=0, tiled=True, a...]
  transfers between devices with their start and end apart: 18 -> 18, of which waited for: 11 -> 11; matrix products, arithmetic and copies ran while one was open for 1% -> 1% of each run, Pallas kernels for 22% -> 21%
where the time goes in v3:
time: 196 us; the launch traced here: 195 us
  waiting for transfers between devices  73.8 us (38%)
  Pallas kernels  55.1 us (28%)
  starting transfers between devices  42.6 us (22%)
  blocking collectives  18.4 us (9%)
  local copies, waits for them, and re-layouts  4.49 us (2%)
    all_to_all x1, waiting for transfers between devices, local(): lax.all_to_all(back.reshape(owners, 2 * CAP, HALF), 'expert', split_axis=...  27.5 us
    ppermute x8, waiting for transfers between devices, hop(): return lax.ppermute(value, 'expert', pairs)  27 us
    pallas_call x2, Pallas kernels, experts(): pl.pallas_call(functools.partial(expert_kernel, chunks, groups, has_base)...  23.5 us
    all_to_all x3, starting transfers between devices, exchange(): lax.all_to_all(sent, 'expert', split_axis=0, concat_axis=0, tiled=True, a...  21.2 us
    all_to_all x1, blocking collectives, exchange(): lax.all_to_all(sent, 'expert', split_axis=0, concat_axis=0, tiled=True, a...  18.4 us
    pallas_call x2, Pallas kernels, weight_grads(): pl.pallas_call(functools.partial(weight_kernel, len(xs), bool(received)),...  14.8 us
    all_to_all x3, waiting for transfers between devices, exchange(): lax.all_to_all(sent, 'expert', split_axis=0, concat_axis=0, tiled=True, a...  11.7 us
    pallas_call x4, Pallas kernels, build(): pl.pallas_call(functools.partial(build_kernel, jobs, sources, len(shapes)...  11 us
  transfers between devices with their start and end apart: 18, of which 11 were waited for; matrix products, arithmetic and copies ran while one was open for 1% of the time, Pallas kernels for 21%

profile of v3, /device:TPU:32, one launch (start us, length us, event | category | flops | bytes accessed | tf_op | source)
XLA Modules:
  0.0 195.2 jit_solution(16427384649038366024)
XLA Ops:
  8.0 18.4 %all_to_all.25.refs_0_ = bf16[16,1,8,2048]{3,2,1,0:T(8,128)(2,1)} all-to-all(bf16[16,1,8,2048]{3,2,1,0:T(8,128)(2,1)} %shard_map.103), channel_id=1, replica_groups={{0,16,32,48,64,80,96,112,128,144,160,176,192,208,224,240},{2,18,34,50,6..., dimensions={0} | all-to-all | bytes 1048576 | tf_op jit(solution)/shard_map/all_to_all | solution.py:384
  26.4 3.0 %collective-permute-done.1.refs_1_.refs_4_.refs_5_ = bf16[128,4224]{1,0:T(8,128)(2,1)S(1)} collective-permute-done((bf16[128,4224]{1,0:T(8,128)(2,1)S(1)}, bf16[128,4224]{1,0:T(8,128)(2,1)S(1)}, u32[]{:S(2)}, u32[]{:S(2)}) %collective-permute-start.1) | collective-permute-done | bytes 1081376 | tf_op jit(solution)/shard_map/ppermute | solution.py:361
  30.4 2.9 %collective-permute-done.refs_0_.refs_2_.refs_3_ = bf16[128,4224]{1,0:T(8,128)(2,1)} collective-permute-done((bf16[128,4224]{1,0:T(8,128)(2,1)S(1)}, bf16[128,4224]{1,0:T(8,128)(2,1)}, u32[]{:S(2)}, u32[]{:S(2)}) %collective-permute-start) | collective-permute-done | bytes 1081376 | tf_op jit(solution)/shard_map/ppermute | solution.py:361
  33.3 3.0 %collective-permute-start.3 = (bf16[128,4224]{1,0:T(8,128)(2,1)}, bf16[128,4224]{1,0:T(8,128)(2,1)S(1)}, u32[]{:S(2)}, u32[]{:S(2)}) collective-permute-start(bf16[128,4224]{1,0:T(8,128)(2,1)} %copy-done.1), channel_id=1, source_target_pairs={{0,14},{2,0},{4,2},{6,4},{8,6},{10,8},{12,10},{14,12},{16,30},{18,... | collective-permute-start | bytes 3244040 | tf_op jit(solution)/shard_map/ppermute | solution.py:361
  36.3 3.1 %shard_map.104 = bf16[16,2,8,2048]{3,2,1,0:T(8,128)(2,1)} custom-call(s32[2]{0:T(128)S(1)} %pad_add_fusion.place_ref, bf16[128,4224]{1,0:T(8,128)(2,1)} %collective-permute-done.refs_0_.refs_2_.refs_3_, bf16[128,4224]{1,0:T(8,128)(2,1)} %copy-done.1, bf16[128,4224]{1,0:T(8,128)(2,1)} %collective-permute-done.refs_0_.refs_2_.refs_3_, ...), custom_call_target="tpu_custom_call" | custom-call | flops 1 | bytes 1 | tf_op jit(solution)/shard_map/pallas_call | solution.py:120
  39.4 7.1 %all-to-all-start.1 = ((bf16[16,2,8,2048]{3,2,1,0:T(8,128)(2,1)}), bf16[16,2,8,2048]{3,2,1,0:T(8,128)(2,1)}, u32[]{:S(2)}, u32[]{:S(2)}) async-start(bf16[16,2,8,2048]{3,2,1,0:T(8,128)(2,1)} %shard_map.104), calls=%async_computation.1 | async-start | bytes 2097152 | tf_op jit(solution)/shard_map/all_to_all | solution.py:384
  46.5 12.7 %collective-permute-done.2.refs_0_.refs_2_.refs_3_.refs_4_.refs_5_ = bf16[128,4224]{1,0:T(8,128)(2,1)S(1)} collective-permute-done((bf16[128,4224]{1,0:T(8,128)(2,1)}, bf16[128,4224]{1,0:T(8,128)(2,1)S(1)}, u32[]{:S(2)}, u32[]{:S(2)}) %collective-permute-start.2) | collective-permute-done | bytes 1081376 | tf_op jit(solution)/shard_map/ppermute | solution.py:361
  59.2 3.0 %shard_map.105 = (bf16[24,1,8,2048]{3,2,1,0:T(8,128)(2,1)}, bf16[24,1,8,2048]{3,2,1,0:T(8,128)(2,1)}) custom-call(s32[2]{0:T(128)S(1)} %pad_add_fusion.place_ref, bf16[128,4224]{1,0:T(8,128)(2,1)S(1)} %collective-permute-done.2.refs_0_.refs_2_.refs_3_.refs_4_.refs_5_, ...), custom_call_target="tpu_custom_call" | custom-call | flops 1 | bytes 1 | tf_op jit(solution)/shard_map/pallas_call | solution.py:120
  62.1 2.9 %collective-permute-start.8 = (bf16[24,1,8,2048]{3,2,1,0:T(8,128)(2,1)}, bf16[24,1,8,2048]{3,2,1,0:T(8,128)(2,1)}, u32[]{:S(2)}, u32[]{:S(2)}) collective-permute-start(bf16[24,1,8,2048]{3,2,1,0:T(8,128)(2,1)} %get-tuple-element.36), channel_id=1, source_target_pairs={{0,14},{2,0},{4,2},{6,4},{8,6},{10,8},{12,10},{14,12},{16,30},{18,... | collective-permute-start | bytes 2359304 | tf_op jit(solution)/shard_map/ppermute | solution.py:361
  65.1 2.7 %shard_map.106 = bf16[16,2,8,2048]{3,2,1,0:T(8,128)(2,1)} custom-call(s32[2]{0:T(128)S(1)} %pad_add_fusion.place_ref, bf16[24,1,8,2048]{3,2,1,0:T(8,128)(2,1)} %get-tuple-element.34.refs_0_, bf16[16,2,8,2048]{3,2,1,0:T(8,128)(2,1)} %all-to-all-done.1.refs_1_, bf16[128,4224]{1,0:T(8,128)(2,1)S(1)} %collective-permute-done.2.refs_0_.refs_2_.refs_3_.refs_4_.refs_5_, ...), custom_call_target="tpu_custom_call" | custom-call | flops 1 | bytes 1 | tf_op jit(solution)/shard_map/pallas_call | solution.py:120
  67.8 7.0 %all-to-all-start.2 = ((bf16[16,2,8,2048]{3,2,1,0:T(8,128)(2,1)}), bf16[16,2,8,2048]{3,2,1,0:T(8,128)(2,1)S(1)}, u32[]{:S(2)}, u32[]{:S(2)}) async-start(bf16[16,2,8,2048]{3,2,1,0:T(8,128)(2,1)} %shard_map.106), calls=%async_computation.2 | async-start | bytes 2097152 | tf_op jit(solution)/shard_map/all_to_all | solution.py:384
  74.8 5.4 %collective-permute-done.8.right_ref = bf16[24,1,8,2048]{3,2,1,0:T(8,128)(2,1)} collective-permute-done((bf16[24,1,8,2048]{3,2,1,0:T(8,128)(2,1)}, bf16[24,1,8,2048]{3,2,1,0:T(8,128)(2,1)}, u32[]{:S(2)}, u32[]{:S(2)}) %collective-permute-start.8) | collective-permute-done | bytes 786464 | tf_op jit(solution)/shard_map/ppermute | solution.py:361
  81.2 2.8 %collective-permute-start.10 = (bf16[8,1,8,2048]{3,2,1,0:T(8,128)(2,1)S(1)}, bf16[8,1,8,2048]{3,2,1,0:T(8,128)(2,1)S(1)}, u32[]{:S(2)}, u32[]{:S(2)}) collective-permute-start(bf16[8,1,8,2048]{3,2,1,0:T(8,128)(2,1)S(1)} %slice.9), channel_id=1, source_target_pairs={{0,14},{2,0},{4,2},{6,4},{8,6},{10,8},{12,10},{14,12},{16,30},{18,... | collective-permute-start | bytes 786440 | tf_op jit(solution)/shard_map/ppermute | solution.py:361
  85.7 4.3 %all-to-all-done.2.refs_2_.after_ref = bf16[16,2,8,2048]{3,2,1,0:T(8,128)(2,1)S(1)} async-done(((bf16[16,2,8,2048]{3,2,1,0:T(8,128)(2,1)}), bf16[16,2,8,2048]{3,2,1,0:T(8,128)(2,1)S(1)}, u32[]{:S(2)}, u32[]{:S(2)}) %all-to-all-start.2) | async-done | bytes 1048608 | tf_op jit(solution)/shard_map/all_to_all | solution.py:384
  90.0 3.0 %collective-permute-done.9.far_left_ref = bf16[8,1,8,2048]{3,2,1,0:T(8,128)(2,1)S(1)} collective-permute-done((bf16[8,1,8,2048]{3,2,1,0:T(8,128)(2,1)S(1)}, bf16[8,1,8,2048]{3,2,1,0:T(8,128)(2,1)S(1)}, u32[]{:S(2)}, u32[]{:S(2)}) %collective-permute-start.9) | collective-permute-done | bytes 262176 | tf_op jit(solution)/shard_map/ppermute | solution.py:361
  95.3 7.1 %all-to-all-start.3 = ((bf16[16,3,8,2048]{3,2,1,0:T(8,128)(2,1)}), bf16[16,3,8,2048]{3,2,1,0:T(8,128)(2,1)}, u32[]{:S(2)}, u32[]{:S(2)}) async-start(bf16[16,3,8,2048]{3,2,1,0:T(8,128)(2,1)} %shard_map.108), calls=%async_computation.3 | async-start | bytes 3145728 | tf_op jit(solution)/shard_map/all_to_all | solution.py:384
  102.4 12.7 %shard_map.107 = (bf16[320,1024]{1,0:T(8,128)(2,1)}, bf16[320,1024]{1,0:T(8,128)(2,1)}, bf16[320,1024]{1,0:T(8,128)(2,1)}, bf16[320,1024]{1,0:T(8,128)(2,1)}, bf...) custom-call(s32[2]{0:T(128)S(1)} %pad_add_fusion.place_ref, ...), custom_call_target="tpu_custom_call" | custom-call | flops 1 | bytes 1 | tf_op jit(solution)/shard_map/pallas_call | solution.py:255
  115.1 7.4 %all-to-all-done.3.refs_1_ = bf16[16,3,8,2048]{3,2,1,0:T(8,128)(2,1)} async-done(((bf16[16,3,8,2048]{3,2,1,0:T(8,128)(2,1)}), bf16[16,3,8,2048]{3,2,1,0:T(8,128)(2,1)}, u32[]{:S(2)}, u32[]{:S(2)}) %all-to-all-start.3) | async-done | bytes 1572896 | tf_op jit(solution)/shard_map/all_to_all | solution.py:384
  122.5 10.9 %shard_map.109 = (bf16[192,1024]{1,0:T(8,128)(2,1)}, bf16[192,1024]{1,0:T(8,128)(2,1)}, bf16[192,1024]{1,0:T(8,128)(2,1)}, bf16[192,1024]{1,0:T(8,128)(2,1)}, bf...) custom-call(s32[2]{0:T(128)S(1)} %pad_add_fusion.place_ref, ...), custom_call_target="tpu_custom_call", output_to_operand_aliasing={{7}: (1, {})} | custom-call | flops 1 | bytes 1 | tf_op jit(solution)/shard_map/pallas_call | solution.py:255
  133.4 9.3 %all-to-all-start.4 = ((bf16[128,8,1024]{2,1,0:T(8,128)(2,1)}), bf16[128,8,1024]{2,1,0:T(8,128)(2,1)S(1)}, u32[]{:S(2)}, u32[]{:S(2)}) async-start(bf16[128,8,1024]{2,1,0:T(8,128)(2,1)} %bitcast.11), calls=%async_computation.4 | async-start | bytes 4194304 | tf_op jit(solution)/shard_map/all_to_all | solution.py:415
  142.6 7.4 %shard_map.111 = (bf16[1024,768]{1,0:T(8,128)(2,1)}, bf16[1024,768]{1,0:T(8,128)(2,1)}, bf16[768,1024]{1,0:T(8,128)(2,1)}) custom-call(bf16[320,1024]{1,0:T(8,128)(2,1)} %get-tuple-element.48.refs_0_, bf16[192,1024]{1,0:T(8,128)(2,1)} %get-tuple-element.49.refs_1_, bf16[320,1024]{1,0:T(8,128)(2,1)} %get-tuple-element.50.refs_2_, ...), custom_call_target="tpu_custom_call" | custom-call | flops 1 | bytes 1 | tf_op jit(solution)/shard_map/pallas_call | solution.py:307
  150.7 3.0 %collective-permute-done.11.refs_10_ = bf16[1024,768]{1,0:T(8,128)(2,1)S(1)} collective-permute-done((bf16[1024,768]{1,0:T(8,128)(2,1)}, bf16[1024,768]{1,0:T(8,128)(2,1)S(1)}, u32[]{:S(2)}, u32[]{:S(2)}) %collective-permute-start.11) | collective-permute-done | bytes 1572896 | tf_op jit(solution)/shard_map/ppermute | solution.py:364
  158.2 7.4 %shard_map.112 = (bf16[1024,768]{1,0:T(8,128)(2,1)}, bf16[1024,768]{1,0:T(8,128)(2,1)}, bf16[768,1024]{1,0:T(8,128)(2,1)}) custom-call(bf16[320,1024]{1,0:T(8,128)(2,1)} %get-tuple-element.38.refs_0_, bf16[192,1024]{1,0:T(8,128)(2,1)} %get-tuple-element.39.refs_1_, bf16[320,1024]{1,0:T(8,128)(2,1)} %get-tuple-element.40.refs_2_, ...), custom_call_target="tpu_custom_call" | custom-call | flops 1 | bytes 1 | tf_op jit(solution)/shard_map/pallas_call | solution.py:307
  165.6 27.5 %all-to-all-done.4 = bf16[128,8,1024]{2,1,0:T(8,128)(2,1)S(1)} async-done(((bf16[128,8,1024]{2,1,0:T(8,128)(2,1)}), bf16[128,8,1024]{2,1,0:T(8,128)(2,1)S(1)}, u32[]{:S(2)}, u32[]{:S(2)}) %all-to-all-start.4) | async-done | bytes 2097184 | tf_op jit(solution)/shard_map/all_to_all | solution.py:415
  (33 shorter events, 20.5 us)
Async XLA Ops:
  3.6 25.9 %collective-permute-start.1 = (bf16[128,4224]{1,0:T(8,128)(2,1)S(1)}, bf16[128,4224]{1,0:T(8,128)(2,1)S(1)}, u32[]{:S(2)}, u32[]{:S(2)}) collective-permute-start(bf16[128,4224]{1,0:T(8,128)(2,1)S(1)} %shard_map.102.refs_0_.refs_1_.refs_2_.meta_ref), channel_id=1, source_target_pairs={{0,14},{2,0},{4,2},{6,4},{8,6},{10,8},{12,10},{14,12},{16,30},{18,... | collective-permute-start | bytes 3244040 | tf_op jit(solution)/shard_map/ppermute | solution.py:361
  5.5 27.8 %collective-permute-start = (bf16[128,4224]{1,0:T(8,128)(2,1)S(1)}, bf16[128,4224]{1,0:T(8,128)(2,1)}, u32[]{:S(2)}, u32[]{:S(2)}) collective-permute-start(bf16[128,4224]{1,0:T(8,128)(2,1)S(1)} %shard_map.102.refs_0_.refs_1_.refs_2_.meta_ref), channel_id=1, source_target_pairs={{0,2},{2,4},{4,6},{6,8},{8,10},{10,12},{12,14},{14,0},{16,18},{18,... | collective-permute-start | bytes 3244040 | tf_op jit(solution)/shard_map/ppermute | solution.py:361
  29.5 1.0 copy-start.1
  33.3 25.8 %collective-permute-start.2 = (bf16[128,4224]{1,0:T(8,128)(2,1)}, bf16[128,4224]{1,0:T(8,128)(2,1)S(1)}, u32[]{:S(2)}, u32[]{:S(2)}) collective-permute-start(bf16[128,4224]{1,0:T(8,128)(2,1)} %collective-permute-done.refs_0_.refs_2_.refs_3_), channel_id=1, source_target_pairs={{0,2},{2,4},{4,6},{6,8},{8,10},{10,12},{12,14},{14,0},{16,18},{18,... | collective-permute-start | bytes 3244040 | tf_op jit(solution)/shard_map/ppermute | solution.py:361
  33.3 25.8 %collective-permute-start.3 = (bf16[128,4224]{1,0:T(8,128)(2,1)}, bf16[128,4224]{1,0:T(8,128)(2,1)S(1)}, u32[]{:S(2)}, u32[]{:S(2)}) collective-permute-start(bf16[128,4224]{1,0:T(8,128)(2,1)} %copy-done.1), channel_id=1, source_target_pairs={{0,14},{2,0},{4,2},{6,4},{8,6},{10,8},{12,10},{14,12},{16,30},{18,... | collective-permute-start | bytes 3244040 | tf_op jit(solution)/shard_map/ppermute | solution.py:361
  39.4 25.7 %all-to-all-start.1 = ((bf16[16,2,8,2048]{3,2,1,0:T(8,128)(2,1)}), bf16[16,2,8,2048]{3,2,1,0:T(8,128)(2,1)}, u32[]{:S(2)}, u32[]{:S(2)}) async-start(bf16[16,2,8,2048]{3,2,1,0:T(8,128)(2,1)} %shard_map.104), calls=%async_computation.1 | async-start | bytes 2097152 | tf_op jit(solution)/shard_map/all_to_all | solution.py:384
  62.1 18.1 %collective-permute-start.8 = (bf16[24,1,8,2048]{3,2,1,0:T(8,128)(2,1)}, bf16[24,1,8,2048]{3,2,1,0:T(8,128)(2,1)}, u32[]{:S(2)}, u32[]{:S(2)}) collective-permute-start(bf16[24,1,8,2048]{3,2,1,0:T(8,128)(2,1)} %get-tuple-element.36), channel_id=1, source_target_pairs={{0,14},{2,0},{4,2},{6,4},{8,6},{10,8},{12,10},{14,12},{16,30},{18,... | collective-permute-start | bytes 2359304 | tf_op jit(solution)/shard_map/ppermute | solution.py:361
  65.1 18.8 %collective-permute-start.7 = (bf16[24,1,8,2048]{3,2,1,0:T(8,128)(2,1)}, bf16[24,1,8,2048]{3,2,1,0:T(8,128)(2,1)}, u32[]{:S(2)}, u32[]{:S(2)}) collective-permute-start(bf16[24,1,8,2048]{3,2,1,0:T(8,128)(2,1)} %get-tuple-element.34.refs_0_), channel_id=1, source_target_pairs={{0,2},{2,4},{4,6},{6,8},{8,10},{10,12},{12,14},{14,0},{16,18},{18,... | collective-permute-start | bytes 2359304 | tf_op jit(solution)/shard_map/ppermute | solution.py:361
  67.8 22.3 %all-to-all-start.2 = ((bf16[16,2,8,2048]{3,2,1,0:T(8,128)(2,1)}), bf16[16,2,8,2048]{3,2,1,0:T(8,128)(2,1)S(1)}, u32[]{:S(2)}, u32[]{:S(2)}) async-start(bf16[16,2,8,2048]{3,2,1,0:T(8,128)(2,1)} %shard_map.106), calls=%async_computation.2 | async-start | bytes 2097152 | tf_op jit(solution)/shard_map/all_to_all | solution.py:384
  81.2 8.9 %collective-permute-start.10 = (bf16[8,1,8,2048]{3,2,1,0:T(8,128)(2,1)S(1)}, bf16[8,1,8,2048]{3,2,1,0:T(8,128)(2,1)S(1)}, u32[]{:S(2)}, u32[]{:S(2)}) collective-permute-start(bf16[8,1,8,2048]{3,2,1,0:T(8,128)(2,1)S(1)} %slice.9), channel_id=1, source_target_pairs={{0,14},{2,0},{4,2},{6,4},{8,6},{10,8},{12,10},{14,12},{16,30},{18,... | collective-permute-start | bytes 786440 | tf_op jit(solution)/shard_map/ppermute | solution.py:361
  84.9 8.1 %collective-permute-start.9 = (bf16[8,1,8,2048]{3,2,1,0:T(8,128)(2,1)S(1)}, bf16[8,1,8,2048]{3,2,1,0:T(8,128)(2,1)S(1)}, u32[]{:S(2)}, u32[]{:S(2)}) collective-permute-start(bf16[8,1,8,2048]{3,2,1,0:T(8,128)(2,1)S(1)} %slice.8), channel_id=1, source_target_pairs={{0,2},{2,4},{4,6},{6,8},{8,10},{10,12},{12,14},{14,0},{16,18},{18,... | collective-permute-start | bytes 786440 | tf_op jit(solution)/shard_map/ppermute | solution.py:361
  85.0 17.4 %collective-permute-start.4 = (bf16[1024,768]{1,0:T(8,128)(2,1)}, bf16[1024,768]{1,0:T(8,128)(2,1)}, u32[]{:S(2)}, u32[]{:S(2)}) collective-permute-start(bf16[1024,768]{1,0:T(8,128)(2,1)} %bitcast.12), channel_id=1, source_target_pairs={{0,1},{1,0},{2,3},{3,2},{4,5},{5,4},{6,7},{7,6},{8,9},{9,8},{10,11... | collective-permute-start | bytes 4718600 | tf_op jit(solution)/shard_map/ppermute | solution.py:364
  85.1 17.3 %collective-permute-start.5 = (bf16[1024,768]{1,0:T(8,128)(2,1)}, bf16[1024,768]{1,0:T(8,128)(2,1)}, u32[]{:S(2)}, u32[]{:S(2)}) collective-permute-start(bf16[1024,768]{1,0:T(8,128)(2,1)} %bitcast.15), channel_id=1, source_target_pairs={{0,1},{1,0},{2,3},{3,2},{4,5},{5,4},{6,7},{7,6},{8,9},{9,8},{10,11... | collective-permute-start | bytes 4718600 | tf_op jit(solution)/shard_map/ppermute | solution.py:364
  85.6 16.8 %collective-permute-start.6 = (bf16[768,1024]{1,0:T(8,128)(2,1)}, bf16[768,1024]{1,0:T(8,128)(2,1)}, u32[]{:S(2)}, u32[]{:S(2)}) collective-permute-start(bf16[768,1024]{1,0:T(8,128)(2,1)} %bitcast.18), channel_id=1, source_target_pairs={{0,1},{1,0},{2,3},{3,2},{4,5},{5,4},{6,7},{7,6},{8,9},{9,8},{10,11... | collective-permute-start | bytes 4718600 | tf_op jit(solution)/shard_map/ppermute | solution.py:364
  95.3 7.1 %copy-start = (bf16[16,1,8,2048]{3,2,1,0:T(8,128)(2,1)S(1)}, bf16[16,1,8,2048]{3,2,1,0:T(8,128)(2,1)}, u32[]{:S(2)}) copy-start(bf16[16,1,8,2048]{3,2,1,0:T(8,128)(2,1)} %all_to_all.25.refs_0_) | copy-start | bytes 1572868
  95.3 27.2 %all-to-all-start.3 = ((bf16[16,3,8,2048]{3,2,1,0:T(8,128)(2,1)}), bf16[16,3,8,2048]{3,2,1,0:T(8,128)(2,1)}, u32[]{:S(2)}, u32[]{:S(2)}) async-start(bf16[16,3,8,2048]{3,2,1,0:T(8,128)(2,1)} %shard_map.108), calls=%async_computation.3 | async-start | bytes 3145728 | tf_op jit(solution)/shard_map/all_to_all | solution.py:384
  133.4 59.8 %all-to-all-start.4 = ((bf16[128,8,1024]{2,1,0:T(8,128)(2,1)}), bf16[128,8,1024]{2,1,0:T(8,128)(2,1)S(1)}, u32[]{:S(2)}, u32[]{:S(2)}) async-start(bf16[128,8,1024]{2,1,0:T(8,128)(2,1)} %bitcast.11), calls=%async_computation.4 | async-start | bytes 4194304 | tf_op jit(solution)/shard_map/all_to_all | solution.py:415
  150.0 3.6 %collective-permute-start.11 = (bf16[1024,768]{1,0:T(8,128)(2,1)}, bf16[1024,768]{1,0:T(8,128)(2,1)S(1)}, u32[]{:S(2)}, u32[]{:S(2)}) collective-permute-start(bf16[1024,768]{1,0:T(8,128)(2,1)} %get-tuple-element.52), channel_id=1, source_target_pairs={{0,1},{1,0},{2,3},{3,2},{4,5},{5,4},{6,7},{7,6},{8,9},{9,8},{10,11... | collective-permute-start | bytes 4718600 | tf_op jit(solution)/shard_map/ppermute | solution.py:364
  150.1 5.9 %collective-permute-start.12 = (bf16[1024,768]{1,0:T(8,128)(2,1)}, bf16[1024,768]{1,0:T(8,128)(2,1)S(1)}, u32[]{:S(2)}, u32[]{:S(2)}) collective-permute-start(bf16[1024,768]{1,0:T(8,128)(2,1)} %get-tuple-element.53), channel_id=1, source_target_pairs={{0,1},{1,0},{2,3},{3,2},{4,5},{5,4},{6,7},{7,6},{8,9},{9,8},{10,11... | collective-permute-start | bytes 4718600 | tf_op jit(solution)/shard_map/ppermute | solution.py:364
  150.6 7.6 %collective-permute-start.13 = (bf16[768,1024]{1,0:T(8,128)(2,1)}, bf16[768,1024]{1,0:T(8,128)(2,1)S(1)}, u32[]{:S(2)}, u32[]{:S(2)}) collective-permute-start(bf16[768,1024]{1,0:T(8,128)(2,1)} %get-tuple-element.54), channel_id=1, source_target_pairs={{0,1},{1,0},{2,3},{3,2},{4,5},{5,4},{6,7},{7,6},{8,9},{9,8},{10,11... | collective-permute-start | bytes 4718600 | tf_op jit(solution)/shard_map/ppermute | solution.py:364

commit v4 on v3

--- a/solution.py
+++ b/solution.py
@@ -59,16 +59,20 @@
     tokens = x_ref.shape[0]
     out_ref[:, 0:width] = x_ref[...]
     out_ref[:, width : 2 * width] = grad_ref[...]
-    lane = lax.broadcasted_iota(jnp.int32, (tokens, META), 1)
-    packed = jnp.zeros((tokens, META), F32)
+    row = lax.broadcasted_iota(jnp.int32, (META, tokens), 0)
+    packed = jnp.zeros((META, tokens), F32)
     for k in range(2):
-        packed = jnp.where(lane == k, ids_ref[:, k : k + 1].astype(F32), packed)
-        rest = gates_ref[:, k : k + 1]
+        packed = jnp.where(row == k, ids_ref[k : k + 1, :].astype(F32), packed)
+        rest = gates_ref[k : k + 1, :]
         for part in range(3):
             piece = rest.astype(BF).astype(F32)
-            packed = jnp.where(lane == 2 + 3 * k + part, piece, packed)
+            packed = jnp.where(row == 2 + 3 * k + part, piece, packed)
             rest = rest - piece
-    out_ref[:, 2 * width :] = packed.astype(BF)
+    same = lax.broadcasted_iota(jnp.int32, (tokens, tokens), 0) == lax.broadcasted_iota(
+        jnp.int32, (tokens, tokens), 1
+    )
+    columns = dot(same.astype(F32).astype(BF), packed.astype(BF), 1, 1)
+    out_ref[:, 2 * width :] = columns.astype(BF)
 
 
 def pack(x, grad, ids, gates):
@@ -77,7 +81,7 @@
         out_shape=jax.ShapeDtypeStruct((x.shape[0], 2 * x.shape[1] + META), BF),
         compiler_params=pltpu.CompilerParams(vmem_limit_bytes=VMEM_LIMIT),
         cost_estimate=TOKEN_COST,
-    )(*far_memory([x, grad]), ids, gates)
+    )(*far_memory([x, grad, ids, gates]))
 
 
 def build_kernel(jobs, sources, outs, waits, place_ref, *refs):
@@ -321,31 +325,41 @@
     )(*far_memory([*narrow, *whole]), *received)
 
 
-def combine_kernel(meta_ref, back_ref, out_ref):
-    rows = back_ref.shape[0]
+def returns_kernel(meta_ref, low_ref, high_ref):
+    rows = low_ref.shape[0]
     row = lax.broadcasted_iota(jnp.int32, (rows, 128), 0)
     hit, _ = hits(by_token(meta_ref[...]), row >> 3, row & 3)
     upper = ((row >> 2) & 1) == 1
-    low = (hit & ~upper).astype(F32).astype(BF)
-    high = (hit & upper).astype(F32).astype(BF)
-    out_ref[:, 0:HALF] = dot(low, back_ref[...], 0, 0).astype(BF)
-    out_ref[:, HALF : 2 * HALF] = dot(high, back_ref[...], 0, 0).astype(BF)
-
-
-def combine(packed, back):
-    rows = back.shape[0]
+    low_ref[...] = (hit & ~upper).astype(F32).astype(BF)
+    high_ref[...] = (hit & upper).astype(F32).astype(BF)
+
+
+def returns(packed, owners):
+    rows = owners * 2 * CAP
+    whole = pl.BlockSpec((rows, 128), lambda c: (0, 0))
+    return pl.pallas_call(
+        returns_kernel,
+        grid=(1,),
+        out_shape=[jax.ShapeDtypeStruct((rows, 128), BF)] * 2,
+        in_specs=[pl.BlockSpec((128, META), lambda c: (0, 4 * HALF // META))],
+        out_specs=[whole, whole],
+        compiler_params=pltpu.CompilerParams(vmem_limit_bytes=VMEM_LIMIT),
+        cost_estimate=TOKEN_COST,
+    )(packed)
+
+
+def combine_kernel(low_ref, high_ref, back_ref, out_ref):
+    out_ref[:, 0:HALF] = dot(low_ref[...], back_ref[...], 0, 0).astype(BF)
+    out_ref[:, HALF : 2 * HALF] = dot(high_ref[...], back_ref[...], 0, 0).astype(BF)
+
+
+def combine(low, high, back):
     return pl.pallas_call(
         combine_kernel,
-        grid=(1,),
         out_shape=jax.ShapeDtypeStruct((128, 2 * HALF), BF),
-        in_specs=[
-            pl.BlockSpec((128, META), lambda c: (0, 4 * HALF // META)),
-            pl.BlockSpec((rows, HALF), lambda c: (0, 0)),
-        ],
-        out_specs=pl.BlockSpec((128, 2 * HALF), lambda c: (0, 0)),
-        compiler_params=pltpu.CompilerParams(vmem_limit_bytes=VMEM_LIMIT),
-        cost_estimate=TOKEN_COST,
-    )(packed, back)
+        compiler_params=pltpu.CompilerParams(vmem_limit_bytes=VMEM_LIMIT),
+        cost_estimate=TOKEN_COST,
+    )(low, high, back)
 
 
 def local(inputs, out_grad, expert_ids, gates, gate_w, up_w, down_w):
@@ -363,7 +377,7 @@
     def swap(value):
         return lax.ppermute(value, "rep", [(0, 1), (1, 0)])
 
-    packed = pack(inputs, out_grad, expert_ids, gates)
+    packed = pack(inputs, out_grad, expert_ids.T, gates.T)
     data = {0: packed, 1: hop(packed, 1), -1: hop(packed, -1)}
     own = (gate_w[0], up_w[0], down_w[0])
     oth = tuple(swap(w) for w in own)
@@ -417,8 +431,9 @@
     )
     theirs = weight_grads(x_oth, s_oth, gate_grad, up_grad, hid, ())
     received = tuple(swap(part) for part in theirs)
+    low, high, received = lax.optimization_barrier((*returns(packed, owners), received))
     grads = weight_grads(x_own, s_own, gate_grad, up_grad, hid, received)
-    input_grad = combine(packed, returned.reshape(owners * 2 * CAP, HALF))
+    input_grad = combine(low, high, returned.reshape(owners * 2 * CAP, HALF))
     return (input_grad, grads[0][None], grads[1][None], grads[2][None])
 
 

time: 196 us -> 194 us (0.990)
  no operation moved by 1% of the time
where the time goes in v4:
time: 194 us; the launch traced here: 193 us
  waiting for transfers between devices  72.4 us (37%)
  Pallas kernels  55.1 us (28%)
  starting transfers between devices  42.6 us (22%)
  blocking collectives  18.4 us (9%)
  local copies, waits for them, and re-layouts  3.63 us (2%)
    all_to_all x1, waiting for transfers between devices, local(): lax.all_to_all(back.reshape(owners, 2 * CAP, HALF), 'expert', split_axis=...  27.5 us
    ppermute x8, waiting for transfers between devices, hop(): return lax.ppermute(value, 'expert', pairs)  27 us
    pallas_call x2, Pallas kernels, experts(): pl.pallas_call(functools.partial(expert_kernel, chunks, groups, has_base)...  23.6 us
    all_to_all x3, starting transfers between devices, exchange(): lax.all_to_all(sent, 'expert', split_axis=0, concat_axis=0, tiled=True, a...  21.2 us
    all_to_all x1, blocking collectives, exchange(): lax.all_to_all(sent, 'expert', split_axis=0, concat_axis=0, tiled=True, a...  18.4 us
    pallas_call x2, Pallas kernels, weight_grads(): pl.pallas_call(functools.partial(weight_kernel, len(xs), bool(received)),...  14.9 us
    all_to_all x3, waiting for transfers between devices, exchange(): lax.all_to_all(sent, 'expert', split_axis=0, concat_axis=0, tiled=True, a...  11.7 us
    pallas_call x4, Pallas kernels, build(): pl.pallas_call(functools.partial(build_kernel, jobs, sources, len(shapes)...  11 us
  transfers between devices with their start and end apart: 18, of which 11 were waited for; matrix products, arithmetic and copies ran while one was open for 1% of the time, Pallas kernels for 21%

profile of v4, /device:TPU:32, one launch (start us, length us, event | category | flops | bytes accessed | tf_op | source)
XLA Modules:
  0.0 193.0 jit_solution(5920128370859158731)
XLA Ops:
  4.2 2.3 %shard_map.104 = bf16[16,1,8,2048]{3,2,1,0:T(8,128)(2,1)} custom-call(s32[2]{0:T(128)S(1)} %pad_add_fusion.place_ref, bf16[128,4224]{1,0:T(8,128)(2,1)S(1)} %shard_map.102.meta_ref.refs_0_.refs_1_.refs_2_, bf16[128,4224]{1,0:T(8,128)(2,1)S(1)} %shard_map.102.meta_ref.refs_0_.refs_1_.refs_2_, bf16[128,4224]{1,0:T(8,128)(2,1)S(1)} %shard_map.102.meta_ref.refs_0_.refs_1_.refs_2_), custom_call_target="tpu_custom_call" | custom-call | flops 1 | bytes 1 | tf_op jit(solution)/shard_map/pallas_call | solution.py:124
  6.4 18.4 %all_to_all.25.refs_0_ = bf16[16,1,8,2048]{3,2,1,0:T(8,128)(2,1)} all-to-all(bf16[16,1,8,2048]{3,2,1,0:T(8,128)(2,1)} %shard_map.104), channel_id=1, replica_groups={{0,16,32,48,64,80,96,112,128,144,160,176,192,208,224,240},{2,18,34,50,6..., dimensions={0} | all-to-all | bytes 1048576 | tf_op jit(solution)/shard_map/all_to_all | solution.py:398
  24.8 3.0 %collective-permute-done.1.refs_1_.refs_4_.refs_5_ = bf16[128,4224]{1,0:T(8,128)(2,1)S(1)} collective-permute-done((bf16[128,4224]{1,0:T(8,128)(2,1)S(1)}, bf16[128,4224]{1,0:T(8,128)(2,1)S(1)}, u32[]{:S(2)}, u32[]{:S(2)}) %collective-permute-start.1) | collective-permute-done | bytes 1081376 | tf_op jit(solution)/shard_map/ppermute | solution.py:375
  28.8 2.9 %collective-permute-done.refs_0_.refs_2_.refs_3_ = bf16[128,4224]{1,0:T(8,128)(2,1)} collective-permute-done((bf16[128,4224]{1,0:T(8,128)(2,1)S(1)}, bf16[128,4224]{1,0:T(8,128)(2,1)}, u32[]{:S(2)}, u32[]{:S(2)}) %collective-permute-start) | collective-permute-done | bytes 1081376 | tf_op jit(solution)/shard_map/ppermute | solution.py:375
  31.7 3.0 %collective-permute-start.3 = (bf16[128,4224]{1,0:T(8,128)(2,1)}, bf16[128,4224]{1,0:T(8,128)(2,1)S(1)}, u32[]{:S(2)}, u32[]{:S(2)}) collective-permute-start(bf16[128,4224]{1,0:T(8,128)(2,1)} %copy-done.3), channel_id=1, source_target_pairs={{0,14},{2,0},{4,2},{6,4},{8,6},{10,8},{12,10},{14,12},{16,30},{18,... | collective-permute-start | bytes 3244040 | tf_op jit(solution)/shard_map/ppermute | solution.py:375
  34.7 3.1 %shard_map.105 = bf16[16,2,8,2048]{3,2,1,0:T(8,128)(2,1)} custom-call(s32[2]{0:T(128)S(1)} %pad_add_fusion.place_ref, bf16[128,4224]{1,0:T(8,128)(2,1)} %collective-permute-done.refs_0_.refs_2_.refs_3_, bf16[128,4224]{1,0:T(8,128)(2,1)} %copy-done.3, bf16[128,4224]{1,0:T(8,128)(2,1)} %collective-permute-done.refs_0_.refs_2_.refs_3_, ...), custom_call_target="tpu_custom_call" | custom-call | flops 1 | bytes 1 | tf_op jit(solution)/shard_map/pallas_call | solution.py:124
  37.8 7.1 %all-to-all-start.1 = ((bf16[16,2,8,2048]{3,2,1,0:T(8,128)(2,1)}), bf16[16,2,8,2048]{3,2,1,0:T(8,128)(2,1)}, u32[]{:S(2)}, u32[]{:S(2)}) async-start(bf16[16,2,8,2048]{3,2,1,0:T(8,128)(2,1)} %shard_map.105), calls=%async_computation.1 | async-start | bytes 2097152 | tf_op jit(solution)/shard_map/all_to_all | solution.py:398
  44.9 12.7 %collective-permute-done.2.refs_0_.refs_2_.refs_3_.refs_4_.refs_5_ = bf16[128,4224]{1,0:T(8,128)(2,1)S(1)} collective-permute-done((bf16[128,4224]{1,0:T(8,128)(2,1)}, bf16[128,4224]{1,0:T(8,128)(2,1)S(1)}, u32[]{:S(2)}, u32[]{:S(2)}) %collective-permute-start.2) | collective-permute-done | bytes 1081376 | tf_op jit(solution)/shard_map/ppermute | solution.py:375
  57.6 2.9 %shard_map.106 = (bf16[24,1,8,2048]{3,2,1,0:T(8,128)(2,1)}, bf16[24,1,8,2048]{3,2,1,0:T(8,128)(2,1)}) custom-call(s32[2]{0:T(128)S(1)} %pad_add_fusion.place_ref, bf16[128,4224]{1,0:T(8,128)(2,1)S(1)} %collective-permute-done.2.refs_0_.refs_2_.refs_3_.refs_4_.refs_5_, ...), custom_call_target="tpu_custom_call" | custom-call | flops 1 | bytes 1 | tf_op jit(solution)/shard_map/pallas_call | solution.py:124
  60.5 3.0 %collective-permute-start.8 = (bf16[24,1,8,2048]{3,2,1,0:T(8,128)(2,1)}, bf16[24,1,8,2048]{3,2,1,0:T(8,128)(2,1)}, u32[]{:S(2)}, u32[]{:S(2)}) collective-permute-start(bf16[24,1,8,2048]{3,2,1,0:T(8,128)(2,1)} %get-tuple-element.46), channel_id=1, source_target_pairs={{0,14},{2,0},{4,2},{6,4},{8,6},{10,8},{12,10},{14,12},{16,30},{18,... | collective-permute-start | bytes 2359304 | tf_op jit(solution)/shard_map/ppermute | solution.py:375
  63.5 2.7 %shard_map.107 = bf16[16,2,8,2048]{3,2,1,0:T(8,128)(2,1)} custom-call(s32[2]{0:T(128)S(1)} %pad_add_fusion.place_ref, bf16[24,1,8,2048]{3,2,1,0:T(8,128)(2,1)} %get-tuple-element.43.refs_0_, bf16[16,2,8,2048]{3,2,1,0:T(8,128)(2,1)} %all-to-all-done.1.refs_1_, bf16[128,4224]{1,0:T(8,128)(2,1)S(1)} %collective-permute-done.2.refs_0_.refs_2_.refs_3_.refs_4_.refs_5_, ...), custom_call_target="tpu_custom_call" | custom-call | flops 1 | bytes 1 | tf_op jit(solution)/shard_map/pallas_call | solution.py:124
  66.1 7.0 %all-to-all-start.2 = ((bf16[16,2,8,2048]{3,2,1,0:T(8,128)(2,1)}), bf16[16,2,8,2048]{3,2,1,0:T(8,128)(2,1)S(1)}, u32[]{:S(2)}, u32[]{:S(2)}) async-start(bf16[16,2,8,2048]{3,2,1,0:T(8,128)(2,1)} %shard_map.107), calls=%async_computation.2 | async-start | bytes 2097152 | tf_op jit(solution)/shard_map/all_to_all | solution.py:398
  73.2 5.4 %collective-permute-done.8.right_ref = bf16[24,1,8,2048]{3,2,1,0:T(8,128)(2,1)} collective-permute-done((bf16[24,1,8,2048]{3,2,1,0:T(8,128)(2,1)}, bf16[24,1,8,2048]{3,2,1,0:T(8,128)(2,1)}, u32[]{:S(2)}, u32[]{:S(2)}) %collective-permute-start.8) | collective-permute-done | bytes 786464 | tf_op jit(solution)/shard_map/ppermute | solution.py:375
  79.6 2.8 %collective-permute-start.10 = (bf16[8,1,8,2048]{3,2,1,0:T(8,128)(2,1)S(1)}, bf16[8,1,8,2048]{3,2,1,0:T(8,128)(2,1)S(1)}, u32[]{:S(2)}, u32[]{:S(2)}) collective-permute-start(bf16[8,1,8,2048]{3,2,1,0:T(8,128)(2,1)S(1)} %slice.9), channel_id=1, source_target_pairs={{0,14},{2,0},{4,2},{6,4},{8,6},{10,8},{12,10},{14,12},{16,30},{18,... | collective-permute-start | bytes 786440 | tf_op jit(solution)/shard_map/ppermute | solution.py:375
  84.1 4.3 %all-to-all-done.2.refs_2_.after_ref = bf16[16,2,8,2048]{3,2,1,0:T(8,128)(2,1)S(1)} async-done(((bf16[16,2,8,2048]{3,2,1,0:T(8,128)(2,1)}), bf16[16,2,8,2048]{3,2,1,0:T(8,128)(2,1)S(1)}, u32[]{:S(2)}, u32[]{:S(2)}) %all-to-all-start.2) | async-done | bytes 1048608 | tf_op jit(solution)/shard_map/all_to_all | solution.py:398
  88.4 3.0 %collective-permute-done.9.far_left_ref = bf16[8,1,8,2048]{3,2,1,0:T(8,128)(2,1)S(1)} collective-permute-done((bf16[8,1,8,2048]{3,2,1,0:T(8,128)(2,1)S(1)}, bf16[8,1,8,2048]{3,2,1,0:T(8,128)(2,1)S(1)}, u32[]{:S(2)}, u32[]{:S(2)}) %collective-permute-start.9) | collective-permute-done | bytes 262176 | tf_op jit(solution)/shard_map/ppermute | solution.py:375
  93.6 7.1 %all-to-all-start.3 = ((bf16[16,3,8,2048]{3,2,1,0:T(8,128)(2,1)}), bf16[16,3,8,2048]{3,2,1,0:T(8,128)(2,1)}, u32[]{:S(2)}, u32[]{:S(2)}) async-start(bf16[16,3,8,2048]{3,2,1,0:T(8,128)(2,1)} %shard_map.109), calls=%async_computation.3 | async-start | bytes 3145728 | tf_op jit(solution)/shard_map/all_to_all | solution.py:398
  100.8 12.7 %shard_map.108 = (bf16[320,1024]{1,0:T(8,128)(2,1)}, bf16[320,1024]{1,0:T(8,128)(2,1)}, bf16[320,1024]{1,0:T(8,128)(2,1)}, bf16[320,1024]{1,0:T(8,128)(2,1)}, bf...) custom-call(s32[2]{0:T(128)S(1)} %pad_add_fusion.place_ref, ...), custom_call_target="tpu_custom_call" | custom-call | flops 1 | bytes 1 | tf_op jit(solution)/shard_map/pallas_call | solution.py:259
  113.5 7.4 %all-to-all-done.3.refs_1_ = bf16[16,3,8,2048]{3,2,1,0:T(8,128)(2,1)} async-done(((bf16[16,3,8,2048]{3,2,1,0:T(8,128)(2,1)}), bf16[16,3,8,2048]{3,2,1,0:T(8,128)(2,1)}, u32[]{:S(2)}, u32[]{:S(2)}) %all-to-all-start.3) | async-done | bytes 1572896 | tf_op jit(solution)/shard_map/all_to_all | solution.py:398
  120.9 10.9 %shard_map.110 = (bf16[192,1024]{1,0:T(8,128)(2,1)}, bf16[192,1024]{1,0:T(8,128)(2,1)}, bf16[192,1024]{1,0:T(8,128)(2,1)}, bf16[192,1024]{1,0:T(8,128)(2,1)}, bf...) custom-call(s32[2]{0:T(128)S(1)} %pad_add_fusion.place_ref, ...), custom_call_target="tpu_custom_call", output_to_operand_aliasing={{7}: (1, {})} | custom-call | flops 1 | bytes 1 | tf_op jit(solution)/shard_map/pallas_call | solution.py:259
  131.7 9.3 %all-to-all-start.4 = ((bf16[128,8,1024]{2,1,0:T(8,128)(2,1)}), bf16[128,8,1024]{2,1,0:T(8,128)(2,1)S(1)}, u32[]{:S(2)}, u32[]{:S(2)}) async-start(bf16[128,8,1024]{2,1,0:T(8,128)(2,1)} %bitcast.13), calls=%async_computation.4 | async-start | bytes 4194304 | tf_op jit(solution)/shard_map/all_to_all | solution.py:429
  141.0 7.4 %shard_map.111 = (bf16[1024,768]{1,0:T(8,128)(2,1)}, bf16[1024,768]{1,0:T(8,128)(2,1)}, bf16[768,1024]{1,0:T(8,128)(2,1)}) custom-call(bf16[320,1024]{1,0:T(8,128)(2,1)} %get-tuple-element.44.refs_0_, bf16[192,1024]{1,0:T(8,128)(2,1)} %get-tuple-element.47.refs_1_, bf16[320,1024]{1,0:T(8,128)(2,1)} %get-tuple-element.48.refs_2_, ...), custom_call_target="tpu_custom_call" | custom-call | flops 1 | bytes 1 | tf_op jit(solution)/shard_map/pallas_call | solution.py:311
  156.5 7.5 %shard_map.113 = (bf16[1024,768]{1,0:T(8,128)(2,1)}, bf16[1024,768]{1,0:T(8,128)(2,1)}, bf16[768,1024]{1,0:T(8,128)(2,1)}) custom-call(bf16[320,1024]{1,0:T(8,128)(2,1)} %get-tuple-element.62.refs_0_, bf16[192,1024]{1,0:T(8,128)(2,1)} %get-tuple-element.63.refs_1_, bf16[320,1024]{1,0:T(8,128)(2,1)} %get-tuple-element.64.refs_2_, ...), custom_call_target="tpu_custom_call" | custom-call | flops 1 | bytes 1 | tf_op jit(solution)/shard_map/pallas_call | solution.py:311
  164.0 27.5 %all-to-all-done.4 = bf16[128,8,1024]{2,1,0:T(8,128)(2,1)S(1)} async-done(((bf16[128,8,1024]{2,1,0:T(8,128)(2,1)}), bf16[128,8,1024]{2,1,0:T(8,128)(2,1)S(1)}, u32[]{:S(2)}, u32[]{:S(2)}) %all-to-all-start.4) | async-done | bytes 2097184 | tf_op jit(solution)/shard_map/all_to_all | solution.py:429
  (36 shorter events, 19.1 us)
Async XLA Ops:
  2.0 25.8 %collective-permute-start.1 = (bf16[128,4224]{1,0:T(8,128)(2,1)S(1)}, bf16[128,4224]{1,0:T(8,128)(2,1)S(1)}, u32[]{:S(2)}, u32[]{:S(2)}) collective-permute-start(bf16[128,4224]{1,0:T(8,128)(2,1)S(1)} %shard_map.102.meta_ref.refs_0_.refs_1_.refs_2_), channel_id=1, source_target_pairs={{0,14},{2,0},{4,2},{6,4},{8,6},{10,8},{12,10},{14,12},{16,30},{18,... | collective-permute-start | bytes 3244040 | tf_op jit(solution)/shard_map/ppermute | solution.py:375
  3.9 27.8 %collective-permute-start = (bf16[128,4224]{1,0:T(8,128)(2,1)S(1)}, bf16[128,4224]{1,0:T(8,128)(2,1)}, u32[]{:S(2)}, u32[]{:S(2)}) collective-permute-start(bf16[128,4224]{1,0:T(8,128)(2,1)S(1)} %shard_map.102.meta_ref.refs_0_.refs_1_.refs_2_), channel_id=1, source_target_pairs={{0,2},{2,4},{4,6},{6,8},{8,10},{10,12},{12,14},{14,0},{16,18},{18,... | collective-permute-start | bytes 3244040 | tf_op jit(solution)/shard_map/ppermute | solution.py:375
  27.9 1.0 copy-start.3
  31.7 25.8 %collective-permute-start.2 = (bf16[128,4224]{1,0:T(8,128)(2,1)}, bf16[128,4224]{1,0:T(8,128)(2,1)S(1)}, u32[]{:S(2)}, u32[]{:S(2)}) collective-permute-start(bf16[128,4224]{1,0:T(8,128)(2,1)} %collective-permute-done.refs_0_.refs_2_.refs_3_), channel_id=1, source_target_pairs={{0,2},{2,4},{4,6},{6,8},{8,10},{10,12},{12,14},{14,0},{16,18},{18,... | collective-permute-start | bytes 3244040 | tf_op jit(solution)/shard_map/ppermute | solution.py:375
  31.7 25.8 %collective-permute-start.3 = (bf16[128,4224]{1,0:T(8,128)(2,1)}, bf16[128,4224]{1,0:T(8,128)(2,1)S(1)}, u32[]{:S(2)}, u32[]{:S(2)}) collective-permute-start(bf16[128,4224]{1,0:T(8,128)(2,1)} %copy-done.3), channel_id=1, source_target_pairs={{0,14},{2,0},{4,2},{6,4},{8,6},{10,8},{12,10},{14,12},{16,30},{18,... | collective-permute-start | bytes 3244040 | tf_op jit(solution)/shard_map/ppermute | solution.py:375
  37.8 25.7 %all-to-all-start.1 = ((bf16[16,2,8,2048]{3,2,1,0:T(8,128)(2,1)}), bf16[16,2,8,2048]{3,2,1,0:T(8,128)(2,1)}, u32[]{:S(2)}, u32[]{:S(2)}) async-start(bf16[16,2,8,2048]{3,2,1,0:T(8,128)(2,1)} %shard_map.105), calls=%async_computation.1 | async-start | bytes 2097152 | tf_op jit(solution)/shard_map/all_to_all | solution.py:398
  60.5 18.1 %collective-permute-start.8 = (bf16[24,1,8,2048]{3,2,1,0:T(8,128)(2,1)}, bf16[24,1,8,2048]{3,2,1,0:T(8,128)(2,1)}, u32[]{:S(2)}, u32[]{:S(2)}) collective-permute-start(bf16[24,1,8,2048]{3,2,1,0:T(8,128)(2,1)} %get-tuple-element.46), channel_id=1, source_target_pairs={{0,14},{2,0},{4,2},{6,4},{8,6},{10,8},{12,10},{14,12},{16,30},{18,... | collective-permute-start | bytes 2359304 | tf_op jit(solution)/shard_map/ppermute | solution.py:375
  63.5 18.8 %collective-permute-start.7 = (bf16[24,1,8,2048]{3,2,1,0:T(8,128)(2,1)}, bf16[24,1,8,2048]{3,2,1,0:T(8,128)(2,1)}, u32[]{:S(2)}, u32[]{:S(2)}) collective-permute-start(bf16[24,1,8,2048]{3,2,1,0:T(8,128)(2,1)} %get-tuple-element.43.refs_0_), channel_id=1, source_target_pairs={{0,2},{2,4},{4,6},{6,8},{8,10},{10,12},{12,14},{14,0},{16,18},{18,... | collective-permute-start | bytes 2359304 | tf_op jit(solution)/shard_map/ppermute | solution.py:375
  66.1 22.3 %all-to-all-start.2 = ((bf16[16,2,8,2048]{3,2,1,0:T(8,128)(2,1)}), bf16[16,2,8,2048]{3,2,1,0:T(8,128)(2,1)S(1)}, u32[]{:S(2)}, u32[]{:S(2)}) async-start(bf16[16,2,8,2048]{3,2,1,0:T(8,128)(2,1)} %shard_map.107), calls=%async_computation.2 | async-start | bytes 2097152 | tf_op jit(solution)/shard_map/all_to_all | solution.py:398
  79.6 8.9 %collective-permute-start.10 = (bf16[8,1,8,2048]{3,2,1,0:T(8,128)(2,1)S(1)}, bf16[8,1,8,2048]{3,2,1,0:T(8,128)(2,1)S(1)}, u32[]{:S(2)}, u32[]{:S(2)}) collective-permute-start(bf16[8,1,8,2048]{3,2,1,0:T(8,128)(2,1)S(1)} %slice.9), channel_id=1, source_target_pairs={{0,14},{2,0},{4,2},{6,4},{8,6},{10,8},{12,10},{14,12},{16,30},{18,... | collective-permute-start | bytes 786440 | tf_op jit(solution)/shard_map/ppermute | solution.py:375
  83.3 8.1 %collective-permute-start.9 = (bf16[8,1,8,2048]{3,2,1,0:T(8,128)(2,1)S(1)}, bf16[8,1,8,2048]{3,2,1,0:T(8,128)(2,1)S(1)}, u32[]{:S(2)}, u32[]{:S(2)}) collective-permute-start(bf16[8,1,8,2048]{3,2,1,0:T(8,128)(2,1)S(1)} %slice.8), channel_id=1, source_target_pairs={{0,2},{2,4},{4,6},{6,8},{8,10},{10,12},{12,14},{14,0},{16,18},{18,... | collective-permute-start | bytes 786440 | tf_op jit(solution)/shard_map/ppermute | solution.py:375
  83.4 17.4 %collective-permute-start.4 = (bf16[1024,768]{1,0:T(8,128)(2,1)}, bf16[1024,768]{1,0:T(8,128)(2,1)}, u32[]{:S(2)}, u32[]{:S(2)}) collective-permute-start(bf16[1024,768]{1,0:T(8,128)(2,1)} %bitcast.14), channel_id=1, source_target_pairs={{0,1},{1,0},{2,3},{3,2},{4,5},{5,4},{6,7},{7,6},{8,9},{9,8},{10,11... | collective-permute-start | bytes 4718600 | tf_op jit(solution)/shard_map/ppermute | solution.py:378
  83.5 17.3 %collective-permute-start.5 = (bf16[1024,768]{1,0:T(8,128)(2,1)}, bf16[1024,768]{1,0:T(8,128)(2,1)}, u32[]{:S(2)}, u32[]{:S(2)}) collective-permute-start(bf16[1024,768]{1,0:T(8,128)(2,1)} %bitcast.17), channel_id=1, source_target_pairs={{0,1},{1,0},{2,3},{3,2},{4,5},{5,4},{6,7},{7,6},{8,9},{9,8},{10,11... | collective-permute-start | bytes 4718600 | tf_op jit(solution)/shard_map/ppermute | solution.py:378
  84.0 16.8 %collective-permute-start.6 = (bf16[768,1024]{1,0:T(8,128)(2,1)}, bf16[768,1024]{1,0:T(8,128)(2,1)}, u32[]{:S(2)}, u32[]{:S(2)}) collective-permute-start(bf16[768,1024]{1,0:T(8,128)(2,1)} %bitcast.20), channel_id=1, source_target_pairs={{0,1},{1,0},{2,3},{3,2},{4,5},{5,4},{6,7},{7,6},{8,9},{9,8},{10,11... | collective-permute-start | bytes 4718600 | tf_op jit(solution)/shard_map/ppermute | solution.py:378
  93.6 7.1 %copy-start = (bf16[16,1,8,2048]{3,2,1,0:T(8,128)(2,1)S(1)}, bf16[16,1,8,2048]{3,2,1,0:T(8,128)(2,1)}, u32[]{:S(2)}) copy-start(bf16[16,1,8,2048]{3,2,1,0:T(8,128)(2,1)} %all_to_all.25.refs_0_) | copy-start | bytes 1572868
  93.6 27.2 %all-to-all-start.3 = ((bf16[16,3,8,2048]{3,2,1,0:T(8,128)(2,1)}), bf16[16,3,8,2048]{3,2,1,0:T(8,128)(2,1)}, u32[]{:S(2)}, u32[]{:S(2)}) async-start(bf16[16,3,8,2048]{3,2,1,0:T(8,128)(2,1)} %shard_map.109), calls=%async_computation.3 | async-start | bytes 3145728 | tf_op jit(solution)/shard_map/all_to_all | solution.py:398
  131.7 59.8 %all-to-all-start.4 = ((bf16[128,8,1024]{2,1,0:T(8,128)(2,1)}), bf16[128,8,1024]{2,1,0:T(8,128)(2,1)S(1)}, u32[]{:S(2)}, u32[]{:S(2)}) async-start(bf16[128,8,1024]{2,1,0:T(8,128)(2,1)} %bitcast.13), calls=%async_computation.4 | async-start | bytes 4194304 | tf_op jit(solution)/shard_map/all_to_all | solution.py:429
  148.4 3.6 %collective-permute-start.11 = (bf16[1024,768]{1,0:T(8,128)(2,1)}, bf16[1024,768]{1,0:T(8,128)(2,1)S(1)}, u32[]{:S(2)}, u32[]{:S(2)}) collective-permute-start(bf16[1024,768]{1,0:T(8,128)(2,1)} %get-tuple-element.56), channel_id=1, source_target_pairs={{0,1},{1,0},{2,3},{3,2},{4,5},{5,4},{6,7},{7,6},{8,9},{9,8},{10,11... | collective-permute-start | bytes 4718600 | tf_op jit(solution)/shard_map/ppermute | solution.py:378
  148.4 5.9 %collective-permute-start.12 = (bf16[1024,768]{1,0:T(8,128)(2,1)}, bf16[1024,768]{1,0:T(8,128)(2,1)S(1)}, u32[]{:S(2)}, u32[]{:S(2)}) collective-permute-start(bf16[1024,768]{1,0:T(8,128)(2,1)} %get-tuple-element.57), channel_id=1, source_target_pairs={{0,1},{1,0},{2,3},{3,2},{4,5},{5,4},{6,7},{7,6},{8,9},{9,8},{10,11... | collective-permute-start | bytes 4718600 | tf_op jit(solution)/shard_map/ppermute | solution.py:378
  148.9 7.6 %collective-permute-start.13 = (bf16[768,1024]{1,0:T(8,128)(2,1)}, bf16[768,1024]{1,0:T(8,128)(2,1)S(1)}, u32[]{:S(2)}, u32[]{:S(2)}) collective-permute-start(bf16[768,1024]{1,0:T(8,128)(2,1)} %get-tuple-element.58), channel_id=1, source_target_pairs={{0,1},{1,0},{2,3},{3,2},{4,5},{5,4},{6,7},{7,6},{8,9},{9,8},{10,11... | collective-permute-start | bytes 4718600 | tf_op jit(solution)/shard_map/ppermute | solution.py:378
  149.6 0.7 copy-start.1
  156.5 34.9 %copy-start.2 = (bf16[1024,128]{1,0:T(8,128)(2,1)S(1)}, bf16[1024,128]{1,0:T(8,128)(2,1)}, u32[]{:S(2)}) copy-start(bf16[1024,128]{1,0:T(8,128)(2,1)} %copy-done.1) | copy-start | bytes 786436

commit v5 on v4

--- a/solution.py
+++ b/solution.py
@@ -140,29 +140,48 @@
     )(place, *after, *planes, *[p for p in planes for _ in range(2)])
 
 
-def join_kernel(left_ref, right_ref, far_left_ref, far_right_ref, after_ref, out_ref):
-    del after_ref
-    half = far_left_ref.shape[0]
+def third_kernel(left_ref, right_ref, out_ref):
     out_ref[:, 0:1] = left_ref[...]
     out_ref[:, 1:2] = right_ref[...]
-    out_ref[0:half, 2:3] = far_left_ref[...]
-    out_ref[half:, 2:3] = far_right_ref[...]
+
+
+def fourth_kernel(base_ref, left_ref, right_ref, after_ref, out_ref, sems):
+    del base_ref, after_ref
+    half = left_ref.shape[0]
+    copies = [
+        pltpu.make_async_copy(left_ref.at[:, 0], out_ref.at[0:half, 2], sems.at[0]),
+        pltpu.make_async_copy(right_ref.at[:, 0], out_ref.at[half:, 2], sems.at[1]),
+    ]
+    for copy in copies:
+        copy.start()
+    for copy in copies:
+        copy.wait()
 
 
 def join(third, fourth, groups, after):
     features = third[0].shape[3]
-    shape = (groups, 1, 2 * CAP)
-    specs = [pl.BlockSpec(shape + (COLS,), lambda c: (0, 0, 0, c))] * 2
-    specs += [pl.BlockSpec(v.shape[:3] + (COLS,), lambda c: (0, 0, 0, c)) for v in fourth]
-    return pl.pallas_call(
-        join_kernel,
+    shape = pltpu.HBM((groups, 3, 2 * CAP, features), BF)
+    anywhere = pl.BlockSpec(memory_space=pl.ANY)
+    base = pl.pallas_call(
+        third_kernel,
         grid=(features // COLS,),
-        out_shape=pltpu.HBM((groups, 3, 2 * CAP, features), BF),
-        in_specs=specs + [pl.BlockSpec(memory_space=pl.ANY)],
-        out_specs=pl.BlockSpec((groups, 3, 2 * CAP, COLS), lambda c: (0, 0, 0, c)),
-        compiler_params=pltpu.CompilerParams(vmem_limit_bytes=VMEM_LIMIT),
-        cost_estimate=TOKEN_COST,
-    )(*third, *fourth, after)
+        out_shape=shape,
+        in_specs=[pl.BlockSpec((groups, 1, 2 * CAP, COLS), lambda c: (0, 0, 0, c))] * 2,
+        out_specs=pl.BlockSpec((groups, 2, 2 * CAP, COLS), lambda c: (0, 0, 0, c)),
+        compiler_params=pltpu.CompilerParams(vmem_limit_bytes=VMEM_LIMIT),
+        cost_estimate=TOKEN_COST,
+    )(*third)
+    base, after = lax.optimization_barrier((base, after))
+    return pl.pallas_call(
+        fourth_kernel,
+        out_shape=shape,
+        in_specs=[anywhere] * 4,
+        out_specs=anywhere,
+        scratch_shapes=[pltpu.SemaphoreType.DMA((2,))],
+        input_output_aliases={0: 0},
+        compiler_params=pltpu.CompilerParams(vmem_limit_bytes=VMEM_LIMIT),
+        cost_estimate=TOKEN_COST,
+    )(*far_memory([base]), *fourth, after)
 
 
 def expert_kernel(chunks, groups, has_base, place_ref, *refs):

time: 194 us -> 197 us (1.015)
    all_to_all x1, waiting for transfers between devices: 27.5 us -> 31 us  [local(): lax.all_to_all(back.reshape(owners, 2 * CAP, HALF), 'expert', split_axis=...]
    all_to_all x3, waiting for transfers between devices: 11.7 us -> 9.69 us  [exchange(): lax.all_to_all(sent, 'expert', split_axis=0, concat_axis=0, tiled=True, a...]
where the time goes in v5:
time: 197 us; the launch traced here: 196 us
  waiting for transfers between devices  73.9 us (38%)
  Pallas kernels  55.7 us (28%)
  starting transfers between devices  43.4 us (22%)
  blocking collectives  18.4 us (9%)
  local copies, waits for them, and re-layouts  3.61 us (2%)
    all_to_all x1, waiting for transfers between devices, local(): lax.all_to_all(back.reshape(owners, 2 * CAP, HALF), 'expert', split_axis=...  31 us
    ppermute x8, waiting for transfers between devices, hop(): return lax.ppermute(value, 'expert', pairs)  27 us
    pallas_call x2, Pallas kernels, experts(): pl.pallas_call(functools.partial(expert_kernel, chunks, groups, has_base)...  23.6 us
    all_to_all x3, starting transfers between devices, exchange(): lax.all_to_all(sent, 'expert', split_axis=0, concat_axis=0, tiled=True, a...  21.2 us
    all_to_all x1, blocking collectives, exchange(): lax.all_to_all(sent, 'expert', split_axis=0, concat_axis=0, tiled=True, a...  18.4 us
    pallas_call x2, Pallas kernels, weight_grads(): pl.pallas_call(functools.partial(weight_kernel, len(xs), bool(received)),...  14.9 us
    pallas_call x4, Pallas kernels, build(): pl.pallas_call(functools.partial(build_kernel, jobs, sources, len(shapes)...  11 us
    ppermute x8, starting transfers between devices, hop(): return lax.ppermute(value, 'expert', pairs)  10.8 us
  transfers between devices with their start and end apart: 18, of which 11 were waited for; matrix products, arithmetic and copies ran while one was open for 1% of the time, Pallas kernels for 21%

profile of v5, /device:TPU:32, one launch (start us, length us, event | category | flops | bytes accessed | tf_op | source)
XLA Modules:
  0.0 195.9 jit_solution(11958442882050609723)
XLA Ops:
  4.2 2.3 %shard_map.104 = bf16[16,1,8,2048]{3,2,1,0:T(8,128)(2,1)} custom-call(s32[2]{0:T(128)S(1)} %pad_add_fusion.place_ref, bf16[128,4224]{1,0:T(8,128)(2,1)S(1)} %shard_map.102.meta_ref.refs_0_.refs_1_.refs_2_, bf16[128,4224]{1,0:T(8,128)(2,1)S(1)} %shard_map.102.meta_ref.refs_0_.refs_1_.refs_2_, bf16[128,4224]{1,0:T(8,128)(2,1)S(1)} %shard_map.102.meta_ref.refs_0_.refs_1_.refs_2_), custom_call_target="tpu_custom_call" | custom-call | flops 1 | bytes 1 | tf_op jit(solution)/shard_map/pallas_call | solution.py:124
  6.4 18.4 %all_to_all.25.refs_0_ = bf16[16,1,8,2048]{3,2,1,0:T(8,128)(2,1)} all-to-all(bf16[16,1,8,2048]{3,2,1,0:T(8,128)(2,1)} %shard_map.104), channel_id=1, replica_groups={{0,16,32,48,64,80,96,112,128,144,160,176,192,208,224,240},{2,18,34,50,6..., dimensions={0} | all-to-all | bytes 1048576 | tf_op jit(solution)/shard_map/all_to_all | solution.py:417
  24.8 3.0 %collective-permute-done.1.refs_1_.refs_4_.refs_5_ = bf16[128,4224]{1,0:T(8,128)(2,1)S(1)} collective-permute-done((bf16[128,4224]{1,0:T(8,128)(2,1)S(1)}, bf16[128,4224]{1,0:T(8,128)(2,1)S(1)}, u32[]{:S(2)}, u32[]{:S(2)}) %collective-permute-start.1) | collective-permute-done | bytes 1081376 | tf_op jit(solution)/shard_map/ppermute | solution.py:394
  28.8 2.9 %collective-permute-done.refs_0_.refs_2_.refs_3_ = bf16[128,4224]{1,0:T(8,128)(2,1)} collective-permute-done((bf16[128,4224]{1,0:T(8,128)(2,1)S(1)}, bf16[128,4224]{1,0:T(8,128)(2,1)}, u32[]{:S(2)}, u32[]{:S(2)}) %collective-permute-start) | collective-permute-done | bytes 1081376 | tf_op jit(solution)/shard_map/ppermute | solution.py:394
  31.7 3.0 %collective-permute-start.3 = (bf16[128,4224]{1,0:T(8,128)(2,1)}, bf16[128,4224]{1,0:T(8,128)(2,1)S(1)}, u32[]{:S(2)}, u32[]{:S(2)}) collective-permute-start(bf16[128,4224]{1,0:T(8,128)(2,1)} %copy-done.3), channel_id=1, source_target_pairs={{0,14},{2,0},{4,2},{6,4},{8,6},{10,8},{12,10},{14,12},{16,30},{18,... | collective-permute-start | bytes 3244040 | tf_op jit(solution)/shard_map/ppermute | solution.py:394
  34.7 3.1 %shard_map.105 = bf16[16,2,8,2048]{3,2,1,0:T(8,128)(2,1)} custom-call(s32[2]{0:T(128)S(1)} %pad_add_fusion.place_ref, bf16[128,4224]{1,0:T(8,128)(2,1)} %collective-permute-done.refs_0_.refs_2_.refs_3_, bf16[128,4224]{1,0:T(8,128)(2,1)} %copy-done.3, bf16[128,4224]{1,0:T(8,128)(2,1)} %collective-permute-done.refs_0_.refs_2_.refs_3_, ...), custom_call_target="tpu_custom_call" | custom-call | flops 1 | bytes 1 | tf_op jit(solution)/shard_map/pallas_call | solution.py:124
  37.8 7.1 %all-to-all-start.1 = ((bf16[16,2,8,2048]{3,2,1,0:T(8,128)(2,1)}), bf16[16,2,8,2048]{3,2,1,0:T(8,128)(2,1)}, u32[]{:S(2)}, u32[]{:S(2)}) async-start(bf16[16,2,8,2048]{3,2,1,0:T(8,128)(2,1)} %shard_map.105), calls=%async_computation.1 | async-start | bytes 2097152 | tf_op jit(solution)/shard_map/all_to_all | solution.py:417
  44.9 12.7 %collective-permute-done.2.refs_0_.refs_2_.refs_3_.refs_4_.refs_5_ = bf16[128,4224]{1,0:T(8,128)(2,1)S(1)} collective-permute-done((bf16[128,4224]{1,0:T(8,128)(2,1)}, bf16[128,4224]{1,0:T(8,128)(2,1)S(1)}, u32[]{:S(2)}, u32[]{:S(2)}) %collective-permute-start.2) | collective-permute-done | bytes 1081376 | tf_op jit(solution)/shard_map/ppermute | solution.py:394
  57.6 2.9 %shard_map.106 = (bf16[24,1,8,2048]{3,2,1,0:T(8,128)(2,1)}, bf16[24,1,8,2048]{3,2,1,0:T(8,128)(2,1)}) custom-call(s32[2]{0:T(128)S(1)} %pad_add_fusion.place_ref, bf16[128,4224]{1,0:T(8,128)(2,1)S(1)} %collective-permute-done.2.refs_0_.refs_2_.refs_3_.refs_4_.refs_5_, ...), custom_call_target="tpu_custom_call" | custom-call | flops 1 | bytes 1 | tf_op jit(solution)/shard_map/pallas_call | solution.py:124
  60.5 3.0 %collective-permute-start.8 = (bf16[24,1,8,2048]{3,2,1,0:T(8,128)(2,1)}, bf16[24,1,8,2048]{3,2,1,0:T(8,128)(2,1)}, u32[]{:S(2)}, u32[]{:S(2)}) collective-permute-start(bf16[24,1,8,2048]{3,2,1,0:T(8,128)(2,1)} %get-tuple-element.48), channel_id=1, source_target_pairs={{0,14},{2,0},{4,2},{6,4},{8,6},{10,8},{12,10},{14,12},{16,30},{18,... | collective-permute-start | bytes 2359304 | tf_op jit(solution)/shard_map/ppermute | solution.py:394
  63.5 2.7 %shard_map.107 = bf16[16,2,8,2048]{3,2,1,0:T(8,128)(2,1)} custom-call(s32[2]{0:T(128)S(1)} %pad_add_fusion.place_ref, bf16[24,1,8,2048]{3,2,1,0:T(8,128)(2,1)} %get-tuple-element.45.refs_0_, bf16[16,2,8,2048]{3,2,1,0:T(8,128)(2,1)} %all-to-all-done.1.refs_1_, bf16[128,4224]{1,0:T(8,128)(2,1)S(1)} %collective-permute-done.2.refs_0_.refs_2_.refs_3_.refs_4_.refs_5_, ...), custom_call_target="tpu_custom_call" | custom-call | flops 1 | bytes 1 | tf_op jit(solution)/shard_map/pallas_call | solution.py:124
  66.1 7.0 %all-to-all-start.2 = ((bf16[16,2,8,2048]{3,2,1,0:T(8,128)(2,1)}), bf16[16,2,8,2048]{3,2,1,0:T(8,128)(2,1)S(1)}, u32[]{:S(2)}, u32[]{:S(2)}) async-start(bf16[16,2,8,2048]{3,2,1,0:T(8,128)(2,1)} %shard_map.107), calls=%async_computation.2 | async-start | bytes 2097152 | tf_op jit(solution)/shard_map/all_to_all | solution.py:417
  73.2 5.4 %collective-permute-done.8.right_ref = bf16[24,1,8,2048]{3,2,1,0:T(8,128)(2,1)} collective-permute-done((bf16[24,1,8,2048]{3,2,1,0:T(8,128)(2,1)}, bf16[24,1,8,2048]{3,2,1,0:T(8,128)(2,1)}, u32[]{:S(2)}, u32[]{:S(2)}) %collective-permute-start.8) | collective-permute-done | bytes 786464 | tf_op jit(solution)/shard_map/ppermute | solution.py:394
  79.6 2.8 %collective-permute-start.10 = (bf16[8,1,8,2048]{3,2,1,0:T(8,128)(2,1)S(1)}, bf16[8,1,8,2048]{3,2,1,0:T(8,128)(2,1)S(1)}, u32[]{:S(2)}, u32[]{:S(2)}) collective-permute-start(bf16[8,1,8,2048]{3,2,1,0:T(8,128)(2,1)S(1)} %slice.9), channel_id=1, source_target_pairs={{0,14},{2,0},{4,2},{6,4},{8,6},{10,8},{12,10},{14,12},{16,30},{18,... | collective-permute-start | bytes 786440 | tf_op jit(solution)/shard_map/ppermute | solution.py:394
  86.1 2.3 %all-to-all-done.2.refs_2_.after_ref = bf16[16,2,8,2048]{3,2,1,0:T(8,128)(2,1)S(1)} async-done(((bf16[16,2,8,2048]{3,2,1,0:T(8,128)(2,1)}), bf16[16,2,8,2048]{3,2,1,0:T(8,128)(2,1)S(1)}, u32[]{:S(2)}, u32[]{:S(2)}) %all-to-all-start.2) | async-done | bytes 1048608 | tf_op jit(solution)/shard_map/all_to_all | solution.py:417
  88.4 3.0 %collective-permute-done.9.left_ref = bf16[8,1,8,2048]{3,2,1,0:T(8,128)(2,1)S(1)} collective-permute-done((bf16[8,1,8,2048]{3,2,1,0:T(8,128)(2,1)S(1)}, bf16[8,1,8,2048]{3,2,1,0:T(8,128)(2,1)S(1)}, u32[]{:S(2)}, u32[]{:S(2)}) %collective-permute-start.9) | collective-permute-done | bytes 262176 | tf_op jit(solution)/shard_map/ppermute | solution.py:394
  92.2 7.1 %all-to-all-start.3 = ((bf16[16,3,8,2048]{3,2,1,0:T(8,128)(2,1)}), bf16[16,3,8,2048]{3,2,1,0:T(8,128)(2,1)}, u32[]{:S(2)}, u32[]{:S(2)}) async-start(bf16[16,3,8,2048]{3,2,1,0:T(8,128)(2,1)} %shard_map.110), calls=%async_computation.3 | async-start | bytes 3145728 | tf_op jit(solution)/shard_map/all_to_all | solution.py:417
  99.4 12.7 %shard_map.108 = (bf16[320,1024]{1,0:T(8,128)(2,1)}, bf16[320,1024]{1,0:T(8,128)(2,1)}, bf16[320,1024]{1,0:T(8,128)(2,1)}, bf16[320,1024]{1,0:T(8,128)(2,1)}, bf...) custom-call(s32[2]{0:T(128)S(1)} %pad_add_fusion.place_ref, ...), custom_call_target="tpu_custom_call" | custom-call | flops 1 | bytes 1 | tf_op jit(solution)/shard_map/pallas_call | solution.py:278
  112.1 7.4 %all-to-all-done.3.refs_1_ = bf16[16,3,8,2048]{3,2,1,0:T(8,128)(2,1)} async-done(((bf16[16,3,8,2048]{3,2,1,0:T(8,128)(2,1)}), bf16[16,3,8,2048]{3,2,1,0:T(8,128)(2,1)}, u32[]{:S(2)}, u32[]{:S(2)}) %all-to-all-start.3) | async-done | bytes 1572896 | tf_op jit(solution)/shard_map/all_to_all | solution.py:417
  119.5 10.9 %shard_map.111 = (bf16[192,1024]{1,0:T(8,128)(2,1)}, bf16[192,1024]{1,0:T(8,128)(2,1)}, bf16[192,1024]{1,0:T(8,128)(2,1)}, bf16[192,1024]{1,0:T(8,128)(2,1)}, bf...) custom-call(s32[2]{0:T(128)S(1)} %pad_add_fusion.place_ref, ...), custom_call_target="tpu_custom_call", output_to_operand_aliasing={{7}: (1, {})} | custom-call | flops 1 | bytes 1 | tf_op jit(solution)/shard_map/pallas_call | solution.py:278
  130.3 10.0 %all-to-all-start.4 = ((bf16[128,8,1024]{2,1,0:T(8,128)(2,1)}), bf16[128,8,1024]{2,1,0:T(8,128)(2,1)S(1)}, u32[]{:S(2)}, u32[]{:S(2)}) async-start(bf16[128,8,1024]{2,1,0:T(8,128)(2,1)} %bitcast.13), calls=%async_computation.4 | async-start | bytes 4194304 | tf_op jit(solution)/shard_map/all_to_all | solution.py:448
  140.3 7.4 %shard_map.112 = (bf16[1024,768]{1,0:T(8,128)(2,1)}, bf16[1024,768]{1,0:T(8,128)(2,1)}, bf16[768,1024]{1,0:T(8,128)(2,1)}) custom-call(bf16[320,1024]{1,0:T(8,128)(2,1)} %get-tuple-element.46.refs_0_, bf16[192,1024]{1,0:T(8,128)(2,1)} %get-tuple-element.51.refs_1_, bf16[320,1024]{1,0:T(8,128)(2,1)} %get-tuple-element.52.refs_2_, ...), custom_call_target="tpu_custom_call" | custom-call | flops 1 | bytes 1 | tf_op jit(solution)/shard_map/pallas_call | solution.py:330
  155.9 7.5 %shard_map.114 = (bf16[1024,768]{1,0:T(8,128)(2,1)}, bf16[1024,768]{1,0:T(8,128)(2,1)}, bf16[768,1024]{1,0:T(8,128)(2,1)}) custom-call(bf16[320,1024]{1,0:T(8,128)(2,1)} %get-tuple-element.66.refs_0_, bf16[192,1024]{1,0:T(8,128)(2,1)} %get-tuple-element.67.refs_1_, bf16[320,1024]{1,0:T(8,128)(2,1)} %get-tuple-element.68.refs_2_, ...), custom_call_target="tpu_custom_call" | custom-call | flops 1 | bytes 1 | tf_op jit(solution)/shard_map/pallas_call | solution.py:330
  163.3 31.0 %all-to-all-done.4 = bf16[128,8,1024]{2,1,0:T(8,128)(2,1)S(1)} async-done(((bf16[128,8,1024]{2,1,0:T(8,128)(2,1)}), bf16[128,8,1024]{2,1,0:T(8,128)(2,1)S(1)}, u32[]{:S(2)}, u32[]{:S(2)}) %all-to-all-start.4) | async-done | bytes 2097184 | tf_op jit(solution)/shard_map/all_to_all | solution.py:448
  (37 shorter events, 19.8 us)
Async XLA Ops:
  2.0 25.8 %collective-permute-start.1 = (bf16[128,4224]{1,0:T(8,128)(2,1)S(1)}, bf16[128,4224]{1,0:T(8,128)(2,1)S(1)}, u32[]{:S(2)}, u32[]{:S(2)}) collective-permute-start(bf16[128,4224]{1,0:T(8,128)(2,1)S(1)} %shard_map.102.meta_ref.refs_0_.refs_1_.refs_2_), channel_id=1, source_target_pairs={{0,14},{2,0},{4,2},{6,4},{8,6},{10,8},{12,10},{14,12},{16,30},{18,... | collective-permute-start | bytes 3244040 | tf_op jit(solution)/shard_map/ppermute | solution.py:394
  3.9 27.8 %collective-permute-start = (bf16[128,4224]{1,0:T(8,128)(2,1)S(1)}, bf16[128,4224]{1,0:T(8,128)(2,1)}, u32[]{:S(2)}, u32[]{:S(2)}) collective-permute-start(bf16[128,4224]{1,0:T(8,128)(2,1)S(1)} %shard_map.102.meta_ref.refs_0_.refs_1_.refs_2_), channel_id=1, source_target_pairs={{0,2},{2,4},{4,6},{6,8},{8,10},{10,12},{12,14},{14,0},{16,18},{18,... | collective-permute-start | bytes 3244040 | tf_op jit(solution)/shard_map/ppermute | solution.py:394
  27.9 1.0 copy-start.3
  31.7 25.8 %collective-permute-start.2 = (bf16[128,4224]{1,0:T(8,128)(2,1)}, bf16[128,4224]{1,0:T(8,128)(2,1)S(1)}, u32[]{:S(2)}, u32[]{:S(2)}) collective-permute-start(bf16[128,4224]{1,0:T(8,128)(2,1)} %collective-permute-done.refs_0_.refs_2_.refs_3_), channel_id=1, source_target_pairs={{0,2},{2,4},{4,6},{6,8},{8,10},{10,12},{12,14},{14,0},{16,18},{18,... | collective-permute-start | bytes 3244040 | tf_op jit(solution)/shard_map/ppermute | solution.py:394
  31.7 25.8 %collective-permute-start.3 = (bf16[128,4224]{1,0:T(8,128)(2,1)}, bf16[128,4224]{1,0:T(8,128)(2,1)S(1)}, u32[]{:S(2)}, u32[]{:S(2)}) collective-permute-start(bf16[128,4224]{1,0:T(8,128)(2,1)} %copy-done.3), channel_id=1, source_target_pairs={{0,14},{2,0},{4,2},{6,4},{8,6},{10,8},{12,10},{14,12},{16,30},{18,... | collective-permute-start | bytes 3244040 | tf_op jit(solution)/shard_map/ppermute | solution.py:394
  37.8 25.7 %all-to-all-start.1 = ((bf16[16,2,8,2048]{3,2,1,0:T(8,128)(2,1)}), bf16[16,2,8,2048]{3,2,1,0:T(8,128)(2,1)}, u32[]{:S(2)}, u32[]{:S(2)}) async-start(bf16[16,2,8,2048]{3,2,1,0:T(8,128)(2,1)} %shard_map.105), calls=%async_computation.1 | async-start | bytes 2097152 | tf_op jit(solution)/shard_map/all_to_all | solution.py:417
  60.5 18.1 %collective-permute-start.8 = (bf16[24,1,8,2048]{3,2,1,0:T(8,128)(2,1)}, bf16[24,1,8,2048]{3,2,1,0:T(8,128)(2,1)}, u32[]{:S(2)}, u32[]{:S(2)}) collective-permute-start(bf16[24,1,8,2048]{3,2,1,0:T(8,128)(2,1)} %get-tuple-element.48), channel_id=1, source_target_pairs={{0,14},{2,0},{4,2},{6,4},{8,6},{10,8},{12,10},{14,12},{16,30},{18,... | collective-permute-start | bytes 2359304 | tf_op jit(solution)/shard_map/ppermute | solution.py:394
  63.5 18.8 %collective-permute-start.7 = (bf16[24,1,8,2048]{3,2,1,0:T(8,128)(2,1)}, bf16[24,1,8,2048]{3,2,1,0:T(8,128)(2,1)}, u32[]{:S(2)}, u32[]{:S(2)}) collective-permute-start(bf16[24,1,8,2048]{3,2,1,0:T(8,128)(2,1)} %get-tuple-element.45.refs_0_), channel_id=1, source_target_pairs={{0,2},{2,4},{4,6},{6,8},{8,10},{10,12},{12,14},{14,0},{16,18},{18,... | collective-permute-start | bytes 2359304 | tf_op jit(solution)/shard_map/ppermute | solution.py:394
  66.1 22.3 %all-to-all-start.2 = ((bf16[16,2,8,2048]{3,2,1,0:T(8,128)(2,1)}), bf16[16,2,8,2048]{3,2,1,0:T(8,128)(2,1)S(1)}, u32[]{:S(2)}, u32[]{:S(2)}) async-start(bf16[16,2,8,2048]{3,2,1,0:T(8,128)(2,1)} %shard_map.107), calls=%async_computation.2 | async-start | bytes 2097152 | tf_op jit(solution)/shard_map/all_to_all | solution.py:417
  79.6 8.9 %collective-permute-start.10 = (bf16[8,1,8,2048]{3,2,1,0:T(8,128)(2,1)S(1)}, bf16[8,1,8,2048]{3,2,1,0:T(8,128)(2,1)S(1)}, u32[]{:S(2)}, u32[]{:S(2)}) collective-permute-start(bf16[8,1,8,2048]{3,2,1,0:T(8,128)(2,1)S(1)} %slice.9), channel_id=1, source_target_pairs={{0,14},{2,0},{4,2},{6,4},{8,6},{10,8},{12,10},{14,12},{16,30},{18,... | collective-permute-start | bytes 786440 | tf_op jit(solution)/shard_map/ppermute | solution.py:394
  83.3 8.1 %collective-permute-start.9 = (bf16[8,1,8,2048]{3,2,1,0:T(8,128)(2,1)S(1)}, bf16[8,1,8,2048]{3,2,1,0:T(8,128)(2,1)S(1)}, u32[]{:S(2)}, u32[]{:S(2)}) collective-permute-start(bf16[8,1,8,2048]{3,2,1,0:T(8,128)(2,1)S(1)} %slice.8), channel_id=1, source_target_pairs={{0,2},{2,4},{4,6},{6,8},{8,10},{10,12},{12,14},{14,0},{16,18},{18,... | collective-permute-start | bytes 786440 | tf_op jit(solution)/shard_map/ppermute | solution.py:394
  83.4 16.0 %collective-permute-start.4 = (bf16[1024,768]{1,0:T(8,128)(2,1)}, bf16[1024,768]{1,0:T(8,128)(2,1)}, u32[]{:S(2)}, u32[]{:S(2)}) collective-permute-start(bf16[1024,768]{1,0:T(8,128)(2,1)} %bitcast.14), channel_id=1, source_target_pairs={{0,1},{1,0},{2,3},{3,2},{4,5},{5,4},{6,7},{7,6},{8,9},{9,8},{10,11... | collective-permute-start | bytes 4718600 | tf_op jit(solution)/shard_map/ppermute | solution.py:397
  83.5 15.9 %collective-permute-start.5 = (bf16[1024,768]{1,0:T(8,128)(2,1)}, bf16[1024,768]{1,0:T(8,128)(2,1)}, u32[]{:S(2)}, u32[]{:S(2)}) collective-permute-start(bf16[1024,768]{1,0:T(8,128)(2,1)} %bitcast.17), channel_id=1, source_target_pairs={{0,1},{1,0},{2,3},{3,2},{4,5},{5,4},{6,7},{7,6},{8,9},{9,8},{10,11... | collective-permute-start | bytes 4718600 | tf_op jit(solution)/shard_map/ppermute | solution.py:397
  84.0 15.4 %collective-permute-start.6 = (bf16[768,1024]{1,0:T(8,128)(2,1)}, bf16[768,1024]{1,0:T(8,128)(2,1)}, u32[]{:S(2)}, u32[]{:S(2)}) collective-permute-start(bf16[768,1024]{1,0:T(8,128)(2,1)} %bitcast.20), channel_id=1, source_target_pairs={{0,1},{1,0},{2,3},{3,2},{4,5},{5,4},{6,7},{7,6},{8,9},{9,8},{10,11... | collective-permute-start | bytes 4718600 | tf_op jit(solution)/shard_map/ppermute | solution.py:397
  92.2 7.2 %copy-start = (bf16[16,1,8,2048]{3,2,1,0:T(8,128)(2,1)S(1)}, bf16[16,1,8,2048]{3,2,1,0:T(8,128)(2,1)}, u32[]{:S(2)}) copy-start(bf16[16,1,8,2048]{3,2,1,0:T(8,128)(2,1)} %all_to_all.25.refs_0_) | copy-start | bytes 1572868
  92.2 27.2 %all-to-all-start.3 = ((bf16[16,3,8,2048]{3,2,1,0:T(8,128)(2,1)}), bf16[16,3,8,2048]{3,2,1,0:T(8,128)(2,1)}, u32[]{:S(2)}, u32[]{:S(2)}) async-start(bf16[16,3,8,2048]{3,2,1,0:T(8,128)(2,1)} %shard_map.110), calls=%async_computation.3 | async-start | bytes 3145728 | tf_op jit(solution)/shard_map/all_to_all | solution.py:417
  130.3 64.0 %all-to-all-start.4 = ((bf16[128,8,1024]{2,1,0:T(8,128)(2,1)}), bf16[128,8,1024]{2,1,0:T(8,128)(2,1)S(1)}, u32[]{:S(2)}, u32[]{:S(2)}) async-start(bf16[128,8,1024]{2,1,0:T(8,128)(2,1)} %bitcast.13), calls=%async_computation.4 | async-start | bytes 4194304 | tf_op jit(solution)/shard_map/all_to_all | solution.py:448
  147.7 3.6 %collective-permute-start.11 = (bf16[1024,768]{1,0:T(8,128)(2,1)}, bf16[1024,768]{1,0:T(8,128)(2,1)S(1)}, u32[]{:S(2)}, u32[]{:S(2)}) collective-permute-start(bf16[1024,768]{1,0:T(8,128)(2,1)} %get-tuple-element.60), channel_id=1, source_target_pairs={{0,1},{1,0},{2,3},{3,2},{4,5},{5,4},{6,7},{7,6},{8,9},{9,8},{10,11... | collective-permute-start | bytes 4718600 | tf_op jit(solution)/shard_map/ppermute | solution.py:397
  147.8 5.9 %collective-permute-start.12 = (bf16[1024,768]{1,0:T(8,128)(2,1)}, bf16[1024,768]{1,0:T(8,128)(2,1)S(1)}, u32[]{:S(2)}, u32[]{:S(2)}) collective-permute-start(bf16[1024,768]{1,0:T(8,128)(2,1)} %get-tuple-element.61), channel_id=1, source_target_pairs={{0,1},{1,0},{2,3},{3,2},{4,5},{5,4},{6,7},{7,6},{8,9},{9,8},{10,11... | collective-permute-start | bytes 4718600 | tf_op jit(solution)/shard_map/ppermute | solution.py:397
  148.3 7.6 %collective-permute-start.13 = (bf16[768,1024]{1,0:T(8,128)(2,1)}, bf16[768,1024]{1,0:T(8,128)(2,1)S(1)}, u32[]{:S(2)}, u32[]{:S(2)}) collective-permute-start(bf16[768,1024]{1,0:T(8,128)(2,1)} %get-tuple-element.62), channel_id=1, source_target_pairs={{0,1},{1,0},{2,3},{3,2},{4,5},{5,4},{6,7},{7,6},{8,9},{9,8},{10,11... | collective-permute-start | bytes 4718600 | tf_op jit(solution)/shard_map/ppermute | solution.py:397
  148.9 0.7 copy-start.1
  155.9 38.5 %copy-start.2 = (bf16[1024,128]{1,0:T(8,128)(2,1)S(1)}, bf16[1024,128]{1,0:T(8,128)(2,1)}, u32[]{:S(2)}) copy-start(bf16[1024,128]{1,0:T(8,128)(2,1)} %copy-done.1) | copy-start | bytes 786436

commit v6 on v4

--- a/solution.py
+++ b/solution.py
@@ -11,6 +11,7 @@
 CAP = 4
 META = 128
 EXPERT_LIMIT = 40 * 1024 * 1024
+BESIDE_LIMIT = 60 * 1024 * 1024
 HALF = 1024
 COLS = 1024
 WTILE = 256
@@ -111,7 +112,7 @@
         )
 
 
-def build(jobs, place, planes, shapes, after=()):
+def build(jobs, place, planes, shapes, after=(), limit=VMEM_LIMIT):
     features = (planes[0].shape[1] - META) // 2
     sources = len(planes)
     tokens = planes[0].shape[0]
@@ -135,7 +136,7 @@
         * sources,
         out_specs=[pl.BlockSpec(shape + (COLS,), lambda c: (0, 0, 0, c)) for shape in shapes],
         scratch_shapes=scratch,
-        compiler_params=pltpu.CompilerParams(vmem_limit_bytes=VMEM_LIMIT),
+        compiler_params=pltpu.CompilerParams(vmem_limit_bytes=limit),
         cost_estimate=TOKEN_COST,
     )(place, *after, *planes, *[p for p in planes for _ in range(2)])
 
@@ -167,11 +168,12 @@
 
 def expert_kernel(chunks, groups, has_base, place_ref, *refs):
     refs = refs[1:] if has_base else refs
-    recvs, refs = refs[: len(chunks)], refs[len(chunks) :]
+    arrived, refs = refs[: len(chunks)], refs[len(chunks) :]
     sources, results, back = refs[:6], refs[6:13], refs[13]
     held, refs = refs[14:20], refs[20:]
+    recvs, refs = refs[: len(chunks)], refs[len(chunks) :]
     x_own, x_oth, s_own, s_oth, hid_ref, gg_ref, ug_ref = refs[:7]
-    stage, load_sems, store_sems, back_sems = refs[7:]
+    stage, load_sems, store_sems, back_sems, recv_sems = refs[7:]
     wg_own, wg_oth, wu_own, wu_oth, wd_own, wd_oth = held
     place = place_ref[0]
     rep = place_ref[1]
@@ -181,10 +183,14 @@
     stores = [
         pltpu.make_async_copy(refs[i], results[i], store_sems.at[i]) for i in range(len(results))
     ]
-    for load in loads:
-        load.start()
+    takes = [
+        pltpu.make_async_copy(arrived[i], recvs[i], recv_sems.at[i]) for i in range(len(recvs))
+    ]
+    for copy in takes + loads:
+        copy.start()
     start = 0
-    for recv, planes in zip(recvs, chunks):
+    for copy, recv, planes in zip(takes, recvs, chunks):
+        copy.wait()
         slots = groups * len(planes) * CAP
         row = lax.broadcasted_iota(jnp.int32, (2 * slots, 2 * slots), 0)
         col = lax.broadcasted_iota(jnp.int32, (2 * slots, 2 * slots), 1)
@@ -265,10 +271,10 @@
         ),
         in_specs=[pl.BlockSpec(memory_space=pltpu.SMEM)]
         + [anywhere for _ in bases]
-        + [pl.BlockSpec(memory_space=pltpu.VMEM) for _ in recvs]
+        + [anywhere for _ in recvs]
         + [anywhere] * 6,
         out_specs=[anywhere] * 8,
-        scratch_shapes=[pltpu.VMEM(w.shape, BF) for w in weights]
+        scratch_shapes=[pltpu.VMEM(v.shape, BF) for v in (*weights, *recvs)]
         + [pltpu.VMEM((slots, HALF), BF)] * 4
         + [pltpu.VMEM((slots, hidden), BF)] * 3
         + [
@@ -276,6 +282,7 @@
             pltpu.SemaphoreType.DMA((6,)),
             pltpu.SemaphoreType.DMA((7,)),
             pltpu.SemaphoreType.DMA((planes,)),
+            pltpu.SemaphoreType.DMA((len(recvs),)),
         ],
         input_output_aliases={1: 7} if has_base else {},
         compiler_params=pltpu.CompilerParams(vmem_limit_bytes=EXPERT_LIMIT),
@@ -391,6 +398,7 @@
             far_memory([data[p] for p in planes]) if planes == CHUNKS[1] else [data[p] for p in planes],
             [(groups, len(planes))],
             after,
+            BESIDE_LIMIT if planes == CHUNKS[0] else VMEM_LIMIT,
         )
         return sent
 
@@ -418,7 +426,7 @@
         (),
     )
     third = (hop(far[0], 1), hop(far[1], -1))
-    recv_second = exchange(near(CHUNKS[2], far_memory([far[0], recv_next])))
+    recv_second = exchange(near(CHUNKS[2], [*far_memory([far[0]]), recv_next]))
     fourth = (hop(third[0][groups:], 1), hop(third[1][groups:], -1))
     recv_far = exchange(join(third, fourth, groups, recv_second))
     *early, back = experts(

time: 194 us -> 195 us (level)
  no operation moved by 1% of the time
where the time goes in v6:
time: 195 us; the launch traced here: 194 us
  waiting for transfers between devices  73 us (37%)
  Pallas kernels  56.1 us (29%)
  starting transfers between devices  42.5 us (22%)
  blocking collectives  18.4 us (9%)
  local copies, waits for them, and re-layouts  2.93 us (2%)
    all_to_all x1, waiting for transfers between devices, local(): lax.all_to_all(back.reshape(owners, 2 * CAP, HALF), 'expert', split_axis=...  27.5 us
    ppermute x8, waiting for transfers between devices, hop(): return lax.ppermute(value, 'expert', pairs)  25.9 us
    pallas_call x2, Pallas kernels, experts(): pl.pallas_call(functools.partial(expert_kernel, chunks, groups, has_base)...  24 us
    all_to_all x3, starting transfers between devices, exchange(): lax.all_to_all(sent, 'expert', split_axis=0, concat_axis=0, tiled=True, a...  21.3 us
    all_to_all x1, blocking collectives, exchange(): lax.all_to_all(sent, 'expert', split_axis=0, concat_axis=0, tiled=True, a...  18.4 us
    pallas_call x2, Pallas kernels, weight_grads(): pl.pallas_call(functools.partial(weight_kernel, len(xs), bool(received)),...  14.9 us
    all_to_all x3, waiting for transfers between devices, exchange(): lax.all_to_all(sent, 'expert', split_axis=0, concat_axis=0, tiled=True, a...  12.7 us
    pallas_call x4, Pallas kernels, build(): pl.pallas_call(functools.partial(build_kernel, jobs, sources, len(shapes)...  11.4 us
  transfers between devices with their start and end apart: 18, of which 11 were waited for; matrix products, arithmetic and copies ran while one was open for 1% of the time, Pallas kernels for 21%

profile of v6, /device:TPU:32, one launch (start us, length us, event | category | flops | bytes accessed | tf_op | source)
XLA Modules:
  0.0 194.5 jit_solution(17723406985983505052)
XLA Ops:
  4.7 2.7 %shard_map.104 = bf16[16,1,8,2048]{3,2,1,0:T(8,128)(2,1)} custom-call(s32[2]{0:T(128)} %pad_add_fusion.place_ref, bf16[128,4224]{1,0:T(8,128)(2,1)} %copy-done, bf16[128,4224]{1,0:T(8,128)(2,1)} %copy-done, bf16[128,4224]{1,0:T(8,128)(2,1)} %copy-done), custom_call_target="tpu_custom_call" | custom-call | flops 1 | bytes 1 | tf_op jit(solution)/shard_map/pallas_call | solution.py:125
  7.4 18.4 %all_to_all.25.refs_0_ = bf16[16,1,8,2048]{3,2,1,0:T(8,128)(2,1)} all-to-all(bf16[16,1,8,2048]{3,2,1,0:T(8,128)(2,1)} %shard_map.104), channel_id=1, replica_groups={{0,16,32,48,64,80,96,112,128,144,160,176,192,208,224,240},{2,18,34,50,6..., dimensions={0} | all-to-all | bytes 1048576 | tf_op jit(solution)/shard_map/all_to_all | solution.py:406
  28.9 2.9 %collective-permute-done.refs_0_.refs_2_.refs_3_ = bf16[128,4224]{1,0:T(8,128)(2,1)} collective-permute-done((bf16[128,4224]{1,0:T(8,128)(2,1)S(1)}, bf16[128,4224]{1,0:T(8,128)(2,1)}, u32[]{:S(2)}, u32[]{:S(2)}) %collective-permute-start) | collective-permute-done | bytes 1081376 | tf_op jit(solution)/shard_map/ppermute | solution.py:382
  31.8 3.0 %collective-permute-start.3 = (bf16[128,4224]{1,0:T(8,128)(2,1)}, bf16[128,4224]{1,0:T(8,128)(2,1)S(1)}, u32[]{:S(2)}, u32[]{:S(2)}) collective-permute-start(bf16[128,4224]{1,0:T(8,128)(2,1)} %copy-done.4), channel_id=1, source_target_pairs={{0,14},{2,0},{4,2},{6,4},{8,6},{10,8},{12,10},{14,12},{16,30},{18,... | collective-permute-start | bytes 3244040 | tf_op jit(solution)/shard_map/ppermute | solution.py:382
  34.7 3.1 %shard_map.105 = bf16[16,2,8,2048]{3,2,1,0:T(8,128)(2,1)} custom-call(s32[2]{0:T(128)S(1)} %copy-done.3, bf16[128,4224]{1,0:T(8,128)(2,1)} %collective-permute-done.refs_0_.refs_2_.refs_3_, bf16[128,4224]{1,0:T(8,128)(2,1)} %copy-done.4, bf16[128,4224]{1,0:T(8,128)(2,1)} %collective-permute-done.refs_0_.refs_2_.refs_3_, ...), custom_call_target="tpu_custom_call" | custom-call | flops 1 | bytes 1 | tf_op jit(solution)/shard_map/pallas_call | solution.py:125
  37.9 7.0 %all-to-all-start.1 = ((bf16[16,2,8,2048]{3,2,1,0:T(8,128)(2,1)}), bf16[16,2,8,2048]{3,2,1,0:T(8,128)(2,1)S(1)}, u32[]{:S(2)}, u32[]{:S(2)}) async-start(bf16[16,2,8,2048]{3,2,1,0:T(8,128)(2,1)} %shard_map.105), calls=%async_computation.1 | async-start | bytes 2097152 | tf_op jit(solution)/shard_map/all_to_all | solution.py:406
  44.9 12.7 %collective-permute-done.2.refs_0_.refs_2_.refs_3_.refs_4_.refs_5_ = bf16[128,4224]{1,0:T(8,128)(2,1)S(1)} collective-permute-done((bf16[128,4224]{1,0:T(8,128)(2,1)}, bf16[128,4224]{1,0:T(8,128)(2,1)S(1)}, u32[]{:S(2)}, u32[]{:S(2)}) %collective-permute-start.2) | collective-permute-done | bytes 1081376 | tf_op jit(solution)/shard_map/ppermute | solution.py:382
  57.6 3.0 %shard_map.106 = (bf16[24,1,8,2048]{3,2,1,0:T(8,128)(2,1)}, bf16[24,1,8,2048]{3,2,1,0:T(8,128)(2,1)}) custom-call(s32[2]{0:T(128)S(1)} %copy-done.3, bf16[128,4224]{1,0:T(8,128)(2,1)S(1)} %collective-permute-done.2.refs_0_.refs_2_.refs_3_.refs_4_.refs_5_, bf16[128,4224]{1,0:T(8,128)(2,1)S(1)} %collective-permute-done.3.refs_1_.refs_4_.refs_5_.refs_3_.refs_6_.refs_7_, ...), custom_call_target="tpu_custom_call" | custom-call | flops 1 | bytes 1 | tf_op jit(solution)/shard_map/pallas_call | solution.py:125
  60.6 3.0 %collective-permute-start.8 = (bf16[24,1,8,2048]{3,2,1,0:T(8,128)(2,1)}, bf16[24,1,8,2048]{3,2,1,0:T(8,128)(2,1)}, u32[]{:S(2)}, u32[]{:S(2)}) collective-permute-start(bf16[24,1,8,2048]{3,2,1,0:T(8,128)(2,1)} %get-tuple-element.46), channel_id=1, source_target_pairs={{0,14},{2,0},{4,2},{6,4},{8,6},{10,8},{12,10},{14,12},{16,30},{18,... | collective-permute-start | bytes 2359304 | tf_op jit(solution)/shard_map/ppermute | solution.py:382
  63.6 2.7 %shard_map.107 = bf16[16,2,8,2048]{3,2,1,0:T(8,128)(2,1)} custom-call(s32[2]{0:T(128)S(1)} %copy-done.3, bf16[24,1,8,2048]{3,2,1,0:T(8,128)(2,1)} %get-tuple-element.43.refs_0_, bf16[16,2,8,2048]{3,2,1,0:T(8,128)(2,1)S(1)} %all-to-all-done.1.refs_1_, bf16[128,4224]{1,0:T(8,128)(2,1)S(1)} %collective-permute-done.2.refs_0_.refs_2_.refs_3_.refs_4_.refs_5_, ...), custom_call_target="tpu_custom_call" | custom-call | flops 1 | bytes 1 | tf_op jit(solution)/shard_map/pallas_call | solution.py:125
  66.2 7.0 %all-to-all-start.2 = ((bf16[16,2,8,2048]{3,2,1,0:T(8,128)(2,1)}), bf16[16,2,8,2048]{3,2,1,0:T(8,128)(2,1)S(1)}, u32[]{:S(2)}, u32[]{:S(2)}) async-start(bf16[16,2,8,2048]{3,2,1,0:T(8,128)(2,1)} %shard_map.107), calls=%async_computation.2 | async-start | bytes 2097152 | tf_op jit(solution)/shard_map/all_to_all | solution.py:406
  73.3 5.3 %collective-permute-done.8.right_ref = bf16[24,1,8,2048]{3,2,1,0:T(8,128)(2,1)} collective-permute-done((bf16[24,1,8,2048]{3,2,1,0:T(8,128)(2,1)}, bf16[24,1,8,2048]{3,2,1,0:T(8,128)(2,1)}, u32[]{:S(2)}, u32[]{:S(2)}) %collective-permute-start.8) | collective-permute-done | bytes 786464 | tf_op jit(solution)/shard_map/ppermute | solution.py:382
  79.5 2.7 %collective-permute-start.10 = (bf16[8,1,8,2048]{3,2,1,0:T(8,128)(2,1)S(1)}, bf16[8,1,8,2048]{3,2,1,0:T(8,128)(2,1)S(1)}, u32[]{:S(2)}, u32[]{:S(2)}) collective-permute-start(bf16[8,1,8,2048]{3,2,1,0:T(8,128)(2,1)S(1)} %slice.9), channel_id=1, source_target_pairs={{0,14},{2,0},{4,2},{6,4},{8,6},{10,8},{12,10},{14,12},{16,30},{18,... | collective-permute-start | bytes 786440 | tf_op jit(solution)/shard_map/ppermute | solution.py:382
  84.0 4.5 %all-to-all-done.2.refs_2_.after_ref = bf16[16,2,8,2048]{3,2,1,0:T(8,128)(2,1)S(1)} async-done(((bf16[16,2,8,2048]{3,2,1,0:T(8,128)(2,1)}), bf16[16,2,8,2048]{3,2,1,0:T(8,128)(2,1)S(1)}, u32[]{:S(2)}, u32[]{:S(2)}) %all-to-all-start.2) | async-done | bytes 1048608 | tf_op jit(solution)/shard_map/all_to_all | solution.py:406
  88.5 2.9 %collective-permute-done.9.far_left_ref = bf16[8,1,8,2048]{3,2,1,0:T(8,128)(2,1)S(1)} collective-permute-done((bf16[8,1,8,2048]{3,2,1,0:T(8,128)(2,1)S(1)}, bf16[8,1,8,2048]{3,2,1,0:T(8,128)(2,1)S(1)}, u32[]{:S(2)}, u32[]{:S(2)}) %collective-permute-start.9) | collective-permute-done | bytes 262176 | tf_op jit(solution)/shard_map/ppermute | solution.py:382
  93.6 7.2 %all-to-all-start.3 = ((bf16[16,3,8,2048]{3,2,1,0:T(8,128)(2,1)}), bf16[16,3,8,2048]{3,2,1,0:T(8,128)(2,1)}, u32[]{:S(2)}, u32[]{:S(2)}) async-start(bf16[16,3,8,2048]{3,2,1,0:T(8,128)(2,1)} %shard_map.109), calls=%async_computation.3 | async-start | bytes 3145728 | tf_op jit(solution)/shard_map/all_to_all | solution.py:406
  100.8 11.8 %shard_map.108 = (bf16[320,1024]{1,0:T(8,128)(2,1)}, bf16[320,1024]{1,0:T(8,128)(2,1)}, bf16[320,1024]{1,0:T(8,128)(2,1)}, bf16[320,1024]{1,0:T(8,128)(2,1)}, bf...) custom-call(s32[2]{0:T(128)S(1)} %copy-done.3, ...), custom_call_target="tpu_custom_call" | custom-call | flops 1 | bytes 1 | tf_op jit(solution)/shard_map/pallas_call | solution.py:265
  112.7 8.3 %all-to-all-done.3.refs_1_ = bf16[16,3,8,2048]{3,2,1,0:T(8,128)(2,1)} async-done(((bf16[16,3,8,2048]{3,2,1,0:T(8,128)(2,1)}), bf16[16,3,8,2048]{3,2,1,0:T(8,128)(2,1)}, u32[]{:S(2)}, u32[]{:S(2)}) %all-to-all-start.3) | async-done | bytes 1572896 | tf_op jit(solution)/shard_map/all_to_all | solution.py:406
  120.9 12.2 %shard_map.110 = (bf16[192,1024]{1,0:T(8,128)(2,1)}, bf16[192,1024]{1,0:T(8,128)(2,1)}, bf16[192,1024]{1,0:T(8,128)(2,1)}, bf16[192,1024]{1,0:T(8,128)(2,1)}, bf...) custom-call(s32[2]{0:T(128)S(1)} %copy-done.3, ...), custom_call_target="tpu_custom_call", output_to_operand_aliasing={{7}: (1, {})} | custom-call | flops 1 | bytes 1 | tf_op jit(solution)/shard_map/pallas_call | solution.py:265
  133.4 9.0 %all-to-all-start.4 = ((bf16[128,8,1024]{2,1,0:T(8,128)(2,1)}), bf16[128,8,1024]{2,1,0:T(8,128)(2,1)S(1)}, u32[]{:S(2)}, u32[]{:S(2)}) async-start(bf16[128,8,1024]{2,1,0:T(8,128)(2,1)} %bitcast.13), calls=%async_computation.4 | async-start | bytes 4194304 | tf_op jit(solution)/shard_map/all_to_all | solution.py:437
  142.4 7.5 %shard_map.111 = (bf16[1024,768]{1,0:T(8,128)(2,1)}, bf16[1024,768]{1,0:T(8,128)(2,1)}, bf16[768,1024]{1,0:T(8,128)(2,1)}) custom-call(bf16[320,1024]{1,0:T(8,128)(2,1)} %get-tuple-element.44.refs_0_, bf16[192,1024]{1,0:T(8,128)(2,1)} %get-tuple-element.47.refs_1_, bf16[320,1024]{1,0:T(8,128)(2,1)} %get-tuple-element.48.refs_2_, ...), custom_call_target="tpu_custom_call" | custom-call | flops 1 | bytes 1 | tf_op jit(solution)/shard_map/pallas_call | solution.py:318
  151.1 2.4 %collective-permute-done.11.refs_10_ = bf16[1024,768]{1,0:T(8,128)(2,1)S(1)} collective-permute-done((bf16[1024,768]{1,0:T(8,128)(2,1)}, bf16[1024,768]{1,0:T(8,128)(2,1)S(1)}, u32[]{:S(2)}, u32[]{:S(2)}) %collective-permute-start.11) | collective-permute-done | bytes 1572896 | tf_op jit(solution)/shard_map/ppermute | solution.py:385
  158.0 7.4 %shard_map.113 = (bf16[1024,768]{1,0:T(8,128)(2,1)}, bf16[1024,768]{1,0:T(8,128)(2,1)}, bf16[768,1024]{1,0:T(8,128)(2,1)}) custom-call(bf16[320,1024]{1,0:T(8,128)(2,1)} %get-tuple-element.62.refs_0_, bf16[192,1024]{1,0:T(8,128)(2,1)} %get-tuple-element.63.refs_1_, bf16[320,1024]{1,0:T(8,128)(2,1)} %get-tuple-element.64.refs_2_, ...), custom_call_target="tpu_custom_call" | custom-call | flops 1 | bytes 1 | tf_op jit(solution)/shard_map/pallas_call | solution.py:318
  165.5 27.5 %all-to-all-done.4 = bf16[128,8,1024]{2,1,0:T(8,128)(2,1)S(1)} async-done(((bf16[128,8,1024]{2,1,0:T(8,128)(2,1)}), bf16[128,8,1024]{2,1,0:T(8,128)(2,1)S(1)}, u32[]{:S(2)}, u32[]{:S(2)}) %all-to-all-start.4) | async-done | bytes 2097184 | tf_op jit(solution)/shard_map/all_to_all | solution.py:437
  (38 shorter events, 19.4 us)
Async XLA Ops:
  2.0 2.7 %copy-start = (bf16[128,4224]{1,0:T(8,128)(2,1)}, bf16[128,4224]{1,0:T(8,128)(2,1)S(1)}, u32[]{:S(2)}) copy-start(bf16[128,4224]{1,0:T(8,128)(2,1)S(1)} %shard_map.102.meta_ref.refs_0_.refs_1_.refs_2_) | copy-start | bytes 3244036
  2.0 25.9 %collective-permute-start.1 = (bf16[128,4224]{1,0:T(8,128)(2,1)S(1)}, bf16[128,4224]{1,0:T(8,128)(2,1)S(1)}, u32[]{:S(2)}, u32[]{:S(2)}) collective-permute-start(bf16[128,4224]{1,0:T(8,128)(2,1)S(1)} %shard_map.102.meta_ref.refs_0_.refs_1_.refs_2_), channel_id=1, source_target_pairs={{0,14},{2,0},{4,2},{6,4},{8,6},{10,8},{12,10},{14,12},{16,30},{18,... | collective-permute-start | bytes 3244040 | tf_op jit(solution)/shard_map/ppermute | solution.py:382
  4.0 27.8 %collective-permute-start = (bf16[128,4224]{1,0:T(8,128)(2,1)S(1)}, bf16[128,4224]{1,0:T(8,128)(2,1)}, u32[]{:S(2)}, u32[]{:S(2)}) collective-permute-start(bf16[128,4224]{1,0:T(8,128)(2,1)S(1)} %shard_map.102.meta_ref.refs_0_.refs_1_.refs_2_), channel_id=1, source_target_pairs={{0,2},{2,4},{4,6},{6,8},{8,10},{10,12},{12,14},{14,0},{16,18},{18,... | collective-permute-start | bytes 3244040 | tf_op jit(solution)/shard_map/ppermute | solution.py:382
  4.7 30.0 %copy-start.3 = (s32[2]{0:T(128)S(1)}, s32[2]{0:T(128)}, u32[]{:S(2)}) copy-start(s32[2]{0:T(128)} %pad_add_fusion.place_ref) | copy-start | bytes 28
  27.9 1.0 copy-start.4
  31.8 25.8 %collective-permute-start.2 = (bf16[128,4224]{1,0:T(8,128)(2,1)}, bf16[128,4224]{1,0:T(8,128)(2,1)S(1)}, u32[]{:S(2)}, u32[]{:S(2)}) collective-permute-start(bf16[128,4224]{1,0:T(8,128)(2,1)} %collective-permute-done.refs_0_.refs_2_.refs_3_), channel_id=1, source_target_pairs={{0,2},{2,4},{4,6},{6,8},{8,10},{10,12},{12,14},{14,0},{16,18},{18,... | collective-permute-start | bytes 3244040 | tf_op jit(solution)/shard_map/ppermute | solution.py:382
  31.8 25.8 %collective-permute-start.3 = (bf16[128,4224]{1,0:T(8,128)(2,1)}, bf16[128,4224]{1,0:T(8,128)(2,1)S(1)}, u32[]{:S(2)}, u32[]{:S(2)}) collective-permute-start(bf16[128,4224]{1,0:T(8,128)(2,1)} %copy-done.4), channel_id=1, source_target_pairs={{0,14},{2,0},{4,2},{6,4},{8,6},{10,8},{12,10},{14,12},{16,30},{18,... | collective-permute-start | bytes 3244040 | tf_op jit(solution)/shard_map/ppermute | solution.py:382
  37.9 25.7 %all-to-all-start.1 = ((bf16[16,2,8,2048]{3,2,1,0:T(8,128)(2,1)}), bf16[16,2,8,2048]{3,2,1,0:T(8,128)(2,1)S(1)}, u32[]{:S(2)}, u32[]{:S(2)}) async-start(bf16[16,2,8,2048]{3,2,1,0:T(8,128)(2,1)} %shard_map.105), calls=%async_computation.1 | async-start | bytes 2097152 | tf_op jit(solution)/shard_map/all_to_all | solution.py:406
  60.6 18.0 %collective-permute-start.8 = (bf16[24,1,8,2048]{3,2,1,0:T(8,128)(2,1)}, bf16[24,1,8,2048]{3,2,1,0:T(8,128)(2,1)}, u32[]{:S(2)}, u32[]{:S(2)}) collective-permute-start(bf16[24,1,8,2048]{3,2,1,0:T(8,128)(2,1)} %get-tuple-element.46), channel_id=1, source_target_pairs={{0,14},{2,0},{4,2},{6,4},{8,6},{10,8},{12,10},{14,12},{16,30},{18,... | collective-permute-start | bytes 2359304 | tf_op jit(solution)/shard_map/ppermute | solution.py:382
  63.5 18.7 %collective-permute-start.7 = (bf16[24,1,8,2048]{3,2,1,0:T(8,128)(2,1)}, bf16[24,1,8,2048]{3,2,1,0:T(8,128)(2,1)}, u32[]{:S(2)}, u32[]{:S(2)}) collective-permute-start(bf16[24,1,8,2048]{3,2,1,0:T(8,128)(2,1)} %get-tuple-element.43.refs_0_), channel_id=1, source_target_pairs={{0,2},{2,4},{4,6},{6,8},{8,10},{10,12},{12,14},{14,0},{16,18},{18,... | collective-permute-start | bytes 2359304 | tf_op jit(solution)/shard_map/ppermute | solution.py:382
  66.2 22.3 %all-to-all-start.2 = ((bf16[16,2,8,2048]{3,2,1,0:T(8,128)(2,1)}), bf16[16,2,8,2048]{3,2,1,0:T(8,128)(2,1)S(1)}, u32[]{:S(2)}, u32[]{:S(2)}) async-start(bf16[16,2,8,2048]{3,2,1,0:T(8,128)(2,1)} %shard_map.107), calls=%async_computation.2 | async-start | bytes 2097152 | tf_op jit(solution)/shard_map/all_to_all | solution.py:406
  79.5 9.0 %collective-permute-start.10 = (bf16[8,1,8,2048]{3,2,1,0:T(8,128)(2,1)S(1)}, bf16[8,1,8,2048]{3,2,1,0:T(8,128)(2,1)S(1)}, u32[]{:S(2)}, u32[]{:S(2)}) collective-permute-start(bf16[8,1,8,2048]{3,2,1,0:T(8,128)(2,1)S(1)} %slice.9), channel_id=1, source_target_pairs={{0,14},{2,0},{4,2},{6,4},{8,6},{10,8},{12,10},{14,12},{16,30},{18,... | collective-permute-start | bytes 786440 | tf_op jit(solution)/shard_map/ppermute | solution.py:382
  83.2 8.1 %collective-permute-start.9 = (bf16[8,1,8,2048]{3,2,1,0:T(8,128)(2,1)S(1)}, bf16[8,1,8,2048]{3,2,1,0:T(8,128)(2,1)S(1)}, u32[]{:S(2)}, u32[]{:S(2)}) collective-permute-start(bf16[8,1,8,2048]{3,2,1,0:T(8,128)(2,1)S(1)} %slice.8), channel_id=1, source_target_pairs={{0,2},{2,4},{4,6},{6,8},{8,10},{10,12},{12,14},{14,0},{16,18},{18,... | collective-permute-start | bytes 786440 | tf_op jit(solution)/shard_map/ppermute | solution.py:382
  83.3 17.5 %collective-permute-start.4 = (bf16[1024,768]{1,0:T(8,128)(2,1)}, bf16[1024,768]{1,0:T(8,128)(2,1)}, u32[]{:S(2)}, u32[]{:S(2)}) collective-permute-start(bf16[1024,768]{1,0:T(8,128)(2,1)} %bitcast.14), channel_id=1, source_target_pairs={{0,1},{1,0},{2,3},{3,2},{4,5},{5,4},{6,7},{7,6},{8,9},{9,8},{10,11... | collective-permute-start | bytes 4718600 | tf_op jit(solution)/shard_map/ppermute | solution.py:385
  83.4 17.4 %collective-permute-start.5 = (bf16[1024,768]{1,0:T(8,128)(2,1)}, bf16[1024,768]{1,0:T(8,128)(2,1)}, u32[]{:S(2)}, u32[]{:S(2)}) collective-permute-start(bf16[1024,768]{1,0:T(8,128)(2,1)} %bitcast.17), channel_id=1, source_target_pairs={{0,1},{1,0},{2,3},{3,2},{4,5},{5,4},{6,7},{7,6},{8,9},{9,8},{10,11... | collective-permute-start | bytes 4718600 | tf_op jit(solution)/shard_map/ppermute | solution.py:385
  83.9 16.9 %collective-permute-start.6 = (bf16[768,1024]{1,0:T(8,128)(2,1)}, bf16[768,1024]{1,0:T(8,128)(2,1)}, u32[]{:S(2)}, u32[]{:S(2)}) collective-permute-start(bf16[768,1024]{1,0:T(8,128)(2,1)} %bitcast.20), channel_id=1, source_target_pairs={{0,1},{1,0},{2,3},{3,2},{4,5},{5,4},{6,7},{7,6},{8,9},{9,8},{10,11... | collective-permute-start | bytes 4718600 | tf_op jit(solution)/shard_map/ppermute | solution.py:385
  93.6 7.3 %copy-start.2 = (bf16[16,1,8,2048]{3,2,1,0:T(8,128)(2,1)S(1)}, bf16[16,1,8,2048]{3,2,1,0:T(8,128)(2,1)}, u32[]{:S(2)}) copy-start(bf16[16,1,8,2048]{3,2,1,0:T(8,128)(2,1)} %all_to_all.25.refs_0_) | copy-start | bytes 1572868
  93.6 27.3 %all-to-all-start.3 = ((bf16[16,3,8,2048]{3,2,1,0:T(8,128)(2,1)}), bf16[16,3,8,2048]{3,2,1,0:T(8,128)(2,1)}, u32[]{:S(2)}, u32[]{:S(2)}) async-start(bf16[16,3,8,2048]{3,2,1,0:T(8,128)(2,1)} %shard_map.109), calls=%async_computation.3 | async-start | bytes 3145728 | tf_op jit(solution)/shard_map/all_to_all | solution.py:406
  133.4 59.6 %all-to-all-start.4 = ((bf16[128,8,1024]{2,1,0:T(8,128)(2,1)}), bf16[128,8,1024]{2,1,0:T(8,128)(2,1)S(1)}, u32[]{:S(2)}, u32[]{:S(2)}) async-start(bf16[128,8,1024]{2,1,0:T(8,128)(2,1)} %bitcast.13), calls=%async_computation.4 | async-start | bytes 4194304 | tf_op jit(solution)/shard_map/all_to_all | solution.py:437
  142.4 8.1 %copy-start.1 = (bf16[128,4224]{1,0:T(8,128)(2,1)S(1)}, bf16[128,4224]{1,0:T(8,128)(2,1)}, u32[]{:S(2)}) copy-start(bf16[128,4224]{1,0:T(8,128)(2,1)} %copy-done) | copy-start | bytes 3244036
  149.9 3.6 %collective-permute-start.11 = (bf16[1024,768]{1,0:T(8,128)(2,1)}, bf16[1024,768]{1,0:T(8,128)(2,1)S(1)}, u32[]{:S(2)}, u32[]{:S(2)}) collective-permute-start(bf16[1024,768]{1,0:T(8,128)(2,1)} %get-tuple-element.56), channel_id=1, source_target_pairs={{0,1},{1,0},{2,3},{3,2},{4,5},{5,4},{6,7},{7,6},{8,9},{9,8},{10,11... | collective-permute-start | bytes 4718600 | tf_op jit(solution)/shard_map/ppermute | solution.py:385
  149.9 5.9 %collective-permute-start.12 = (bf16[1024,768]{1,0:T(8,128)(2,1)}, bf16[1024,768]{1,0:T(8,128)(2,1)S(1)}, u32[]{:S(2)}, u32[]{:S(2)}) collective-permute-start(bf16[1024,768]{1,0:T(8,128)(2,1)} %get-tuple-element.57), channel_id=1, source_target_pairs={{0,1},{1,0},{2,3},{3,2},{4,5},{5,4},{6,7},{7,6},{8,9},{9,8},{10,11... | collective-permute-start | bytes 4718600 | tf_op jit(solution)/shard_map/ppermute | solution.py:385
  150.4 7.6 %collective-permute-start.13 = (bf16[768,1024]{1,0:T(8,128)(2,1)}, bf16[768,1024]{1,0:T(8,128)(2,1)S(1)}, u32[]{:S(2)}, u32[]{:S(2)}) collective-permute-start(bf16[768,1024]{1,0:T(8,128)(2,1)} %get-tuple-element.58), channel_id=1, source_target_pairs={{0,1},{1,0},{2,3},{3,2},{4,5},{5,4},{6,7},{7,6},{8,9},{9,8},{10,11... | collective-permute-start | bytes 4718600 | tf_op jit(solution)/shard_map/ppermute | solution.py:385
